TPU v7x, 32 devices: a whole 2x2x4 slice. The times are simulated.
32 devices in a mesh: section: 4 (over y, x), dp: 8 (over z, core).
Axes of the slice: x: 2, y: 2, z: 4, core: 2. Of those that a mesh axis runs over, the one named last changes fastest.
Arguments:
- inputs: bfloat16 [4, 16, 196, 256], P(None, 'dp'), may hold values from -6 to 6
- cotangent: bfloat16 [4, 16, 196, 256], P(None, 'dp'), may hold values from -6 to 6
- routes: int32 [2, 4, 16, 49, 4], P(None, None, 'dp'), may hold values from 0 to 48, all different within a row
- vectors: float32 [4, 16, 256], P('section'), may hold values from -1.2 to 1.48
- in_weight: bfloat16 [4, 256, 768], P('section'), may hold values from -0.375 to 0.375
- out_weight: bfloat16 [4, 768, 256], P('section'), may hold values from -0.75 to 0.75
Outputs:
- final: bfloat16 [4, 16, 196, 256], P('section', 'dp')
- input_grad: bfloat16 [4, 16, 196, 256], P('section', 'dp')
- grad_vectors: float32 [4, 16, 256], P('section')
- grad_in_weight: float32 [4, 256, 768], P('section')
- grad_out_weight: float32 [4, 768, 256], P('section')
Inputs may be any that keep to these rules, and one draw needn't show every extreme that they name: `routes`: each row names 4 different regions of the same image.
All inputs are finite; a program needn't handle non-finite values.
Results may differ from a plain program's by a relative error of at most 0.02.
Values may be sent and summed in bfloat16 or wider, within the bound.
A program may use at most 192 MiB of HBM per device.

v0:
```python
import jax
import jax.numpy as jnp
from jax import lax
from jax.sharding import PartitionSpec as P

D = 256
HEADS = 8
HEAD_DIM = 32
HID = 768
SIDE = 14
WIN = 7
TOPK = 4
VEC_ROWS = 16
PATCHES = 196
REGIONS = 49
INSIDE = 4


EPSILON = 1e-06


def passed_along(value, axis, by):
    devices = lax.axis_size(axis)
    pairs = [(i, i + by) for i in range(devices) if 0 <= i + by < devices]
    return lax.ppermute(value, axis, pairs)


def broadcast(block, axis, source):
    block = jnp.where(lax.axis_index(axis) == source, block, jnp.zeros_like(block))
    return lax.psum(block, axis)


def layer_norm(values, gain, offset):
    average = jnp.mean(values, axis=-1, keepdims=True)
    centred = values - average
    spread = jnp.mean(centred * centred, axis=-1, keepdims=True)
    inverse = lax.rsqrt(spread + EPSILON)
    normal_hat = centred * inverse
    return (normal_hat * gain + offset, normal_hat, inverse)


def norm_backward(grad_normed, normal_hat, inverse, gain):
    scaled = grad_normed * gain
    first_mean = jnp.mean(scaled, axis=-1, keepdims=True)
    second_mean = jnp.mean(scaled * normal_hat, axis=-1, keepdims=True)
    return inverse * (scaled - first_mean - normal_hat * second_mean)


def to_regions(tokens):
    images = tokens.shape[0]
    channels = tokens.shape[-1]
    cell_side = SIDE // WIN
    grid_view = tokens.reshape(images, WIN, cell_side, WIN, cell_side, channels).transpose(
        0, 1, 3, 2, 4, 5
    )
    return grid_view.reshape(images, WIN * WIN, cell_side * cell_side, channels)


def from_regions(regions):
    images = regions.shape[0]
    channels = regions.shape[-1]
    cell_side = SIDE // WIN
    grid_view = regions.reshape(images, WIN, WIN, cell_side, cell_side, channels).transpose(
        0, 1, 3, 2, 4, 5
    )
    return grid_view.reshape(images, SIDE * SIDE, channels)


def pad_grid(values):
    return jnp.pad(values, ((0, 0), (1, 1), (1, 1), (0, 0)))


def exact_gelu(values):
    return jax.nn.gelu(values, approximate=False)


def put_slot(buffer, value, slot_index, is_live):
    current = lax.dynamic_index_in_dim(buffer, slot_index, 0, keepdims=False)
    return lax.dynamic_update_index_in_dim(
        buffer, jnp.where(is_live, value, current), slot_index, 0
    )


def row_product(left, right):
    return lax.dot_general(
        left, right, (((0,), (0,)), ((), ())), preferred_element_type=jnp.float32
    )


def per_device(inputs, cotangent, routes, vectors, in_weight, out_weight):
    section_count = lax.axis_size("section")
    section_index = lax.axis_index("section")
    last_section = section_count - 1
    micro_count = inputs.shape[0]
    per_micro = inputs.shape[1]
    row_count = per_micro * PATCHES
    tick_count = micro_count + section_count - 1
    is_attention = section_index % 2 == 0
    layer_routes = lax.dynamic_index_in_dim(routes, section_index // 2, 0, keepdims=False)
    section_table = vectors[0]
    weight_in = in_weight[0]
    weight_out = out_weight[0]
    weight_proj = weight_out[:D]
    scale_factor = HEAD_DIM ** (-0.5)

    def attend_parts(block_in, route_rows):
        grid_start = block_in.astype(jnp.float32).reshape(per_micro, SIDE, SIDE, D)
        padded = pad_grid(grid_start)
        mixed_grid = grid_start + section_table[15]
        for row_shift in range(3):
            for col_shift in range(3):
                window_view = padded[
                    :, row_shift : row_shift + SIDE, col_shift : col_shift + SIDE, :
                ]
                mixed_grid = mixed_grid + window_view * section_table[6 + 3 * row_shift + col_shift]
        mixed_rows = mixed_grid.reshape(row_count, D)
        normed, normal_hat, inverse = layer_norm(mixed_rows, section_table[0], section_table[1])
        normed_low = normed.astype(jnp.bfloat16)
        projected = jnp.dot(normed_low, weight_in, preferred_element_type=jnp.float32).astype(
            jnp.bfloat16
        )
        projected = projected.reshape(per_micro, PATCHES, 3 * D)
        queries = to_regions(projected[:, :, :D]).reshape(
            per_micro, REGIONS, INSIDE, HEADS, HEAD_DIM
        )
        key_value = jnp.concatenate(
            [to_regions(projected[:, :, D : 2 * D]), to_regions(projected[:, :, 2 * D :])], axis=-1
        )
        key_value = key_value.reshape(per_micro, REGIONS, INSIDE * 2 * D)
        chooser = (route_rows[..., None] == jnp.arange(REGIONS, dtype=jnp.int32)).astype(
            jnp.bfloat16
        )
        chooser = chooser.reshape(per_micro, REGIONS * TOPK, REGIONS)
        routed = jnp.einsum(
            "bsr,brf->bsf", chooser, key_value, preferred_element_type=jnp.float32
        ).astype(jnp.bfloat16)
        routed = routed.reshape(per_micro, REGIONS, TOPK * INSIDE, 2, HEADS, HEAD_DIM)
        keys_routed = routed[:, :, :, 0]
        values_routed = routed[:, :, :, 1]
        scores = (
            jnp.einsum(
                "bgphd,bgjhd->bghpj", queries, keys_routed, preferred_element_type=jnp.float32
            )
            * scale_factor
        )
        row_peak = jnp.max(scores, axis=-1, keepdims=True)
        expo_scores = jnp.exp(scores - row_peak)
        attention_weights = expo_scores / jnp.sum(expo_scores, axis=-1, keepdims=True)
        weights_low = attention_weights.astype(jnp.bfloat16)
        attended = jnp.einsum(
            "bghpj,bgjhd->bgphd", weights_low, values_routed, preferred_element_type=jnp.float32
        )
        attended = attended.astype(jnp.bfloat16).reshape(per_micro, REGIONS, INSIDE, D)
        attended_rows = from_regions(attended).reshape(row_count, D)
        return (
            padded,
            mixed_rows,
            normal_hat,
            inverse,
            normed_low,
            queries,
            keys_routed,
            values_routed,
            chooser,
            attention_weights,
            weights_low,
            attended_rows,
        )

    def attention_forward(block_in, route_rows):
        parts = attend_parts(block_in, route_rows)
        branch = (
            jnp.dot(parts[11], weight_proj, preferred_element_type=jnp.float32) + section_table[2]
        )
        return (parts[1] + branch).astype(jnp.bfloat16).reshape(per_micro, PATCHES, D)

    def attention_backward(block_in, route_rows, grad_block):
        (
            padded,
            mixed_rows,
            normal_hat,
            inverse,
            normed_low,
            queries,
            keys_routed,
            values_routed,
            chooser,
            attention_weights,
            weights_low,
            attended_rows,
        ) = attend_parts(block_in, route_rows)
        grad_low = grad_block.reshape(row_count, D)
        grad_rows = grad_low.astype(jnp.float32)
        grad_attended = jnp.dot(grad_low, weight_proj.T, preferred_element_type=jnp.float32).astype(
            jnp.bfloat16
        )
        grad_attended = to_regions(grad_attended.reshape(per_micro, PATCHES, D))
        grad_attended = grad_attended.reshape(per_micro, REGIONS, INSIDE, HEADS, HEAD_DIM)
        grad_weights = jnp.einsum(
            "bgphd,bgjhd->bghpj", grad_attended, values_routed, preferred_element_type=jnp.float32
        )
        grad_scores = attention_weights * (
            grad_weights - jnp.sum(attention_weights * grad_weights, axis=-1, keepdims=True)
        )
        grad_scores_low = grad_scores.astype(jnp.bfloat16)
        grad_queries = (
            jnp.einsum(
                "bghpj,bgjhd->bgphd",
                grad_scores_low,
                keys_routed,
                preferred_element_type=jnp.float32,
            )
            * scale_factor
        )
        grad_keys = (
            jnp.einsum(
                "bghpj,bgphd->bgjhd", grad_scores_low, queries, preferred_element_type=jnp.float32
            )
            * scale_factor
        )
        grad_values = jnp.einsum(
            "bghpj,bgphd->bgjhd", weights_low, grad_attended, preferred_element_type=jnp.float32
        )
        grad_routed = jnp.stack([grad_keys, grad_values], axis=3).reshape(
            per_micro, REGIONS * TOPK, INSIDE * 2 * D
        )
        upper_part = grad_routed.astype(jnp.bfloat16)
        lower_part = (grad_routed - upper_part.astype(jnp.float32)).astype(jnp.bfloat16)
        both_parts = jnp.concatenate([upper_part, lower_part], axis=-1)
        summed_parts = jnp.einsum(
            "bsr,bsf->brf", chooser, both_parts, preferred_element_type=jnp.float32
        )
        width_half = INSIDE * 2 * D
        grad_key_value = summed_parts[..., :width_half] + summed_parts[..., width_half:]
        grad_key_value = grad_key_value.reshape(per_micro, REGIONS, INSIDE, 2 * D)
        grad_projected = jnp.concatenate(
            [
                from_regions(grad_queries.reshape(per_micro, REGIONS, INSIDE, D)),
                from_regions(grad_key_value[..., :D]),
                from_regions(grad_key_value[..., D:]),
            ],
            axis=-1,
        )
        grad_projected = grad_projected.reshape(row_count, 3 * D).astype(jnp.bfloat16)
        grad_normed = jnp.dot(grad_projected, weight_in.T, preferred_element_type=jnp.float32)
        grad_mixed = grad_rows + norm_backward(grad_normed, normal_hat, inverse, section_table[0])
        grad_grid = grad_mixed.reshape(per_micro, SIDE, SIDE, D)
        padded_grad = pad_grid(grad_grid)
        grad_start = grad_grid
        tap_grads = []
        for row_shift in range(3):
            for col_shift in range(3):
                window_view = padded[
                    :, row_shift : row_shift + SIDE, col_shift : col_shift + SIDE, :
                ]
                tap_grads.append(jnp.sum(grad_grid * window_view, axis=(0, 1, 2)))
                back_view = padded_grad[
                    :, 2 - row_shift : 2 - row_shift + SIDE, 2 - col_shift : 2 - col_shift + SIDE, :
                ]
                grad_start = grad_start + back_view * section_table[6 + 3 * row_shift + col_shift]
        zero_row = jnp.zeros((D,), jnp.float32)
        small_grads = jnp.stack(
            [
                jnp.sum(grad_normed * normal_hat, axis=0),
                jnp.sum(grad_normed, axis=0),
                jnp.sum(grad_rows, axis=0),
                zero_row,
                zero_row,
                zero_row,
            ]
            + tap_grads
            + [jnp.sum(grad_mixed, axis=0)]
        )
        middle = jnp.concatenate(
            [attended_rows, jnp.zeros((row_count, 2 * D), jnp.bfloat16)], axis=-1
        )
        return (
            grad_start.reshape(per_micro, PATCHES, D).astype(jnp.bfloat16),
            small_grads,
            normed_low,
            grad_projected,
            middle,
            grad_low,
        )

    def dense_parts(block_in):
        start_rows = block_in.astype(jnp.float32).reshape(row_count, D)
        normed, normal_hat, inverse = layer_norm(start_rows, section_table[0], section_table[1])
        normed_low = normed.astype(jnp.bfloat16)
        hidden = jnp.dot(normed_low, weight_in, preferred_element_type=jnp.float32) + section_table[
            3:6
        ].reshape(HID)
        active_low = exact_gelu(hidden).astype(jnp.bfloat16)
        return (start_rows, normal_hat, inverse, normed_low, hidden, active_low)

    def dense_forward(block_in, route_rows):
        start_rows, normal_hat, inverse, normed_low, hidden, active_low = dense_parts(block_in)
        branch = (
            jnp.dot(active_low, weight_out, preferred_element_type=jnp.float32) + section_table[2]
        )
        return (start_rows + branch).astype(jnp.bfloat16).reshape(per_micro, PATCHES, D)

    def dense_backward(block_in, route_rows, grad_block):
        start_rows, normal_hat, inverse, normed_low, hidden, active_low = dense_parts(block_in)
        grad_low = grad_block.reshape(row_count, D)
        grad_rows = grad_low.astype(jnp.float32)
        grad_active = jnp.dot(grad_low, weight_out.T, preferred_element_type=jnp.float32)
        unused_value, gelu_back = jax.vjp(exact_gelu, hidden)
        grad_hidden_low = gelu_back(grad_active)[0].astype(jnp.bfloat16)
        grad_normed = jnp.dot(grad_hidden_low, weight_in.T, preferred_element_type=jnp.float32)
        grad_start = grad_rows + norm_backward(grad_normed, normal_hat, inverse, section_table[0])
        head_rows = jnp.stack(
            [
                jnp.sum(grad_normed * normal_hat, axis=0),
                jnp.sum(grad_normed, axis=0),
                jnp.sum(grad_rows, axis=0),
            ]
        )
        bias_rows = jnp.sum(grad_hidden_low.astype(jnp.float32), axis=0).reshape(3, D)
        small_grads = jnp.concatenate(
            [head_rows, bias_rows, jnp.zeros((VEC_ROWS - 6, D), jnp.float32)], axis=0
        )
        return (
            grad_start.reshape(per_micro, PATCHES, D).astype(jnp.bfloat16),
            small_grads,
            normed_low,
            grad_hidden_low,
            active_low,
            grad_low,
        )

    zero_block = jnp.zeros((per_micro, PATCHES, D), jnp.bfloat16)
    received = zero_block
    saved_inputs = jnp.zeros((micro_count, per_micro, PATCHES, D), jnp.bfloat16)
    finals = saved_inputs
    for tick_index in range(tick_count):
        micro_index = tick_index - section_index
        is_live = (micro_index >= 0) & (micro_index < micro_count)
        slot_index = jnp.clip(micro_index, 0, micro_count - 1)
        fresh_block = lax.dynamic_index_in_dim(inputs, slot_index, 0, keepdims=False)
        block_in = jnp.where(section_index == 0, fresh_block, received)
        saved_inputs = put_slot(saved_inputs, block_in, slot_index, is_live)
        route_rows = lax.dynamic_index_in_dim(layer_routes, slot_index, 0, keepdims=False)
        result = lax.cond(is_attention, attention_forward, dense_forward, block_in, route_rows)
        finals = put_slot(finals, result, slot_index, is_live & (section_index == last_section))
        if tick_index + 1 < tick_count:
            received = passed_along(result, "section", 1)
    grad_received = zero_block
    first_grads = jnp.zeros_like(saved_inputs)
    small_total = jnp.zeros((VEC_ROWS, D), jnp.float32)
    in_total = jnp.zeros((D, HID), jnp.float32)
    out_total = jnp.zeros((HID, D), jnp.float32)
    for tick_index in range(tick_count):
        micro_index = tick_index - (last_section - section_index)
        is_live = (micro_index >= 0) & (micro_index < micro_count)
        slot_index = jnp.clip(micro_index, 0, micro_count - 1)
        fresh_grad = lax.dynamic_index_in_dim(cotangent, slot_index, 0, keepdims=False)
        grad_block = jnp.where(section_index == last_section, fresh_grad, grad_received)
        block_in = lax.dynamic_index_in_dim(saved_inputs, slot_index, 0, keepdims=False)
        route_rows = lax.dynamic_index_in_dim(layer_routes, slot_index, 0, keepdims=False)
        grad_start, small_part, normed_low, grad_projected, middle, grad_low = lax.cond(
            is_attention, attention_backward, dense_backward, block_in, route_rows, grad_block
        )
        first_grads = put_slot(first_grads, grad_start, slot_index, is_live & (section_index == 0))
        small_part = jnp.where(is_live, small_part, 0.0)
        grad_projected = jnp.where(is_live, grad_projected, jnp.zeros_like(grad_projected))
        grad_low = jnp.where(is_live, grad_low, jnp.zeros_like(grad_low))
        tick_in = row_product(normed_low, grad_projected)
        tick_out = row_product(middle, grad_low)
        small_total = small_total + small_part
        in_total = in_total + tick_in
        out_total = out_total + tick_out
        if tick_index + 1 < tick_count:
            grad_received = passed_along(grad_start, "section", -1)
    summed = lax.psum((small_total, in_total, out_total), "dp")
    image_count = micro_count * per_micro * lax.axis_size("dp")
    all_finals = broadcast(finals, "section", last_section)
    own_final = lax.dynamic_slice_in_dim(all_finals, section_index, 1, 0)
    all_first = broadcast(first_grads, "section", 0)
    own_first = lax.dynamic_slice_in_dim(all_first, section_index, 1, 0)
    return (
        own_final,
        own_first,
        (summed[0] / image_count)[None],
        (summed[1] / image_count)[None],
        (summed[2] / image_count)[None],
    )


def solution(mesh):
    in_specs = (
        P(None, "dp", None, None),
        P(None, "dp", None, None),
        P(None, None, "dp", None, None),
        P("section", None, None),
        P("section", None, None),
        P("section", None, None),
    )
    out_specs = (
        P("section", "dp", None, None),
        P("section", "dp", None, None),
        P("section", None, None),
        P("section", None, None),
        P("section", None, None),
    )
    return jax.shard_map(
        per_device, mesh=mesh, in_specs=in_specs, out_specs=out_specs, check_vma=False
    )
```

profile of v0, /device:TPU:1, one launch (start us, length us, event | category | flops | bytes accessed | tf_op | source)
XLA Modules:
  0.0 1367.5 jit_solution(14880441405552098625)
XLA Ops:
  12.6 35.1 %conditional.22 = (bf16[2,196,256]{2,1,0:T(8,128)(2,1)S(1)}) conditional(s32[]{:T(128)} %convert_element_type.1095, (bf16[2,196,256]{2,1,0:T(8,128)(2,1)S(1)}, f32[16,256]{1,0:T(8,128)S(1)}, bf16[256,768]{1,0:T(8,128)(2,1)S(1)}, bf16[768,256]{1,0:T(8,128)(2,1)S(1)}) %tuple.963, (bf16[2,196,256]{2,1,0:T(8,128)(2,1)S(1)}, f32[16,256]{1,0:T(8,128)S(1)}, ...), branch_computations={%region_0.3_spmd, %region_3.8_spmd} | conditional | flops 329556352 | bytes 25937660 | solution.py:344
  54.0 41.3 %conditional.23 = (bf16[2,196,256]{2,1,0:T(8,128)(2,1)S(1)}) conditional(s32[]{:T(128)} %convert_element_type.1095, (bf16[2,196,256]{2,1,0:T(8,128)(2,1)S(1)}, f32[16,256]{1,0:T(8,128)S(1)}, bf16[256,768]{1,0:T(8,128)(2,1)S(1)}, bf16[768,256]{1,0:T(8,128)(2,1)S(1)}) %tuple.964, (bf16[2,196,256]{2,1,0:T(8,128)(2,1)S(1)}, f32[16,256]{1,0:T(8,128)S(1)}, ...), branch_computations={%region_8.11_spmd, %region_11.16_spmd} | conditional | flops 329556352 | bytes 25937660 | solution.py:344
  100.9 40.8 %conditional.24 = (bf16[2,196,256]{2,1,0:T(8,128)(2,1)S(1)}) conditional(s32[]{:T(128)} %convert_element_type.1095, (bf16[2,196,256]{2,1,0:T(8,128)(2,1)S(1)}, f32[16,256]{1,0:T(8,128)S(1)}, bf16[256,768]{1,0:T(8,128)(2,1)S(1)}, bf16[768,256]{1,0:T(8,128)(2,1)}) %tuple.957, (bf16[2,196,256]{2,1,0:T(8,128)(2,1)S(1)}, f32[16,256]{1,0:T(8,128)S(1)}, ...), branch_computations={%region_16.19_spmd, %region_19.24_spmd} | conditional | flops 329556352 | bytes 25937660 | solution.py:344
  146.8 41.0 %conditional.25 = (bf16[2,196,256]{2,1,0:T(8,128)(2,1)S(1)}) conditional(s32[]{:T(128)} %convert_element_type.1095, (bf16[2,196,256]{2,1,0:T(8,128)(2,1)S(1)}, f32[16,256]{1,0:T(8,128)S(1)}, bf16[256,768]{1,0:T(8,128)(2,1)S(1)}, bf16[768,256]{1,0:T(8,128)(2,1)}) %tuple.958, (bf16[2,196,256]{2,1,0:T(8,128)(2,1)S(1)}, f32[16,256]{1,0:T(8,128)S(1)}, ...), branch_computations={%region_24.27_spmd, %region_27.32_spmd} | conditional | flops 329556352 | bytes 25937660 | solution.py:344
  192.0 40.8 %conditional.26 = (bf16[2,196,256]{2,1,0:T(8,128)(2,1)S(1)}) conditional(s32[]{:T(128)} %convert_element_type.1095, (bf16[2,196,256]{2,1,0:T(8,128)(2,1)S(1)}, f32[16,256]{1,0:T(8,128)S(1)}, bf16[256,768]{1,0:T(8,128)(2,1)S(1)}, bf16[768,256]{1,0:T(8,128)(2,1)}) %tuple.959, (bf16[2,196,256]{2,1,0:T(8,128)(2,1)S(1)}, f32[16,256]{1,0:T(8,128)S(1)}, ...), branch_computations={%region_32.35_spmd, %region_35.40_spmd} | conditional | flops 329556352 | bytes 25937660 | solution.py:344
  237.1 41.0 %conditional.27 = (bf16[2,196,256]{2,1,0:T(8,128)(2,1)S(1)}) conditional(s32[]{:T(128)} %convert_element_type.1095, (bf16[2,196,256]{2,1,0:T(8,128)(2,1)S(1)}, f32[16,256]{1,0:T(8,128)S(1)}, bf16[256,768]{1,0:T(8,128)(2,1)S(1)}, bf16[768,256]{1,0:T(8,128)(2,1)}) %tuple.960, (bf16[2,196,256]{2,1,0:T(8,128)(2,1)S(1)}, f32[16,256]{1,0:T(8,128)S(1)}, ...), branch_computations={%region_40.43_spmd, %region_43.48_spmd} | conditional | flops 329556352 | bytes 25937660 | solution.py:344
  283.3 38.5 %conditional.28 = (bf16[2,196,256]{2,1,0:T(8,128)(2,1)S(1)}) conditional(s32[]{:T(128)} %convert_element_type.1095, (bf16[2,196,256]{2,1,0:T(8,128)(2,1)S(1)}, f32[16,256]{1,0:T(8,128)S(1)}, bf16[256,768]{1,0:T(8,128)(2,1)S(1)}, bf16[768,256]{1,0:T(8,128)(2,1)}) %tuple.961, (bf16[2,196,256]{2,1,0:T(8,128)(2,1)S(1)}, f32[16,256]{1,0:T(8,128)S(1)}, ...), branch_computations={%region_48.51_spmd, %region_51.56_spmd} | conditional | flops 329556352 | bytes 26740504 | solution.py:344
  323.9 121.0 %conditional.29 = (f32[16,256]{1,0:T(8,128)S(1)}, bf16[392,256]{1,0:T(8,128)(2,1)S(1)}, bf16[392,768]{1,0:T(8,128)(2,1)}, bf16[392,768]{1,0:T(8,128)(2,1)}, bf16...) conditional(s32[]{:T(128)} %convert_element_type.1095, (bf16[2,196,256]{2,1,0:T(8,128)(2,1)S(1)}, ...), branch_computations={%region_57.66_spmd, %region_66.87_spmd} | conditional | flops 637869632 | bytes 96718168
  403.0 15.4 %copy.1480 = f32[2,49,16,2,8,32]{5,4,3,2,1,0:T(8,128)} copy(f32[2,49,16,2,8,32]{5,2,4,1,0,3:T(8,128)} %pad_maximum_fusion.7) | data formatting | bytes 6422528 | tf_op jit(solution)/shard_map/cond/branch_1_fun/stack | solution.py:224
  451.4 115.6 %conditional.30 = (f32[16,256]{1,0:T(8,128)S(1)}, bf16[392,256]{1,0:T(8,128)(2,1)S(1)}, bf16[392,768]{1,0:T(8,128)(2,1)}, bf16[392,768]{1,0:T(8,128)(2,1)}, bf16...) conditional(s32[]{:T(128)} %convert_element_type.1095, (bf16[2,196,256]{2,1,0:T(8,128)(2,1)S(1)}, ...), branch_computations={%region_87.96_spmd, %region_96.117_spmd} | conditional | flops 637869632 | bytes 102337976
  524.0 15.4 %copy.1521 = f32[2,49,16,2,8,32]{5,4,3,2,1,0:T(8,128)} copy(f32[2,49,16,2,8,32]{5,2,4,1,0,3:T(8,128)} %pad_maximum_fusion.9) | data formatting | bytes 6422528 | tf_op jit(solution)/shard_map/cond/branch_1_fun/stack | solution.py:224
  574.0 117.9 %conditional.31 = (f32[16,256]{1,0:T(8,128)S(1)}, bf16[392,256]{1,0:T(8,128)(2,1)}, bf16[392,768]{1,0:T(8,128)(2,1)}, bf16[392,768]{1,0:T(8,128)(2,1)}, bf16[392...) conditional(s32[]{:T(128)} %convert_element_type.1095, (bf16[2,196,256]{2,1,0:T(8,128)(2,1)S(1)}, ...), branch_computations={%region_117.126_spmd, %region_126.147_spmd} | conditional | flops 637869632 | bytes 101535128
  649.2 15.4 %copy.1562 = f32[2,49,16,2,8,32]{5,4,3,2,1,0:T(8,128)} copy(f32[2,49,16,2,8,32]{5,2,4,1,0,3:T(8,128)} %pad_maximum_fusion.11) | data formatting | bytes 6422528 | tf_op jit(solution)/shard_map/cond/branch_1_fun/stack | solution.py:224
  699.5 118.0 %conditional.32 = (f32[16,256]{1,0:T(8,128)S(1)}, bf16[392,256]{1,0:T(8,128)(2,1)}, bf16[392,768]{1,0:T(8,128)(2,1)}, bf16[392,768]{1,0:T(8,128)(2,1)}, bf16[392...) conditional(s32[]{:T(128)} %convert_element_type.1095, (bf16[2,196,256]{2,1,0:T(8,128)(2,1)S(1)}, ...), branch_computations={%region_147.156_spmd, %region_156.177_spmd} | conditional | flops 637869632 | bytes 101535128
  774.6 15.4 %copy.1603 = f32[2,49,16,2,8,32]{5,4,3,2,1,0:T(8,128)} copy(f32[2,49,16,2,8,32]{5,2,4,1,0,3:T(8,128)} %pad_maximum_fusion.13) | data formatting | bytes 6422528 | tf_op jit(solution)/shard_map/cond/branch_1_fun/stack | solution.py:224
  825.9 118.2 %conditional.33 = (f32[16,256]{1,0:T(8,128)S(1)}, bf16[392,256]{1,0:T(8,128)(2,1)}, bf16[392,768]{1,0:T(8,128)(2,1)}, bf16[392,768]{1,0:T(8,128)(2,1)}, bf16[392...) conditional(s32[]{:T(128)} %convert_element_type.1095, (bf16[2,196,256]{2,1,0:T(8,128)(2,1)S(1)}, ...), branch_computations={%region_177.186_spmd, %region_186.207_spmd} | conditional | flops 637869632 | bytes 101535128
  901.0 15.4 %copy.1644 = f32[2,49,16,2,8,32]{5,4,3,2,1,0:T(8,128)} copy(f32[2,49,16,2,8,32]{5,2,4,1,0,3:T(8,128)} %pad_maximum_fusion.15) | data formatting | bytes 6422528 | tf_op jit(solution)/shard_map/cond/branch_1_fun/stack | solution.py:224
  952.6 117.2 %conditional.34 = (f32[16,256]{1,0:T(8,128)S(1)}, bf16[392,256]{1,0:T(8,128)(2,1)}, bf16[392,768]{1,0:T(8,128)(2,1)}, bf16[392,768]{1,0:T(8,128)(2,1)}, bf16[392...) conditional(s32[]{:T(128)} %convert_element_type.1095, (bf16[2,196,256]{2,1,0:T(8,128)(2,1)S(1)}, ...), branch_computations={%region_207.216_spmd, %region_216.237_spmd} | conditional | flops 637869632 | bytes 101535128
  1027.4 15.4 %copy.1685 = f32[2,49,16,2,8,32]{5,4,3,2,1,0:T(8,128)} copy(f32[2,49,16,2,8,32]{5,2,4,1,0,3:T(8,128)} %pad_maximum_fusion.17) | data formatting | bytes 6422528 | tf_op jit(solution)/shard_map/cond/branch_1_fun/stack | solution.py:224
  1076.6 117.3 %conditional.35 = (f32[16,256]{1,0:T(8,128)S(1)}, bf16[392,256]{1,0:T(8,128)(2,1)}, bf16[392,768]{1,0:T(8,128)(2,1)}, bf16[392,768]{1,0:T(8,128)(2,1)}, bf16[392...) conditional(s32[]{:T(128)} %convert_element_type.1095, (bf16[2,196,256]{2,1,0:T(8,128)(2,1)S(1)}, ...), branch_computations={%region_237.246_spmd, %region_246.267_spmd} | conditional | flops 637869632 | bytes 101535128
  1151.7 15.4 %copy.1726 = f32[2,49,16,2,8,32]{5,4,3,2,1,0:T(8,128)} copy(f32[2,49,16,2,8,32]{5,2,4,1,0,3:T(8,128)} %pad_maximum_fusion.19) | data formatting | bytes 6422528 | tf_op jit(solution)/shard_map/cond/branch_1_fun/stack | solution.py:224
  1202.1 29.6 %psum.37 = f32[16,256]{1,0:T(8,128)S(1)} all-reduce(f32[16,256]{1,0:T(8,128)S(1)} %select_add_fusion), channel_id=1, replica_groups=mesh['section'=4,'dp'=8] {'dp'}, use_global_device_ids=true, to_apply=%region_268.269 | all-reduce | flops 4096 | bytes 32768 | tf_op jit(solution)/shard_map/psum | solution.py:375
  1232.3 58.3 %all-reduce.33.cloned.1.call-done = (f32[256,768]{1,0:T(8,128)}, f32[768,256]{1,0:T(8,128)}) async-done(((f32[256,768]{1,0:T(8,128)}, f32[768,256]{1,0:T(8,128)}), (f32[256,768]{1,0:T(8,128)}, f32[768,256]{1,0:T(8,128)})) %all-reduce.33.cloned.1.call-update) | async-done | bytes 1572880 | tf_op jit(solution)/shard_map/psum | solution.py:375
  1293.6 63.2 %all-reduce.35.cloned.1.call-done = (bf16[4,2,196,256]{3,2,1,0:T(8,128)(2,1)}, bf16[4,2,196,256]{3,2,1,0:T(8,128)(2,1)}) async-done(((bf16[4,2,196,256]{3,2,1,0:T(8,128)(2,1)}, bf16[4,2,196,256]{3,2,1,0:T(8,128)(2,1)}), (bf16[4,2,196,256]{3,2,1,0:T(8,128)(2,1)}, bf16[4,2,196,256]{3,2,1,0:T(8,128)(2,1)})) %all-reduce.35.cloned.1.call-update) | async-done | bytes 1605648 | tf_op jit(solution)/shard_map/psum | solution.py:30
  (1287 shorter events, 1084.2 us)
Async XLA Ops:
  7.2 1283.4 %all-reduce.33.cloned.1.call-start = ((), (), s32[]{:S(2)}) async-start(), calls=%async_computation | async-start | bytes 3145728 | tf_op jit(solution)/shard_map/psum | solution.py:375
  28.6 8.4 copy-start.134
  47.8 6.1 collective-permute-start
  95.3 5.5 collective-permute-start.1
  141.8 4.9 collective-permute-start.2
  167.0 8.4 copy-start.137
  187.8 4.1 collective-permute-start.3
  232.8 4.1 collective-permute-start.4
  278.1 4.1 collective-permute-start.5
  283.3 39.5 %copy-start.7 = (bf16[2,196,256]{2,1,0:T(8,128)(2,1)S(1)}, bf16[2,196,256]{2,1,0:T(8,128)(2,1)}, u32[]{:S(2)}) copy-start(bf16[2,196,256]{2,1,0:T(8,128)(2,1)} %fusion.1037) | copy-start | bytes 602116
  324.0 117.4 %copy-start.59 = (bf16[392,256]{1,0:T(8,128)(2,1)}, bf16[392,256]{1,0:T(8,128)(2,1)S(1)}, u32[]{:S(2)}) copy-start(bf16[392,256]{1,0:T(8,128)(2,1)S(1)} %reshape.2789) | copy-start | bytes 602116 | tf_op jit(solution)/shard_map/conditional
  444.9 6.5 collective-permute-start.6
  451.6 111.1 %copy-start.8 = (bf16[392,256]{1,0:T(8,128)(2,1)}, bf16[392,256]{1,0:T(8,128)(2,1)S(1)}, u32[]{:S(2)}) copy-start(bf16[392,256]{1,0:T(8,128)(2,1)S(1)} %reshape.2817) | copy-start | bytes 602116 | tf_op jit(solution)/shard_map/conditional.1
  567.1 6.8 collective-permute-start.7
  574.2 113.3 %copy-start.10 = (bf16[392,256]{1,0:T(8,128)(2,1)}, bf16[392,256]{1,0:T(8,128)(2,1)S(1)}, u32[]{:S(2)}) copy-start(bf16[392,256]{1,0:T(8,128)(2,1)S(1)} %reshape.2845) | copy-start | bytes 602116 | tf_op jit(solution)/shard_map/conditional.2
  692.0 7.2 collective-permute-start.8
  699.7 113.3 %copy-start.12 = (bf16[392,256]{1,0:T(8,128)(2,1)}, bf16[392,256]{1,0:T(8,128)(2,1)S(1)}, u32[]{:S(2)}) copy-start(bf16[392,256]{1,0:T(8,128)(2,1)S(1)} %reshape.2873) | copy-start | bytes 602116 | tf_op jit(solution)/shard_map/conditional.3
  817.5 8.4 collective-permute-start.9
  826.1 113.3 %copy-start.14 = (bf16[392,256]{1,0:T(8,128)(2,1)}, bf16[392,256]{1,0:T(8,128)(2,1)S(1)}, u32[]{:S(2)}) copy-start(bf16[392,256]{1,0:T(8,128)(2,1)S(1)} %reshape.2901) | copy-start | bytes 602116 | tf_op jit(solution)/shard_map/conditional.4
  944.2 8.4 collective-permute-start.10
  952.8 113.3 %copy-start.16 = (bf16[392,256]{1,0:T(8,128)(2,1)}, bf16[392,256]{1,0:T(8,128)(2,1)S(1)}, u32[]{:S(2)}) copy-start(bf16[392,256]{1,0:T(8,128)(2,1)S(1)} %reshape.2929) | copy-start | bytes 602116 | tf_op jit(solution)/shard_map/conditional.5
  1069.9 6.6 collective-permute-start.11
  1076.7 113.3 %copy-start.18 = (bf16[392,256]{1,0:T(8,128)(2,1)}, bf16[392,256]{1,0:T(8,128)(2,1)S(1)}, u32[]{:S(2)}) copy-start(bf16[392,256]{1,0:T(8,128)(2,1)S(1)} %reshape.2957) | copy-start | bytes 602116 | tf_op jit(solution)/shard_map/conditional.7
  1199.1 157.7 %all-reduce.35.cloned.1.call-start = ((), (), s32[]{:S(2)}) async-start(), calls=%async_computation.1 | async-start | bytes 3276800 | tf_op jit(solution)/shard_map/psum | solution.py:30
  (172 other events, 591.3 us)
Sparse Core Ops, SparseCore 0:
  1199.2 91.2 all-reduce.32
  1293.7 63.1 all-reduce.34
where the time goes:
time: 1380 us; the launch traced here: 1370 us
  local copies, waits for them, and re-layouts  618 us (45%)
  matrix products  325 us (24%)
  other arithmetic  223 us (16%)
  waiting for transfers between devices  130 us (9%)
  blocking collectives  29.6 us (2%)
  starting transfers between devices  17.8 us (1%)
  between operations  15.1 us (1%)
    slice x14, local copies, waits for them, and re-layouts, attend_parts(): keys_routed = routed[:, :, :, 0]  117 us
    another operation x7, local copies, waits for them, and re-layouts, attention_backward(): jnp.stack([grad_keys, grad_values], axis=3)  108 us
    reshape x14, local copies, waits for them, and re-layouts, attend_parts(): routed.reshape(per_micro, REGIONS, TOPK * INSIDE, 2, HEADS, HEAD_DIM)  99.9 us
    reshape x7, local copies, waits for them, and re-layouts, attention_backward(): jnp.stack([grad_keys, grad_values], axis=3)  98.8 us
    another operation x7, other arithmetic, attention_backward(): jnp.stack([grad_keys, grad_values], axis=3)  84.3 us
    sub x14, matrix products, attend_parts(): expo_scores = jnp.exp(scores - row_peak)  75.3 us
    psum x1, waiting for transfers between devices, broadcast(): return lax.psum(block, axis)  63.2 us
    dot_general x14, matrix products, attend_parts(): jnp.einsum('bghpj,bgjhd->bgphd', weights_low, values_routed, preferred_el...  58.5 us
  transfers between devices with their start and end apart: 14, of which 10 were waited for; matrix products, arithmetic and copies ran while one was open for 4% of the time, Pallas kernels for 0%

commit v1 on v0

v1 whole, which is shorter than its diff:
```python
import functools

import jax
import jax.numpy as jnp
from jax import lax
from jax.experimental import pallas as pl
from jax.experimental.pallas import tpu as pltpu
from jax.sharding import PartitionSpec as P

D = 256
HEADS = 8
HEAD_DIM = 32
HID = 768
SIDE = 14
WIN = 7
TOPK = 4
SECTIONS = 4
VEC_ROWS = 16
PATCHES = 196
REGIONS = 49
EPSILON = 1e-06

PITCH = 16
LIVE = SIDE * PITCH
ROWS = 256
HALO = 24
NEGATIVE = -1e30
LOG2E = 1.4426950408889634
SCALE = HEAD_DIM ** (-0.5)

BF = jnp.bfloat16
F32 = jnp.float32


def dot(a, b, ca=1, cb=0):
    return lax.dot_general(
        a, b, (((ca,), (cb,)), ((), ())), preferred_element_type=jnp.float32
    )


def iota(shape, dim):
    return lax.broadcasted_iota(jnp.int32, shape, dim)


def one_hot(cond):
    return jnp.where(cond, 1.0, 0.0).astype(BF)


def rows_of(i, count=LIVE):
    return pl.ds(pl.multiple_of(i * ROWS, ROWS), count)


def col_sum(x):
    return jnp.sum(x, axis=0, keepdims=True)


def ln_stats(x):
    average = jnp.mean(x, axis=-1, keepdims=True)
    centred = x - average
    spread = jnp.mean(centred * centred, axis=-1, keepdims=True)
    inverse = lax.rsqrt(spread + EPSILON)
    return centred * inverse, inverse


def gelu_pair(x):
    a = jnp.abs(x)
    t = 1.0 / (1.0 + a * (0.3275911 * 0.7071067811865476))
    e = jnp.exp2(x * x * (-0.5 * LOG2E))
    w = t * (0.5 * 1.061405429) + (0.5 * -1.453152027)
    w = w * t + (0.5 * 1.421413741)
    w = w * t + (0.5 * -0.284496736)
    w = w * t + (0.5 * 0.254829592)
    w = w * t * e
    phi = jnp.where(x >= 0, 1.0 - w, w)
    return x * phi, phi + x * e * 0.3989422804014327


def live_mask():
    token = iota((LIVE, D), 0)
    return (token & (PITCH - 1)) < SIDE


def region_one_hot(shape, token_dim):
    token = iota(shape, token_dim)
    region = iota(shape, 1 - token_dim)
    r, c = token >> 4, token & (PITCH - 1)
    own = (r >> 1) * WIN + (c >> 1)
    return one_hot((own == region) & (c < SIDE) & (r < SIDE))


def compute_kernel(
    n,
    x_ref, cot_ref, routes_ref, vec_ref, win_ref, wout_ref,
    fin_ref, gin_ref, gvec_ref, ga_ref, gb_ref,
    hs, zh, inv, nm, pr, pt, at, act, gp, bias, mixed, g, dproj, cv, dom, qm, dsb, tmp, dqt, km, wide,
):
    eye = one_hot(iota((ROWS, ROWS), 0) == iota((ROWS, ROWS), 1))

    def transposed(x):
        return dot(eye, x, 1, 1)

    def head_lanes(h):
        return (iota((ROWS, D), 1) >> 5) == h

    def spread():
        t, p = iota((ROWS, PATCHES), 0), iota((ROWS, PATCHES), 1)
        r, c = t >> 4, t & (PITCH - 1)
        return one_hot((p == r * SIDE + c) & (c < SIDE) & (r < SIDE))

    def gather():
        p, t = iota((PATCHES, ROWS), 0), iota((PATCHES, ROWS), 1)
        r, c = t >> 4, t & (PITCH - 1)
        return one_hot((p == r * SIDE + c) & (c < SIDE) & (r < SIDE))

    zero_tail = jnp.zeros((ROWS - LIVE, D), F32)
    tail = lambda i: pl.ds(i * ROWS + LIVE, ROWS - LIVE)
    cv[0:HALO] = jnp.zeros((HALO, D), F32)
    cv[HALO + LIVE : HALO + LIVE + HALO] = jnp.zeros((HALO, D), F32)
    zero_wide = jnp.zeros((ROWS - LIVE, HID), BF)
    for i in range(n):
        for s in range(SECTIONS):
            nm[s, tail(i)] = zero_tail.astype(BF)
            hs[s, tail(i)] = zero_tail.astype(BF)
        for a in range(2):
            pr[a, tail(i)] = zero_wide
            act[a, tail(i)] = zero_wide
            at[a, tail(i)] = zero_tail.astype(BF)
        g[tail(i)] = zero_tail.astype(BF)
        dproj[tail(i)] = zero_wide

    spread_one = spread()
    key_region = region_one_hot((LIVE, REGIONS), 0)
    query_region = region_one_hot((REGIONS, ROWS), 1)
    for i in range(n):
        hs[0, pl.ds(i * ROWS, ROWS)] = dot(spread_one, x_ref[i]).astype(BF)
        g[pl.ds(i * ROWS, ROWS)] = dot(spread_one, cot_ref[i]).astype(BF)
        for a in range(2):
            picks = routes_ref[a, i]
            lane = iota((REGIONS, REGIONS), 1)
            routed = jnp.zeros((REGIONS, REGIONS), F32)
            for k in range(TOPK):
                routed = routed + jnp.where(picks[:, k : k + 1] == lane, 1.0, 0.0)
            by_region = dot(key_region, routed.astype(BF), 1, 1).astype(BF)
            bias[a, i] = (1.0 - dot(by_region, query_region)) * NEGATIVE

    def conv_load(x):
        cv[HALO : HALO + LIVE] = x

    def conv_at(r, shift):
        return cv[pl.ds(HALO + r * PITCH + shift, PITCH)]

    def attention_forward(s):
        a = s // 2
        vec = vec_ref.at[s]

        def image(i, carry):
            rows = rows_of(i)
            conv_load(hs[s, rows].astype(F32))
            for r in range(SIDE):
                total = conv_at(r, 0) + vec[15:16]
                for u in range(3):
                    for v in range(3):
                        j = 6 + 3 * u + v
                        total = total + conv_at(r, (u - 1) * PITCH + v - 1) * vec[j : j + 1]
                mixed[r * PITCH : (r + 1) * PITCH] = total
            hat, inverse = ln_stats(mixed[...])
            zh[s, rows] = hat
            inv[s, rows] = inverse
            normed = (hat * vec[0:1] + vec[1:2]).astype(BF)
            nm[s, rows] = normed
            pr[a, rows] = dot(normed, win_ref[s]).astype(BF)
            whole = rows_of(i, ROWS)
            tmp[...] = transposed(pr[a, whole, 2 * D : 3 * D]).astype(BF)

            def head(h, carry):
                lanes = pl.ds(pl.multiple_of(h * ROWS, ROWS), ROWS)
                own = pl.ds(pl.multiple_of(h * HEAD_DIM, HEAD_DIM), HEAD_DIM)
                keys = jnp.where(head_lanes(h)[:LIVE], pr[a, rows, D : 2 * D], jnp.zeros((), BF))
                scores = dot(keys, pr[a, whole, 0:D], 1, 1) * (SCALE * LOG2E) + bias[a, i]
                expo = jnp.exp2(scores - jnp.max(scores, axis=0, keepdims=True))
                weights = (expo * (1.0 / col_sum(expo))).astype(BF)
                pt[a, i, :, lanes] = weights
                dqt[own] = dot(tmp[own, 0:LIVE], weights)
                return carry

            lax.fori_loop(0, HEADS, head, 0)
            attended = transposed(dqt[...].astype(BF)).astype(BF)
            at[a, whole] = attended
            out = mixed[...] + dot(attended[:LIVE], wout_ref[s, 0:D]) + vec[2:3]
            hs[s + 1, rows] = out.astype(BF)
            return carry

        lax.fori_loop(0, n, image, 0)

    def dense_forward(s):
        a = s // 2
        vec = vec_ref.at[s]

        def image(i, carry):
            rows = rows_of(i)
            start = hs[s, rows].astype(F32)
            hat, inverse = ln_stats(start)
            zh[s, rows] = hat
            inv[s, rows] = inverse
            normed = (hat * vec[0:1] + vec[1:2]).astype(BF)
            nm[s, rows] = normed
            for j in range(3):
                lanes = slice(j * D, (j + 1) * D)
                hidden = dot(normed, win_ref[s, :, lanes]) + vec[3 + j : 4 + j]
                value, slope = gelu_pair(hidden)
                act[a, rows, lanes] = value.astype(BF)
                gp[a, rows, lanes] = slope
            out = start + dot(act[a, rows], wout_ref[s]) + vec[2:3]
            if s + 1 < SECTIONS:
                hs[s + 1, rows] = jnp.where(live_mask(), out, 0.0).astype(BF)
            else:
                dom[0:LIVE] = out.astype(BF)
                dom[LIVE:ROWS] = jnp.zeros((ROWS - LIVE, D), BF)
                fin_ref[i] = dot(gather(), dom[0:ROWS]).astype(BF)
            return carry

        lax.fori_loop(0, n, image, 0)

    def norm_backward(s, rows, d_normed):
        vec = vec_ref.at[s]
        hat = zh[s, rows]
        scaled = d_normed * vec[0:1]
        first = jnp.mean(scaled, axis=-1, keepdims=True)
        second = jnp.mean(scaled * hat, axis=-1, keepdims=True)
        gvec_ref[s, 0:1] += col_sum(d_normed * hat)
        gvec_ref[s, 1:2] += col_sum(d_normed)
        return inv[s, rows] * (scaled - first - hat * second)

    def dense_backward(s):
        a = s // 2

        def image(i, carry):
            rows = rows_of(i)
            grad = g[rows]
            gvec_ref[s, 2:3] += col_sum(grad.astype(F32))
            for j in range(3):
                lanes = slice(j * D, (j + 1) * D)
                d_active = dot(grad, wout_ref[s, lanes], 1, 1)
                d_hidden = (d_active * gp[a, rows, lanes]).astype(BF)
                dproj[rows, lanes] = d_hidden
                gvec_ref[s, 3 + j : 4 + j] += col_sum(d_hidden.astype(F32))
            d_normed = dot(dproj[rows], win_ref[s], 1, 1)
            out = grad.astype(F32) + norm_backward(s, rows, d_normed)
            wide[rows] = out.astype(BF)
            return carry

        lax.fori_loop(0, n, image, 0)
        ga_ref[s] = dot(nm[s], dproj[...], 0, 0)
        gb_ref[s] = dot(act[a], g[...], 0, 0)
        for i in range(n):
            g[pl.ds(i * ROWS, LIVE)] = wide[pl.ds(i * ROWS, LIVE)]

    def attention_backward(s):
        a = s // 2
        vec = vec_ref.at[s]

        def image(i, carry):
            rows = rows_of(i)
            whole = rows_of(i, ROWS)
            grad = g[rows]
            gvec_ref[s, 2:3] += col_sum(grad.astype(F32))
            d_attended = dot(g[whole], wout_ref[s, 0:D], 1, 1).astype(BF)
            tmp[...] = transposed(pr[a, whole, D : 2 * D]).astype(BF)
            km[...] = d_attended

            def head(h, carry):
                lanes = pl.ds(pl.multiple_of(h * ROWS, ROWS), ROWS)
                own = pl.ds(pl.multiple_of(h * HEAD_DIM, HEAD_DIM), HEAD_DIM)
                mine = head_lanes(h)
                nothing = jnp.zeros((), BF)
                values = jnp.where(mine[:LIVE], pr[a, rows, 2 * D : 3 * D], nothing)
                d_weights = dot(values, km[...], 1, 1)
                weights = pt[a, i, :, lanes].astype(F32)
                both = weights * d_weights
                d_scores = (both - weights * col_sum(both)).astype(BF)
                dsb[:, lanes] = d_scores
                dqt[own] = dot(tmp[own, 0:LIVE], d_scores)
                dom[lanes] = jnp.where(mine, km[...], nothing)
                qm[lanes] = jnp.where(mine, pr[a, whole, 0:D], nothing)
                return carry

            lax.fori_loop(0, HEADS, head, 0)
            dproj[rows, 0:D] = (transposed(dqt[...].astype(BF))[:LIVE] * SCALE).astype(BF)
            dproj[rows, D : 2 * D] = (dot(dsb[...], qm[...]) * SCALE).astype(BF)
            dproj[rows, 2 * D : 3 * D] = dot(pt[a, i], dom[...]).astype(BF)
            d_normed = dot(dproj[rows], win_ref[s], 1, 1)
            d_mixed = grad.astype(F32) + norm_backward(s, rows, d_normed)
            gvec_ref[s, 15:16] += col_sum(d_mixed)
            conv_load(d_mixed)
            taps = [jnp.zeros((PITCH, D), F32) for _ in range(9)]
            for r in range(SIDE):
                here = hs[s, pl.ds(pl.multiple_of(i * ROWS + r * PITCH, PITCH), PITCH)].astype(F32)
                total = conv_at(r, 0)
                for u in range(3):
                    for v in range(3):
                        j = 3 * u + v
                        moved = conv_at(r, (1 - u) * PITCH + 1 - v)
                        total = total + moved * vec[6 + j : 7 + j]
                        taps[j] = taps[j] + moved * here
                token = iota((PITCH, D), 0)
                total = jnp.where(token < SIDE, total, 0.0)
                wide[pl.ds(pl.multiple_of(i * ROWS + r * PITCH, PITCH), PITCH)] = total.astype(BF)
            for j in range(9):
                gvec_ref[s, 6 + j : 7 + j] += col_sum(taps[j])
            return carry

        lax.fori_loop(0, n, image, 0)
        ga_ref[s] = dot(nm[s], dproj[...], 0, 0)
        gb_ref[s, 0:D] = dot(at[a], g[...], 0, 0)
        gb_ref[s, D:HID] = jnp.zeros((HID - D, D), F32)
        for i in range(n):
            g[pl.ds(i * ROWS, LIVE)] = wide[pl.ds(i * ROWS, LIVE)]

    gvec_ref[...] = jnp.zeros_like(gvec_ref)
    attention_forward(0)
    dense_forward(1)
    attention_forward(2)
    dense_forward(3)
    dense_backward(3)
    attention_backward(2)
    dense_backward(1)
    attention_backward(0)
    for i in range(n):
        gin_ref[i] = dot(gather(), g[pl.ds(i * ROWS, ROWS)]).astype(BF)


def compute(x, cot, routes, vec, win, wout):
    n = x.shape[0]
    total = n * ROWS
    vmem = pl.BlockSpec(memory_space=pltpu.VMEM)
    return pl.pallas_call(
        functools.partial(compute_kernel, n),
        out_shape=(
            jax.ShapeDtypeStruct(x.shape, BF),
            jax.ShapeDtypeStruct(x.shape, BF),
            jax.ShapeDtypeStruct((SECTIONS, VEC_ROWS, D), F32),
            jax.ShapeDtypeStruct((SECTIONS, D, HID), F32),
            jax.ShapeDtypeStruct((SECTIONS, HID, D), F32),
        ),
        in_specs=[vmem] * 6,
        out_specs=(vmem,) * 5,
        scratch_shapes=[
            pltpu.VMEM((SECTIONS, total, D), BF),
            pltpu.VMEM((SECTIONS, total, D), F32),
            pltpu.VMEM((SECTIONS, total, 1), F32),
            pltpu.VMEM((SECTIONS, total, D), BF),
            pltpu.VMEM((2, total, HID), BF),
            pltpu.VMEM((2, n, LIVE, HEADS * ROWS), BF),
            pltpu.VMEM((2, total, D), BF),
            pltpu.VMEM((2, total, HID), BF),
            pltpu.VMEM((2, total, HID), F32),
            pltpu.VMEM((2, n, LIVE, ROWS), F32),
            pltpu.VMEM((LIVE, D), F32),
            pltpu.VMEM((total, D), BF),
            pltpu.VMEM((total, HID), BF),
            pltpu.VMEM((LIVE + 2 * HALO, D), F32),
            pltpu.VMEM((HEADS * ROWS, D), BF),
            pltpu.VMEM((HEADS * ROWS, D), BF),
            pltpu.VMEM((LIVE, HEADS * ROWS), BF),
            pltpu.VMEM((D, ROWS), BF),
            pltpu.VMEM((D, ROWS), F32),
            pltpu.VMEM((ROWS, D), BF),
            pltpu.VMEM((total, D), BF),
        ],
        compiler_params=pltpu.CompilerParams(vmem_limit_bytes=56 * 1024 * 1024),
        name="two_layers",
    )(x, cot, routes, vec, win, wout)


def per_device(inputs, cotangent, routes, vectors, in_weight, out_weight):
    section = lax.axis_index("section")
    x = lax.dynamic_index_in_dim(inputs, section, 0, keepdims=False)
    cot = lax.dynamic_index_in_dim(cotangent, section, 0, keepdims=False)
    picks = lax.dynamic_index_in_dim(routes, section, 1, keepdims=False)
    vec = lax.all_gather(vectors[0], "section")
    win = lax.all_gather(in_weight[0], "section")
    wout = lax.all_gather(out_weight[0], "section")
    fin, gin, gvec, ga, gb = compute(x, cot, picks, vec, win, wout)
    images = inputs.shape[0] * inputs.shape[1] * lax.axis_size("dp")
    gvec, ga, gb = (lax.psum_scatter(v, "section") for v in (gvec, ga, gb))
    gvec, ga, gb = lax.psum((gvec, ga, gb), "dp")
    return (
        fin[None],
        gin[None],
        (gvec / images)[None],
        (ga / images)[None],
        (gb / images)[None],
    )


def solution(mesh):
    in_specs = (
        P(None, "dp", None, None),
        P(None, "dp", None, None),
        P(None, None, "dp", None, None),
        P("section", None, None),
        P("section", None, None),
        P("section", None, None),
    )
    out_specs = (
        P("section", "dp", None, None),
        P("section", "dp", None, None),
        P("section", None, None),
        P("section", None, None),
        P("section", None, None),
    )
    return jax.shard_map(
        per_device, mesh=mesh, in_specs=in_specs, out_specs=out_specs, check_vma=False
    )
```

time: 1380 us -> 325 us (0.24)
  local copies, waits for them, and re-layouts: 618 us -> 5.17 us
  matrix products: 325 us -> 0 us
  other arithmetic: 223 us -> 4.73 us
  waiting for transfers between devices: 130 us -> 209 us
  Pallas kernels: 0 us -> 55.1 us
  starting transfers between devices: 17.8 us -> 0.23 us
    reshape x175 -> x0, local copies, waits for them, and re-layouts: 277 us -> none  [the longest x14 99.9 us: attend_parts(): routed.reshape(per_micro, REGIONS, TOPK * INSIDE, 2, HEADS, HEAD_DIM)]
    dot_general x112 -> x0, matrix products: 250 us -> none  [the longest x14 58.5 us: attend_parts(): jnp.einsum('bghpj,bgjhd->bgphd', weights_low, values_routed, preferred_el...]
    another operation x316 -> x0, local copies, waits for them, and re-layouts: 132 us -> none  [the longest x7 108 us: attention_backward(): jnp.stack([grad_keys, grad_values], axis=3)]
    slice x92 -> x0, local copies, waits for them, and re-layouts: 126 us -> none  [the longest x14 117 us: attend_parts(): keys_routed = routed[:, :, :, 0]]
    unnamed x2 -> x9, waiting for transfers between devices: 0.03 us -> 116 us
    another operation x14 -> x0, other arithmetic: 85 us -> none  [the longest x7 84.3 us: attention_backward(): jnp.stack([grad_keys, grad_values], axis=3)]
    psum x2 -> x1, waiting for transfers between devices: 122 us -> 37.4 us  [per_device(): gvec, ga, gb = lax.psum((gvec, ga, gb), 'dp')]
    sub x14 -> x0, matrix products: 75.3 us -> none  [attend_parts(): expo_scores = jnp.exp(scores - row_peak)]
  transfers between devices with their start and end apart: 14 -> 6, of which waited for: 10 -> 6; matrix products, arithmetic and copies ran while one was open for 4% -> 2% of each run, Pallas kernels for 0% -> 0%
where the time goes in v1:
time: 325 us; the launch traced here: 322 us
  waiting for transfers between devices  209 us (64%)
  Pallas kernels  55.1 us (17%)
  blocking collectives  34.1 us (10%)
  between operations  14.2 us (4%)
  local copies, waits for them, and re-layouts  5.17 us (2%)
  other arithmetic  4.73 us (1%)
    unnamed x9, waiting for transfers between devices  116 us
    pallas_call x1, Pallas kernels, compute(): pl.pallas_call(functools.partial(compute_kernel, n), out_shape=(jax.Shape...  55.1 us
    psum x1, waiting for transfers between devices, per_device(): gvec, ga, gb = lax.psum((gvec, ga, gb), 'dp')  37.4 us
    all_gather x1, waiting for transfers between devices, per_device(): wout = lax.all_gather(out_weight[0], 'section')  32.8 us
    psum x1, blocking collectives, per_device(): gvec, ga, gb = lax.psum((gvec, ga, gb), 'dp')  25.4 us
    all_gather x1, waiting for transfers between devices, per_device(): win = lax.all_gather(in_weight[0], 'section')  22.1 us
    all_gather x1, blocking collectives, per_device(): vec = lax.all_gather(vectors[0], 'section')  8.74 us
  transfers between devices with their start and end apart: 6, of which 6 were waited for; matrix products, arithmetic and copies ran while one was open for 2% of the time, Pallas kernels for 0%

profile of v1, /device:TPU:1, one launch (start us, length us, event | category | flops | bytes accessed | tf_op | source)
XLA Modules:
  0.0 322.1 jit_solution(5566430326823035984)
XLA Ops:
  7.2 0.7 all-gather.3.cloned.1.call-update
  8.0 0.7 all-gather.5.cloned.1.call-update
  8.7 0.0 reduce-scatter.12.cloned.1.call-start
  8.7 0.8 copy.18
  9.5 1.3 constant_dynamic-slice_fusion.1
  10.8 0.7 copy.23
  11.5 0.7 copy.24
  12.2 8.7 %all_gather.9.vec_ref = f32[4,16,256]{2,1,0:T(8,128)} all-gather(f32[1,16,256]{2,1,0:T(8,128)} %param.9), channel_id=1, replica_groups=mesh['section'=4,'dp'=8] {'section'}, dimensions={0}, use_global_device_ids=true | all-gather | bytes 81920 | tf_op jit(solution)/shard_map/all_gather | solution.py:380
  21.0 22.1 %all-gather.3.cloned.1.call-done.win_ref = bf16[4,256,768]{2,1,0:T(8,128)(2,1)} async-done(((bf16[1,256,768]{2,1,0:T(8,128)(2,1)}), bf16[4,256,768]{2,1,0:T(8,128)(2,1)}) %all-gather.3.cloned.1.call-update) | async-done | bytes 1572880 | tf_op jit(solution)/shard_map/all_gather | solution.py:381
  43.1 32.8 %all-gather.5.cloned.1.call-done.wout_ref = bf16[4,768,256]{2,1,0:T(8,128)(2,1)} async-done(((bf16[1,768,256]{2,1,0:T(8,128)(2,1)}), bf16[4,768,256]{2,1,0:T(8,128)(2,1)}) %all-gather.5.cloned.1.call-update) | async-done | bytes 1572880 | tf_op jit(solution)/shard_map/all_gather | solution.py:382
  76.0 55.1 %two_layers.1 = (bf16[2,196,256]{2,1,0:T(8,128)(2,1)}, bf16[2,196,256]{2,1,0:T(8,128)(2,1)}, f32[4,16,256]{2,1,0:T(8,128)}, f32[4,256,768]{2,1,0:T(8,128)}, f32[4,768,256]{2,1,0:T(8,128)}) custom-call(bf16[2,196,256]{2,1,0:T(8,128)(2,1)} %bitcast.20, bf16[2,196,256]{2,1,0:T(8,128)(2,1)} %bitcast.19, s32[2,2,49,4]{3,2,1,0:T(8,128)} %bitcast.23, ...), custom_call_target="tpu_custom_call" | custom-call | tf_op jit(solution)/shard_map/two_layers/pallas_call | solution.py:336
  131.1 0.0 reduce-scatter.14.cloned.1.call-start
  131.1 0.5 reduce-scatter.14.cloned.1.call-update
  131.7 0.5 reduce-scatter.10.cloned.1.call-update
  132.3 42.9 %reduce-scatter.12.cloned.1.call-done = f32[1,256,768]{2,1,0:T(8,128)} async-done(((f32[4,256,768]{2,1,0:T(8,128)}), f32[1,256,768]{2,1,0:T(8,128)}) %reduce-scatter.12.cloned.1.call-update) | async-done | bytes 786448
  175.2 46.8 %reduce-scatter.14.cloned.1.call-done = f32[1,768,256]{2,1,0:T(8,128)} async-done(((f32[4,768,256]{2,1,0:T(8,128)}), f32[1,768,256]{2,1,0:T(8,128)}) %reduce-scatter.14.cloned.1.call-update) | async-done | bytes 786448
  222.0 0.8 copy.19
  222.9 0.8 copy.20
  223.7 24.1 %reduce-scatter.10.cloned.1.call-done = f32[1,16,256]{2,1,0:T(8,128)} async-done(((f32[4,16,256]{2,1,0:T(8,128)}), f32[1,16,256]{2,1,0:T(8,128)}) %reduce-scatter.10.cloned.1.call-update) | async-done | bytes 16400
  247.8 25.4 %psum.21 = f32[16,256]{1,0:T(8,128)S(1)} all-reduce(f32[16,256]{1,0:T(8,128)} %bitcast.26), channel_id=1, replica_groups=mesh['section'=4,'dp'=8] {'dp'}, use_global_device_ids=true, to_apply=%region_1.2 | all-reduce | flops 4096 | bytes 32768 | tf_op jit(solution)/shard_map/psum | solution.py:386
  273.2 0.6 multiply_bitcast_fusion.2
  273.8 37.4 %all-reduce.6.cloned.1.call-done = (f32[256,768]{1,0:T(8,128)}, f32[768,256]{1,0:T(8,128)}) async-done(((f32[256,768]{1,0:T(8,128)}, f32[768,256]{1,0:T(8,128)}), (f32[256,768]{1,0:T(8,128)}, f32[768,256]{1,0:T(8,128)})) %all-reduce.6.cloned.1.call-update) | async-done | bytes 1572880 | tf_op jit(solution)/shard_map/psum | solution.py:386
  311.2 2.1 multiply_bitcast_fusion.1
  313.2 2.1 multiply_bitcast_fusion
  (13 shorter events, 0.2 us)
Async XLA Ops:
  7.2 1.6 copy-start
  7.2 35.9 %all-gather.3.cloned.1.call-start = ((), (), s32[]{:S(2)}) async-start(), calls=%async_computation.3 | async-start | bytes 1966080 | tf_op jit(solution)/shard_map/all_gather | solution.py:381
  7.9 68.0 %all-gather.5.cloned.1.call-start = ((), (), s32[]{:S(2)}) async-start(), calls=%async_computation.4 | async-start | bytes 1966080 | tf_op jit(solution)/shard_map/all_gather | solution.py:382
  8.7 166.5 %reduce-scatter.12.cloned.1.call-start = ((), (), s32[]{:S(2)}) async-start(), calls=%async_computation.6 | async-start | bytes 3932160
  131.1 91.0 %copy-start.2 = (bf16[2,196,256]{2,1,0:T(8,128)(2,1)S(1)}, bf16[2,196,256]{2,1,0:T(8,128)(2,1)}, u32[]{:S(2)}) copy-start(bf16[2,196,256]{2,1,0:T(8,128)(2,1)} %get-tuple-element.10) | copy-start | bytes 602116
  131.1 91.8 %copy-start.1 = (bf16[2,196,256]{2,1,0:T(8,128)(2,1)S(1)}, bf16[2,196,256]{2,1,0:T(8,128)(2,1)}, u32[]{:S(2)}) copy-start(bf16[2,196,256]{2,1,0:T(8,128)(2,1)} %get-tuple-element.11) | copy-start | bytes 602116
  131.1 90.9 %reduce-scatter.14.cloned.1.call-start = ((), (), s32[]{:S(2)}) async-start(), calls=%async_computation.7 | async-start | bytes 3932160
  131.7 116.1 %reduce-scatter.10.cloned.1.call-start = ((), (), s32[]{:S(2)}) async-start(), calls=%async_computation.5 | async-start | bytes 81920
  132.2 178.9 %all-reduce.6.cloned.1.call-start = ((), (), s32[]{:S(2)}) async-start(), calls=%async_computation.8 | async-start | bytes 3145728 | tf_op jit(solution)/shard_map/psum | solution.py:386
Sparse Core Ops, SparseCore 0:
  9.9 33.2 all-gather.2
  44.9 30.9 all-gather.4
  131.2 43.9 reduce-scatter.11
  178.0 43.9 reduce-scatter.13
  224.6 23.1 reduce-scatter.9
  250.2 60.9 all-reduce.5

commit v2 on v1

--- a/solution.py
+++ b/solution.py
@@ -18,6 +18,7 @@
 VEC_ROWS = 16
 PATCHES = 196
 REGIONS = 49
+BLOCK = 256
 EPSILON = 1e-06
 
 PITCH = 16
@@ -88,10 +89,9 @@
     return one_hot((own == region) & (c < SIDE) & (r < SIDE))
 
 
-def compute_kernel(
-    n,
-    x_ref, cot_ref, routes_ref, vec_ref, win_ref, wout_ref,
-    fin_ref, gin_ref, gvec_ref, ga_ref, gb_ref,
+def layers(
+    n, before_section, after_grads, poll,
+    x_ref, cot_ref, routes_ref, vec_ref, win_ref, wout_ref, fin_ref, gin_ref, gvec_ref, grad_ref,
     hs, zh, inv, nm, pr, pt, at, act, gp, bias, mixed, g, dproj, cv, dom, qm, dsb, tmp, dqt, km, wide,
 ):
     eye = one_hot(iota((ROWS, ROWS), 0) == iota((ROWS, ROWS), 1))
@@ -216,7 +216,7 @@
             else:
                 dom[0:LIVE] = out.astype(BF)
                 dom[LIVE:ROWS] = jnp.zeros((ROWS - LIVE, D), BF)
-                fin_ref[i] = dot(gather(), dom[0:ROWS]).astype(BF)
+                fin_ref[0, i] = dot(gather(), dom[0:ROWS]).astype(BF)
             return carry
 
         lax.fori_loop(0, n, image, 0)
@@ -247,11 +247,15 @@
             d_normed = dot(dproj[rows], win_ref[s], 1, 1)
             out = grad.astype(F32) + norm_backward(s, rows, d_normed)
             wide[rows] = out.astype(BF)
-            return carry
-
-        lax.fori_loop(0, n, image, 0)
-        ga_ref[s] = dot(nm[s], dproj[...], 0, 0)
-        gb_ref[s] = dot(act[a], g[...], 0, 0)
+
+        for i in range(n):
+            image(i, 0)
+            poll()
+        for j in range(3):
+            lanes = slice(j * D, (j + 1) * D)
+            grad_ref[j] = dot(nm[s], dproj[:, lanes], 0, 0)
+            grad_ref[3 + j] = dot(act[a, :, lanes], g[...], 0, 0)
+        after_grads(s)
         for i in range(n):
             g[pl.ds(i * ROWS, LIVE)] = wide[pl.ds(i * ROWS, LIVE)]
 
@@ -285,6 +289,7 @@
                 return carry
 
             lax.fori_loop(0, HEADS, head, 0)
+            poll()
             dproj[rows, 0:D] = (transposed(dqt[...].astype(BF))[:LIVE] * SCALE).astype(BF)
             dproj[rows, D : 2 * D] = (dot(dsb[...], qm[...]) * SCALE).astype(BF)
             dproj[rows, 2 * D : 3 * D] = dot(pt[a, i], dom[...]).astype(BF)
@@ -307,90 +312,381 @@
                 wide[pl.ds(pl.multiple_of(i * ROWS + r * PITCH, PITCH), PITCH)] = total.astype(BF)
             for j in range(9):
                 gvec_ref[s, 6 + j : 7 + j] += col_sum(taps[j])
-            return carry
-
-        lax.fori_loop(0, n, image, 0)
-        ga_ref[s] = dot(nm[s], dproj[...], 0, 0)
-        gb_ref[s, 0:D] = dot(at[a], g[...], 0, 0)
-        gb_ref[s, D:HID] = jnp.zeros((HID - D, D), F32)
+
+        for i in range(n):
+            image(i, 0)
+            poll()
+        for j in range(3):
+            grad_ref[j] = dot(nm[s], dproj[:, j * D : (j + 1) * D], 0, 0)
+        grad_ref[3] = dot(at[a], g[...], 0, 0)
+        after_grads(s)
         for i in range(n):
             g[pl.ds(i * ROWS, LIVE)] = wide[pl.ds(i * ROWS, LIVE)]
 
     gvec_ref[...] = jnp.zeros_like(gvec_ref)
-    attention_forward(0)
-    dense_forward(1)
-    attention_forward(2)
-    dense_forward(3)
+    for s in range(SECTIONS):
+        before_section(s)
+        (attention_forward, dense_forward)[s % 2](s)
     dense_backward(3)
     attention_backward(2)
     dense_backward(1)
     attention_backward(0)
     for i in range(n):
-        gin_ref[i] = dot(gather(), g[pl.ds(i * ROWS, ROWS)]).astype(BF)
+        gin_ref[0, i] = dot(gather(), g[pl.ds(i * ROWS, ROWS)]).astype(BF)
+
+
+def layer_scratch(n):
+    total = n * ROWS
+    return [
+        pltpu.VMEM((SECTIONS, total, D), BF),
+        pltpu.VMEM((SECTIONS, total, D), F32),
+        pltpu.VMEM((SECTIONS, total, 1), F32),
+        pltpu.VMEM((SECTIONS, total, D), BF),
+        pltpu.VMEM((2, total, HID), BF),
+        pltpu.VMEM((2, n, LIVE, HEADS * ROWS), BF),
+        pltpu.VMEM((2, total, D), BF),
+        pltpu.VMEM((2, total, HID), BF),
+        pltpu.VMEM((2, total, HID), F32),
+        pltpu.VMEM((2, n, LIVE, ROWS), F32),
+        pltpu.VMEM((LIVE, D), F32),
+        pltpu.VMEM((total, D), BF),
+        pltpu.VMEM((total, HID), BF),
+        pltpu.VMEM((LIVE + 2 * HALO, D), F32),
+        pltpu.VMEM((HEADS * ROWS, D), BF),
+        pltpu.VMEM((HEADS * ROWS, D), BF),
+        pltpu.VMEM((LIVE, HEADS * ROWS), BF),
+        pltpu.VMEM((D, ROWS), BF),
+        pltpu.VMEM((D, ROWS), F32),
+        pltpu.VMEM((ROWS, D), BF),
+        pltpu.VMEM((total, D), BF),
+    ]
+
+
+def compute_kernel(n, *refs):
+    x_ref, cot_ref, routes_ref, vec_ref, win_ref, wout_ref, fin_ref, gin_ref, gvec_ref, ga_ref, gb_ref, grad_ref = refs[:12]
+
+    def after_grads(s):
+        for j in range(3):
+            ga_ref[s, :, j * D : (j + 1) * D] = grad_ref[j]
+            if s % 2 == 1 or j == 0:
+                gb_ref[s, j * D : (j + 1) * D] = grad_ref[3 + j]
+            else:
+                gb_ref[s, j * D : (j + 1) * D] = jnp.zeros((D, D), F32)
+
+    layers(
+        n, lambda s: None, after_grads, lambda: None,
+        x_ref, cot_ref, routes_ref, vec_ref, win_ref, wout_ref, fin_ref, gin_ref, gvec_ref, grad_ref, *refs[12:],
+    )
 
 
 def compute(x, cot, routes, vec, win, wout):
     n = x.shape[0]
-    total = n * ROWS
     vmem = pl.BlockSpec(memory_space=pltpu.VMEM)
     return pl.pallas_call(
         functools.partial(compute_kernel, n),
         out_shape=(
-            jax.ShapeDtypeStruct(x.shape, BF),
-            jax.ShapeDtypeStruct(x.shape, BF),
+            jax.ShapeDtypeStruct((1,) + x.shape, BF),
+            jax.ShapeDtypeStruct((1,) + x.shape, BF),
             jax.ShapeDtypeStruct((SECTIONS, VEC_ROWS, D), F32),
             jax.ShapeDtypeStruct((SECTIONS, D, HID), F32),
             jax.ShapeDtypeStruct((SECTIONS, HID, D), F32),
         ),
         in_specs=[vmem] * 6,
         out_specs=(vmem,) * 5,
+        scratch_shapes=[pltpu.VMEM((6, BLOCK, BLOCK), F32)] + layer_scratch(n),
+        compiler_params=pltpu.CompilerParams(vmem_limit_bytes=56 * 1024 * 1024),
+        name="layers_alone",
+    )(x, cot, routes, vec, win, wout)
+
+
+MESH = pl.DeviceIdType.MESH
+HALF = BLOCK // 2
+PART = HALF // SECTIONS
+
+
+def blocks_of(t):
+    return 6 if t % 2 == 1 else 4
+
+
+def whole_kernel(
+    n, dp, images,
+    inputs_ref, cot_in_ref, routes_in_ref, vec_own, win_own, wout_own,
+    fin_ref, gin_ref, gvec_ref, ga_ref, gb_ref,
+    x_ref, cot_ref, routes_ref, vec_ref, win_ref, wout_ref, gvec_part, grad_ref,
+    own_half, send_half, got_half, half_sum, got_part, part_sum, got_dp, result, vec_got, vec_sum, vec_dp,
+    in_sem, w_send, w_recv, f_send, f_recv, v_send, v_recv, h_send, h_recv, p_send, p_recv, d_send, d_recv, r_send, r_recv,
+    gv_send, gv_recv, gd_send, gd_recv,
+    *scratch,
+):
+    me, j = lax.axis_index("section"), lax.axis_index("dp")
+    core = lax.rem(j, 2)
+    steps = (dp // 2).bit_length() - 1
+    peers = [(lax.bitwise_xor(me, k), j) for k in range(1, SECTIONS)]
+    crossed = [(lax.bitwise_xor(me, k), lax.bitwise_xor(j, 1)) for k in range(1, SECTIONS)]
+    mate = (me, lax.bitwise_xor(j, 1))
+    along = [(me, lax.bitwise_xor(j, 2 << b)) for b in range(steps)]
+    waiting = []
+
+    def remote(src, dst, send, recv, device):
+        return pltpu.make_async_remote_copy(src, dst, send, recv, device_id=device, device_id_type=MESH)
+
+    def go(copy, when=None):
+        if when is None:
+            copy.start()
+        else:
+            pl.when(when)(lambda: copy.start())
+        waiting.append((copy, when))
+
+    loads = [
+        pltpu.make_async_copy(inputs_ref.at[me], x_ref, in_sem.at[0]),
+        pltpu.make_async_copy(cot_in_ref.at[me], cot_ref, in_sem.at[1]),
+        pltpu.make_async_copy(routes_in_ref.at[0, me], routes_ref.at[0], in_sem.at[2]),
+        pltpu.make_async_copy(routes_in_ref.at[1, me], routes_ref.at[1], in_sem.at[3]),
+    ]
+    for copy in loads:
+        copy.start()
+
+    barrier = pltpu.get_barrier_semaphore()
+    everyone = peers + crossed + [mate] + along
+    for device in everyone:
+        pl.semaphore_signal(barrier, inc=1, device_id=device, device_id_type=MESH)
+    pl.semaphore_wait(barrier, len(everyone))
+
+    own_rows = pl.ds(pl.multiple_of(core * HALF, HALF), HALF)
+    tail_rows = pl.ds(pl.multiple_of(D + core * D, D), D)
+    pieces = [(win_own, win_ref, own_rows), (wout_own, wout_ref, own_rows), (wout_own, wout_ref, tail_rows)]
+
+    def has(piece, t):
+        return piece < 2 or t % 2 == 1
+
+    odd = lax.rem(me, 2) == 1
+    for k, device in enumerate(peers):
+        go(remote(vec_own.at[0], vec_ref.at[me], v_send.at[k], v_recv.at[k], device))
+    for p, (source, target, rows) in enumerate(pieces):
+        for k, device in enumerate(peers):
+            go(remote(source.at[0, rows], target.at[me, rows], w_send.at[p, k], w_recv.at[p, me], device), None if p < 2 else odd)
+    vec_ref[me] = vec_own[0]
+    win_ref[me] = win_own[0]
+    wout_ref[me] = wout_own[0]
+    for copy in loads:
+        copy.wait()
+    for k, device in enumerate(peers):
+        remote(vec_own.at[0], vec_ref.at[me], v_send.at[k], v_recv.at[k], device).wait_recv()
+
+    def forward_weights(t):
+        for p, (source, target, rows) in enumerate(pieces):
+            if has(p, t):
+                spot = target.at[t, rows]
+
+                @pl.when(me != t)
+                def _():
+                    remote(spot, spot, w_send.at[p, 0], w_recv.at[p, t], mate).wait_recv()
+
+                go(remote(spot, spot, f_send.at[p, t], f_recv.at[p, t], mate), me != t)
+
+    def before_section(t):
+        if t == 0:
+            forward_weights(0)
+        for p, (source, target, rows) in enumerate(pieces):
+            if has(p, t):
+                spot = target.at[t, rows]
+
+                @pl.when(me != t)
+                def _():
+                    remote(spot, spot, f_send.at[p, t], f_recv.at[p, t], mate).wait_recv()
+
+        if t + 1 < SECTIONS:
+            forward_weights(t + 1)
+
+    other_rows = pl.ds(pl.multiple_of((1 - core) * HALF, HALF), HALF)
+    todo = []
+
+    def poll():
+        if todo:
+            todo.pop(0)()
+
+    def after_grads(t):
+        count = blocks_of(t)
+        blocks = pl.ds(0, count)
+        for b in range(count):
+            send_half[t, b] = grad_ref[b, other_rows].astype(BF)
+        halves = remote(send_half.at[t, blocks], got_half.at[t, blocks], h_send.at[t], h_recv.at[t], mate)
+        go(halves)
+        for b in range(count):
+            own_half[t, b] = grad_ref[b, own_rows].astype(BF)
+
+        def quarter(k):
+            return pl.ds(pl.multiple_of(k * PART, PART), PART)
+
+        parts = [
+            remote(
+                half_sum.at[t, blocks, quarter(device[0])], got_part.at[t, k, blocks], p_send.at[t, k], p_recv.at[t, k], device
+            )
+            for k, device in enumerate(peers)
+        ]
+
+        def add_halves():
+            halves.wait_recv()
+            for b in range(count):
+                half_sum[t, b] = (own_half[t, b].astype(F32) + got_half[t, b].astype(F32)).astype(BF)
+            for copy in parts:
+                go(copy)
+
+        doubling = [
+            remote(part_sum.at[t, b, blocks], got_dp.at[t, b, blocks], d_send.at[t, b], d_recv.at[t, b], along[b])
+            for b in range(steps)
+        ]
+
+        def deliver():
+            spot = result.at[blocks, core, quarter(me)]
+            last = part_sum.at[t, steps, blocks]
+            for k, device in enumerate(peers + crossed):
+                go(remote(last, spot, r_send.at[t, k], r_recv.at[core, me], device), device[0] == t)
+            go(remote(last, spot, r_send.at[t, 6], r_recv.at[core, me], mate), me == t)
+
+            @pl.when(me == t)
+            def _():
+                for b in range(count):
+                    result[b, core, quarter(me)] = part_sum[t, steps, b]
+
+        def add_parts():
+            for copy in parts:
+                copy.wait_recv()
+            for b in range(count):
+                total = half_sum[t, b, quarter(me)].astype(F32)
+                for k in range(SECTIONS - 1):
+                    total = total + got_part[t, k, b].astype(F32)
+                part_sum[t, 0, b] = total.astype(BF)
+            if steps > 0:
+                go(doubling[0])
+            else:
+                deliver()
+
+        def add_dp(step):
+            def run():
+                doubling[step].wait_recv()
+                for b in range(count):
+                    total = part_sum[t, step, b].astype(F32) + got_dp[t, step, b].astype(F32)
+                    part_sum[t, step + 1, b] = total.astype(BF)
+                if step + 1 < steps:
+                    go(doubling[step + 1])
+                else:
+                    deliver()
+
+            return run
+
+        todo.append(add_halves)
+        todo.append(add_parts)
+        for step in range(steps):
+            todo.append(add_dp(step))
+
+    layers(
+        n, before_section, after_grads, poll,
+        x_ref, cot_ref, routes_ref, vec_ref, win_ref, wout_ref, fin_ref, gin_ref, gvec_part, grad_ref, *scratch,
+    )
+
+    copies = [
+        remote(gvec_part.at[device[0]], vec_got.at[k], gv_send.at[k], gv_recv.at[k], device) for k, device in enumerate(peers)
+    ]
+    for copy in copies:
+        go(copy)
+    poll()
+    for copy in copies:
+        copy.wait_recv()
+    vec_sum[0] = gvec_part[me] + vec_got[0] + vec_got[1] + vec_got[2]
+    for b in range(steps + 1):
+        copy = remote(vec_sum.at[b], vec_dp.at[b], gd_send.at[b], gd_recv.at[b], (me, lax.bitwise_xor(j, 1 << b)))
+        go(copy)
+        poll()
+        copy.wait_recv()
+        vec_sum[b + 1] = vec_sum[b] + vec_dp[b]
+    while todo:
+        poll()
+    gvec_ref[0] = vec_sum[steps + 1] * (1.0 / images)
+
+    for c in range(2):
+        for k in range(SECTIONS):
+            for parity in range(2):
+                blocks = pl.ds(0, blocks_of(parity))
+                spot = result.at[blocks, c, pl.ds(k * PART, PART)]
+
+                @pl.when(((me != k) | (core != c)) & (lax.rem(me, 2) == parity))
+                def _():
+                    remote(spot, spot, r_send.at[0, 0], r_recv.at[c, k], mate).wait_recv()
+
+    for b in range(3):
+        for c in range(2):
+            rows = slice(c * HALF, (c + 1) * HALF)
+            ga_ref[0, rows, b * D : (b + 1) * D] = result[b, c].astype(F32) * (1.0 / images)
+            gb_ref[0, b * D + c * HALF : b * D + (c + 1) * HALF] = result[3 + b, c].astype(F32) * (1.0 / images)
+
+    @pl.when(lax.rem(me, 2) == 0)
+    def _():
+        gb_ref[0, D:HID] = jnp.zeros((HID - D, D), F32)
+
+    for copy, when in waiting:
+        if when is None:
+            copy.wait_send()
+        else:
+            pl.when(when)(lambda copy=copy: copy.wait_send())
+
+
+def per_device(inputs, cotangent, routes, vectors, in_weight, out_weight):
+    n = inputs.shape[1]
+    dp = lax.axis_size("dp")
+    steps = (dp // 2).bit_length() - 1
+    images = inputs.shape[0] * n * dp
+    vmem = pl.BlockSpec(memory_space=pltpu.VMEM)
+    hbm = pl.BlockSpec(memory_space=pl.ANY)
+    dma = pltpu.SemaphoreType.DMA
+    return pl.pallas_call(
+        functools.partial(whole_kernel, n, dp, images),
+        out_shape=(
+            jax.ShapeDtypeStruct((1,) + inputs.shape[1:], BF),
+            jax.ShapeDtypeStruct((1,) + inputs.shape[1:], BF),
+            jax.ShapeDtypeStruct((1, VEC_ROWS, D), F32),
+            jax.ShapeDtypeStruct((1, D, HID), F32),
+            jax.ShapeDtypeStruct((1, HID, D), F32),
+        ),
+        in_specs=[hbm] * 3 + [vmem] * 3,
+        out_specs=(vmem,) * 5,
         scratch_shapes=[
-            pltpu.VMEM((SECTIONS, total, D), BF),
-            pltpu.VMEM((SECTIONS, total, D), F32),
-            pltpu.VMEM((SECTIONS, total, 1), F32),
-            pltpu.VMEM((SECTIONS, total, D), BF),
-            pltpu.VMEM((2, total, HID), BF),
-            pltpu.VMEM((2, n, LIVE, HEADS * ROWS), BF),
-            pltpu.VMEM((2, total, D), BF),
-            pltpu.VMEM((2, total, HID), BF),
-            pltpu.VMEM((2, total, HID), F32),
-            pltpu.VMEM((2, n, LIVE, ROWS), F32),
-            pltpu.VMEM((LIVE, D), F32),
-            pltpu.VMEM((total, D), BF),
-            pltpu.VMEM((total, HID), BF),
-            pltpu.VMEM((LIVE + 2 * HALO, D), F32),
-            pltpu.VMEM((HEADS * ROWS, D), BF),
-            pltpu.VMEM((HEADS * ROWS, D), BF),
-            pltpu.VMEM((LIVE, HEADS * ROWS), BF),
-            pltpu.VMEM((D, ROWS), BF),
-            pltpu.VMEM((D, ROWS), F32),
-            pltpu.VMEM((ROWS, D), BF),
-            pltpu.VMEM((total, D), BF),
-        ],
-        compiler_params=pltpu.CompilerParams(vmem_limit_bytes=56 * 1024 * 1024),
+            pltpu.VMEM(inputs.shape[1:], BF),
+            pltpu.VMEM(inputs.shape[1:], BF),
+            pltpu.VMEM((2,) + routes.shape[2:], jnp.int32),
+            pltpu.VMEM((SECTIONS, VEC_ROWS, D), F32),
+            pltpu.VMEM((SECTIONS, D, HID), BF),
+            pltpu.VMEM((SECTIONS, HID, D), BF),
+            pltpu.VMEM((SECTIONS, VEC_ROWS, D), F32),
+            pltpu.VMEM((6, BLOCK, BLOCK), F32),
+            pltpu.VMEM((SECTIONS, 6, HALF, BLOCK), BF),
+            pltpu.VMEM((SECTIONS, 6, HALF, BLOCK), BF),
+            pltpu.VMEM((SECTIONS, 6, HALF, BLOCK), BF),
+            pltpu.VMEM((SECTIONS, 6, HALF, BLOCK), BF),
+            pltpu.VMEM((SECTIONS, 3, 6, PART, BLOCK), BF),
+            pltpu.VMEM((SECTIONS, steps + 1, 6, PART, BLOCK), BF),
+            pltpu.VMEM((SECTIONS, max(steps, 1), 6, PART, BLOCK), BF),
+            pltpu.VMEM((6, 2, HALF, BLOCK), BF),
+            pltpu.VMEM((3, VEC_ROWS, D), F32),
+            pltpu.VMEM((steps + 2, VEC_ROWS, D), F32),
+            pltpu.VMEM((steps + 1, VEC_ROWS, D), F32),
+            dma((4,)),
+            dma((3, 3)), dma((3, SECTIONS)),
+            dma((3, SECTIONS)), dma((3, SECTIONS)),
+            dma((3,)), dma((3,)),
+            dma((SECTIONS,)), dma((SECTIONS,)),
+            dma((SECTIONS, 3)), dma((SECTIONS, 3)),
+            dma((SECTIONS, max(steps, 1))), dma((SECTIONS, max(steps, 1))),
+            dma((SECTIONS, 7)), dma((2, SECTIONS)),
+            dma((3,)), dma((3,)),
+            dma((steps + 1,)), dma((steps + 1,)),
+        ]
+        + layer_scratch(n),
+        compiler_params=pltpu.CompilerParams(
+            vmem_limit_bytes=60 * 1024 * 1024, collective_id=0, has_side_effects=True
+        ),
         name="two_layers",
-    )(x, cot, routes, vec, win, wout)
-
-
-def per_device(inputs, cotangent, routes, vectors, in_weight, out_weight):
-    section = lax.axis_index("section")
-    x = lax.dynamic_index_in_dim(inputs, section, 0, keepdims=False)
-    cot = lax.dynamic_index_in_dim(cotangent, section, 0, keepdims=False)
-    picks = lax.dynamic_index_in_dim(routes, section, 1, keepdims=False)
-    vec = lax.all_gather(vectors[0], "section")
-    win = lax.all_gather(in_weight[0], "section")
-    wout = lax.all_gather(out_weight[0], "section")
-    fin, gin, gvec, ga, gb = compute(x, cot, picks, vec, win, wout)
-    images = inputs.shape[0] * inputs.shape[1] * lax.axis_size("dp")
-    gvec, ga, gb = (lax.psum_scatter(v, "section") for v in (gvec, ga, gb))
-    gvec, ga, gb = lax.psum((gvec, ga, gb), "dp")
-    return (
-        fin[None],
-        gin[None],
-        (gvec / images)[None],
-        (ga / images)[None],
-        (gb / images)[None],
-    )
+    )(inputs, cotangent, routes, vectors, in_weight, out_weight)
 
 
 def solution(mesh):

time: 325 us -> 139 us (0.43)
  waiting for transfers between devices: 209 us -> 0 us
  Pallas kernels: 55.1 us -> 126 us
  blocking collectives: 34.1 us -> 0 us
  between operations: 14.2 us -> 0.65 us
  local copies, waits for them, and re-layouts: 5.17 us -> 11.5 us
  other arithmetic: 4.73 us -> 0 us
    unnamed x9 -> x0, waiting for transfers between devices: 116 us -> none
    pallas_call x1, Pallas kernels: 55.1 us -> 126 us  [per_device(): pl.pallas_call(functools.partial(whole_kernel, n, dp, images), out_shape=...]
    all_gather x2 -> x0, waiting for transfers between devices: 55 us -> none  [the longest x1 32.8 us: per_device(): wout = lax.all_gather(out_weight[0], 'section')]
    psum x1 -> x0, waiting for transfers between devices: 37.4 us -> none  [per_device(): gvec, ga, gb = lax.psum((gvec, ga, gb), 'dp')]
    psum x1 -> x0, blocking collectives: 25.4 us -> none  [per_device(): gvec, ga, gb = lax.psum((gvec, ga, gb), 'dp')]
    all_gather x1 -> x0, blocking collectives: 8.74 us -> none  [per_device(): vec = lax.all_gather(vectors[0], 'section')]
    unnamed x8 -> x14, local copies, waits for them, and re-layouts: 1.68 us -> 7.93 us
    broadcast_in_dim x3 -> x0, other arithmetic: 4.73 us -> none  [the longest x1 2.06 us: per_device(): (ga / images)[None]]
  transfers between devices with their start and end apart: 6 -> 0, of which waited for: 6 -> 0; matrix products, arithmetic and copies ran while one was open for 2% -> 0% of each run, Pallas kernels for 0% -> 0%
where the time goes in v2:
time: 139 us
  Pallas kernels  126 us (91%)
  local copies, waits for them, and re-layouts  11.5 us (8%)
    pallas_call x1, Pallas kernels, per_device(): pl.pallas_call(functools.partial(whole_kernel, n, dp, images), out_shape=...  126 us
    unnamed x14, local copies, waits for them, and re-layouts  7.93 us
    pallas_call x2, local copies, waits for them, and re-layouts, per_device(): pl.pallas_call(functools.partial(whole_kernel, n, dp, images), out_shape=...  3.61 us

profile of v2, /device:TPU:1, one launch (start us, length us, event | category | flops | bytes accessed | tf_op | source)
XLA Modules:
  0.0 138.7 jit_solution(13440626648887468690)
XLA Ops:
  0.6 1.8 %copy.13.routes_in_ref = s32[2,4,2,49,4]{4,3,2,1,0:T(8,128)} copy(s32[2,4,2,49,4]{3,4,2,1,0:T(4,128)} %param.8) | data formatting | bytes 25088 | tf_op args[2]
  2.4 0.0 copy-start
  2.4 2.2 %copy.11.inputs_ref = bf16[4,2,196,256]{3,2,1,0:T(8,128)(2,1)} copy(bf16[4,2,196,256]{3,1,2,0:T(2,128)(2,1)} %param.6) | data formatting | bytes 1605632 | tf_op args[0]
  4.6 0.0 copy-done
  4.6 1.0 copy.12.cot_in_ref
  5.7 126.5 %two_layers.1 = (bf16[1,2,196,256]{3,2,1,0:T(8,128)(2,1)}, bf16[1,2,196,256]{3,2,1,0:T(8,128)(2,1)}, f32[1,16,256]{2,1,0:T(8,128)}, f32[1,256,768]{2,1,0:T(8,128)}, f32[1,768,256]{2,1,0:T(8,128)}) custom-call(bf16[4,2,196,256]{3,2,1,0:T(8,128)(2,1)} %copy.11.inputs_ref, bf16[4,2,196,256]{3,2,1,0:T(8,128)(2,1)} %copy.12.cot_in_ref, ...), custom_call_target="tpu_custom_call" | custom-call | tf_op jit(solution)/shard_map/two_layers/pallas_call | solution.py:642
  132.1 0.0 copy-start.2
  132.2 1.8 %copy.14 = bf16[1,2,196,256]{3,1,2,0:T(2,128)(2,1)} copy(bf16[1,2,196,256]{3,2,1,0:T(8,128)(2,1)} %get-tuple-element.5) | data formatting | bytes 401408 | tf_op jit(solution)/shard_map/two_layers/pallas_call | solution.py:642
  134.0 0.0 copy-start.3
  134.0 1.8 %copy.15 = bf16[1,2,196,256]{3,1,2,0:T(2,128)(2,1)} copy(bf16[1,2,196,256]{3,2,1,0:T(8,128)(2,1)} %get-tuple-element.6) | data formatting | bytes 401408 | tf_op jit(solution)/shard_map/two_layers/pallas_call | solution.py:642
  135.8 0.0 copy-done.3
  135.8 0.6 copy.19
  136.4 0.0 copy-done.2
  136.4 0.0 copy-start.1
  136.4 0.9 copy.20
  137.3 0.5 copy-done.1
  137.8 0.9 copy.21
Async XLA Ops:
  2.4 2.2 %copy-start = (bf16[4,2,196,256]{3,1,2,0:T(2,128)(2,1)S(1)}, bf16[4,2,196,256]{3,1,2,0:T(2,128)(2,1)}, u32[]{:S(2)}) copy-start(bf16[4,2,196,256]{3,1,2,0:T(2,128)(2,1)} %param.7) | copy-start | bytes 2408452
  132.1 4.2 %copy-start.2 = (f32[1,256,768]{2,1,0:T(8,128)S(1)}, f32[1,256,768]{2,1,0:T(8,128)}, u32[]{:S(2)}) copy-start(f32[1,256,768]{2,1,0:T(8,128)} %get-tuple-element.18) | copy-start | bytes 2359300
  134.0 1.8 %copy-start.3 = (f32[1,16,256]{2,1,0:T(8,128)S(1)}, f32[1,16,256]{2,1,0:T(8,128)}, u32[]{:S(2)}) copy-start(f32[1,16,256]{2,1,0:T(8,128)} %get-tuple-element.17) | copy-start | bytes 49156
  136.4 1.4 %copy-start.1 = (f32[1,768,256]{2,1,0:T(8,128)S(1)}, f32[1,768,256]{2,1,0:T(8,128)}, u32[]{:S(2)}) copy-start(f32[1,768,256]{2,1,0:T(8,128)} %get-tuple-element.19) | copy-start | bytes 2359300

commit v3 on v2

v3 whole, which is shorter than its diff:
```python
import functools

import jax
import jax.numpy as jnp
from jax import lax
from jax.experimental import pallas as pl
from jax.experimental.pallas import tpu as pltpu
from jax.sharding import PartitionSpec as P

D = 256
HEADS = 8
HEAD_DIM = 32
HID = 768
SIDE = 14
WIN = 7
TOPK = 4
SECTIONS = 4
VEC_ROWS = 16
PATCHES = 196
REGIONS = 49
BLOCK = 256
EPSILON = 1e-06

PITCH = 16
LIVE = SIDE * PITCH
ROWS = 256
HALO = 24
CHUNK = 32
LANES = 128
NEGATIVE = -1e30
LOG2E = 1.4426950408889634
SCALE = HEAD_DIM ** (-0.5)

BF = jnp.bfloat16
F32 = jnp.float32


def dot(a, b, ca=1, cb=0):
    return lax.dot_general(
        a, b, (((ca,), (cb,)), ((), ())), preferred_element_type=jnp.float32
    )


def iota(shape, dim):
    return lax.broadcasted_iota(jnp.int32, shape, dim)


def one_hot(cond):
    return jnp.where(cond, 1.0, 0.0).astype(BF)


def rows_of(i, count=LIVE):
    return pl.ds(pl.multiple_of(i * ROWS, ROWS), count)


def col_sum(x):
    return jnp.sum(x, axis=0, keepdims=True)


def ln_stats(x):
    average = jnp.mean(x, axis=-1, keepdims=True)
    centred = x - average
    spread = jnp.mean(centred * centred, axis=-1, keepdims=True)
    inverse = lax.rsqrt(spread + EPSILON)
    return centred * inverse, inverse


def gelu_pair(x):
    a = jnp.abs(x)
    t = 1.0 / (1.0 + a * (0.3275911 * 0.7071067811865476))
    e = jnp.exp2(x * x * (-0.5 * LOG2E))
    w = t * (0.5 * 1.061405429) + (0.5 * -1.453152027)
    w = w * t + (0.5 * 1.421413741)
    w = w * t + (0.5 * -0.284496736)
    w = w * t + (0.5 * 0.254829592)
    w = w * t * e
    phi = jnp.where(x >= 0, 1.0 - w, w)
    return x * phi, phi + x * e * 0.3989422804014327


def region_one_hot(shape, token_dim):
    token = iota(shape, token_dim)
    region = iota(shape, 1 - token_dim)
    r, c = token >> 4, token & (PITCH - 1)
    own = (r >> 1) * WIN + (c >> 1)
    return one_hot((own == region) & (c < SIDE) & (r < SIDE))


def layers(
    n, at_point,
    x_ref, cot_ref, routes_ref, vec_ref, win_ref, wout_ref, fin_ref, gin_ref, gvec_ref, grad_ref,
    hs, zh, inv, nm, pr, pt, at, act, gp, bias, mixed, g, dproj, cv, cvl, cvr, dom, qm, dsb, tmp, dqt, km, wide,
):
    pairs = PATCHES * n

    def eye():
        return one_hot(iota((ROWS, ROWS), 0) == iota((ROWS, ROWS), 1))

    def transposed(x):
        return dot(eye(), x, 1, 1)

    def spread(i):
        t, p = iota((ROWS, pairs), 0), iota((ROWS, pairs), 1)
        r, c = t >> 4, t & (PITCH - 1)
        return one_hot((p == (r * SIDE + c) * n + i) & (c < SIDE) & (r < SIDE))

    def gather():
        p, t = iota((pairs, n * ROWS), 0), iota((pairs, n * ROWS), 1)
        r, c, i = (t & (ROWS - 1)) >> 4, t & (PITCH - 1), t >> 8
        return one_hot((p == (r * SIDE + c) * n + i) & (c < SIDE) & (r < SIDE))

    def chunks():
        return [slice(c, c + CHUNK) for c in range(0, LIVE, CHUNK)]

    def rows_at(i, c, count):
        return pl.ds(pl.multiple_of(i * ROWS + c, PITCH), count)

    def tail(i):
        return pl.ds(i * ROWS + LIVE, ROWS - LIVE)

    none = jnp.zeros((ROWS - LIVE, D), BF)
    none_wide = jnp.zeros((ROWS - LIVE, HID), BF)
    halo = jnp.zeros((HALO, D), F32)
    for buffer in (cv, cvl, cvr):
        buffer[0:HALO] = halo
        buffer[HALO + LIVE : HALO + LIVE + HALO] = halo
    for i in range(n):
        for s in range(SECTIONS):
            nm[s, tail(i)] = none
            hs[s, tail(i)] = none
        for a in range(2):
            pr[a, tail(i)] = none_wide
            act[a, tail(i)] = none_wide
            at[a, tail(i)] = none
        wide[tail(i)] = none
        dproj[tail(i)] = none_wide
    gvec_ref[...] = jnp.zeros_like(gvec_ref)

    at_point("inputs", 0)
    x_pairs = x_ref[...].reshape(pairs, D)
    cot_pairs = cot_ref[...].reshape(pairs, D)
    for i in range(n):
        spread_i = spread(i)
        hs[0, pl.ds(i * ROWS, ROWS)] = dot(spread_i, x_pairs).astype(BF)
        g[pl.ds(i * ROWS, ROWS)] = dot(spread_i, cot_pairs).astype(BF)

    def conv_load(r0, count, x):
        cv[pl.ds(HALO + r0, count)] = x

    def conv_shift():
        for rows in chunks():
            cvl[HALO + rows.start : HALO + rows.stop] = cv[HALO + rows.start - 1 : HALO + rows.stop - 1]
            cvr[HALO + rows.start : HALO + rows.stop] = cv[HALO + rows.start + 1 : HALO + rows.stop + 1]

    def conv_at(r, u, v):
        start = HALO + (r + u) * PITCH
        return (cvl, cv, cvr)[v + 1][start : start + PITCH]

    def attention_start(s):
        vec = vec_ref.at[s]

        def image(i, carry):
            for rows in chunks():
                conv_load(rows.start, CHUNK, hs[s, rows_at(i, rows.start, CHUNK)].astype(F32))
            conv_shift()
            for r in range(SIDE):
                total = conv_at(r, 0, 0) + vec[15:16]
                for u in (-1, 0, 1):
                    for v in (-1, 0, 1):
                        j = 6 + 3 * (u + 1) + v + 1
                        total = total + conv_at(r, u, v) * vec[j : j + 1]
                here = rows_at(i, r * PITCH, PITCH)
                mixed[here] = total
                hat, inverse = ln_stats(total)
                zh[s, here] = hat
                inv[s, here] = inverse
                nm[s, here] = (hat * vec[0:1] + vec[1:2]).astype(BF)
            return carry

        lax.fori_loop(0, n, image, 0)

    def route_bias():
        key_region = region_one_hot((LIVE, REGIONS), 0)
        query_region = region_one_hot((REGIONS, ROWS), 1)
        for i in range(n):
            for a in range(2):
                picks = routes_ref[a, i]
                region = iota((REGIONS, REGIONS), 0)
                routed = jnp.zeros((REGIONS, REGIONS), F32)
                for k in range(TOPK):
                    routed = routed + jnp.where(picks[k : k + 1] == region, 1.0, 0.0)
                by_region = dot(key_region, routed.astype(BF)).astype(BF)
                bias[a, i] = (1.0 - dot(by_region, query_region)) * NEGATIVE

    def half_of(h):
        return slice((h // 4) * LANES, (h // 4 + 1) * LANES)

    def own_lanes(h, count):
        return (iota((count, LANES), 1) >> 5) == h % 4

    def attention_forward(s):
        a = s // 2
        vec = vec_ref.at[s]

        def image(i, carry):
            rows = rows_of(i)
            whole = rows_of(i, ROWS)
            pr[a, rows] = dot(nm[s, rows], win_ref[s]).astype(BF)
            tmp[...] = transposed(pr[a, whole, 2 * D : 3 * D]).astype(BF)
            for h in range(HEADS):
                lanes = half_of(h)
                keys = jnp.where(own_lanes(h, LIVE), pr[a, rows, slice(D + lanes.start, D + lanes.stop)], jnp.zeros((), BF))
                scores = dot(keys, pr[a, whole, lanes], 1, 1) * (SCALE * LOG2E) + bias[a, i]
                expo = jnp.exp2(scores - jnp.max(scores, axis=0, keepdims=True))
                pt[a, i, :, h * ROWS : (h + 1) * ROWS] = (expo * (1.0 / col_sum(expo))).astype(BF)
            for h in range(HEADS):
                own = slice(h * HEAD_DIM, (h + 1) * HEAD_DIM)
                dqt[own] = dot(tmp[own, 0:LIVE], pt[a, i, :, h * ROWS : (h + 1) * ROWS])
            attended = transposed(dqt[...].astype(BF)).astype(BF)
            at[a, whole] = attended
            out = mixed[rows] + dot(attended[:LIVE], wout_ref[s, 0:D]) + vec[2:3]
            hs[s + 1, rows] = out.astype(BF)
            pl.when(i == 0)(lambda: at_point("next", s))
            return carry

        lax.fori_loop(0, n, image, 0)

    def dense_forward(s):
        a = s // 2
        vec = vec_ref.at[s]
        token = iota((CHUNK, D), 0)

        def image(i, carry):
            rows = rows_of(i)
            for part in chunks():
                here = rows_at(i, part.start, CHUNK)
                hat, inverse = ln_stats(hs[s, here].astype(F32))
                zh[s, here] = hat
                inv[s, here] = inverse
                nm[s, here] = (hat * vec[0:1] + vec[1:2]).astype(BF)
            for j in range(3):
                lanes = slice(j * D, (j + 1) * D)
                hidden = dot(nm[s, rows], win_ref[s, :, lanes]) + vec[3 + j : 4 + j]
                value, slope = gelu_pair(hidden)
                act[a, rows, lanes] = value.astype(BF)
                gp[a, rows, lanes] = slope
            out = hs[s, rows].astype(F32) + dot(act[a, rows], wout_ref[s]) + vec[2:3]
            if s + 1 < SECTIONS:
                live = (iota((LIVE, D), 0) & (PITCH - 1)) < SIDE
                hs[s + 1, rows] = jnp.where(live, out, 0.0).astype(BF)
            else:
                wide[rows] = out.astype(BF)
            pl.when(i == 0)(lambda: at_point("next", s))
            return carry

        lax.fori_loop(0, n, image, 0)

    def norm_backward(s, here, d_normed, sums):
        vec = vec_ref.at[s]
        hat = zh[s, here]
        product = d_normed * hat
        scaled = d_normed * vec[0:1]
        first = jnp.mean(scaled, axis=-1, keepdims=True)
        second = jnp.mean(product * vec[0:1], axis=-1, keepdims=True)
        sums[0] = sums[0] + fold(product)
        sums[1] = sums[1] + fold(d_normed)
        return inv[s, here] * (scaled - first - hat * second)

    def fold(x):
        return jnp.sum(x.reshape(x.shape[0] // 8, 8, x.shape[1]), axis=0)

    def empty():
        return jnp.zeros((8, D), F32)

    def add_row(s, row, total):
        gvec_ref[s, row : row + 1] += col_sum(total)

    def dense_backward(s):
        a = s // 2
        for i in range(n):
            rows = rows_of(i)
            for j in range(3):
                lanes = slice(j * D, (j + 1) * D)
                d_active = dot(g[rows], wout_ref[s, lanes], 1, 1)
                d_hidden = (d_active * gp[a, rows, lanes]).astype(BF)
                dproj[rows, lanes] = d_hidden
                add_row(s, 3 + j, fold(d_hidden.astype(F32)))
        for j in range(3):
            lanes = slice(j * D, (j + 1) * D)
            grad_ref[j] = dot(nm[s], dproj[:, lanes], 0, 0)
            grad_ref[3 + j] = dot(act[a, :, lanes], g[...], 0, 0)
        at_point("grads", s)
        for i in range(n):
            rows = rows_of(i)
            d_normed = dot(dproj[rows], win_ref[s], 1, 1)
            sums = [empty(), empty(), empty()]
            for part in chunks():
                here = rows_at(i, part.start, CHUNK)
                grad = g[here].astype(F32)
                sums[2] = sums[2] + fold(grad)
                out = grad + norm_backward(s, here, d_normed[part], sums)
                g[here] = out.astype(BF)
            for row in range(3):
                add_row(s, row, sums[row])
            at_point("image", 2 * s + i)

    def attention_backward(s):
        a = s // 2
        vec = vec_ref.at[s]
        nothing = jnp.zeros((), BF)
        grad_ref[3] = dot(at[a], g[...], 0, 0)
        for i in range(n):
            rows = rows_of(i)
            whole = rows_of(i, ROWS)
            km[...] = dot(g[whole], wout_ref[s, 0:D], 1, 1).astype(BF)
            tmp[...] = transposed(pr[a, whole, D : 2 * D]).astype(BF)
            for h in range(HEADS):
                lanes = half_of(h)
                row = slice(h * ROWS, (h + 1) * ROWS)
                dom[row] = jnp.where(own_lanes(h, ROWS), km[:, lanes], nothing)
                qm[row] = jnp.where(own_lanes(h, ROWS), pr[a, whole, lanes], nothing)
            for h in range(HEADS):
                lanes = half_of(h)
                row = slice(h * ROWS, (h + 1) * ROWS)
                values = jnp.where(own_lanes(h, LIVE), pr[a, rows, slice(2 * D + lanes.start, 2 * D + lanes.stop)], nothing)
                d_weights = dot(values, km[:, lanes], 1, 1)
                weights = pt[a, i, :, row].astype(F32)
                dsb[:, row] = (weights * (d_weights - col_sum(weights * d_weights))).astype(BF)
                if h == 3:
                    at_point("half", 2 * s + i)
            for half in range(2):
                lanes = slice(2 * D + half * LANES, 2 * D + (half + 1) * LANES)
                four = slice(half * 4 * ROWS, (half + 1) * 4 * ROWS)
                dproj[rows, lanes] = dot(pt[a, i, :, four], dom[four]).astype(BF)
            for h in range(HEADS):
                own = slice(h * HEAD_DIM, (h + 1) * HEAD_DIM)
                dqt[own] = dot(tmp[own, 0:LIVE], dsb[:, h * ROWS : (h + 1) * ROWS])
            for half in range(2):
                lanes = slice(D + half * LANES, D + (half + 1) * LANES)
                four = slice(half * 4 * ROWS, (half + 1) * 4 * ROWS)
                dproj[rows, lanes] = (dot(dsb[:, four], qm[four]) * SCALE).astype(BF)
            dproj[rows, 0:D] = (transposed(dqt[...].astype(BF))[:LIVE] * SCALE).astype(BF)
            at_point("image", 2 * s + i)
        for j in range(3):
            grad_ref[j] = dot(nm[s], dproj[:, j * D : (j + 1) * D], 0, 0)
        at_point("grads", s)
        for i in range(n):
            rows = rows_of(i)
            d_normed = dot(dproj[rows], win_ref[s], 1, 1)
            sums = [empty(), empty(), empty(), empty()]
            for part in chunks():
                here = rows_at(i, part.start, CHUNK)
                grad = g[here].astype(F32)
                sums[2] = sums[2] + fold(grad)
                d_mixed = grad + norm_backward(s, here, d_normed[part], sums)
                sums[3] = sums[3] + fold(d_mixed)
                conv_load(part.start, CHUNK, d_mixed)
            for row, total in zip((0, 1, 2, 15), sums):
                add_row(s, row, total)
            at_point("norm", 2 * s + i)
            conv_shift()
            taps = [empty() for _ in range(9)]
            for r in range(SIDE):
                here = rows_at(i, r * PITCH, PITCH)
                start = hs[s, here].astype(F32)
                total = conv_at(r, 0, 0)
                for u in (-1, 0, 1):
                    for v in (-1, 0, 1):
                        j = 3 * (u + 1) + v + 1
                        moved = conv_at(r, -u, -v)
                        total = total + moved * vec[6 + j : 7 + j]
                        taps[j] = taps[j] + fold(moved * start)
                g[here] = jnp.where(iota((PITCH, D), 0) < SIDE, total, 0.0).astype(BF)
            for j in range(9):
                add_row(s, 6 + j, taps[j])
            at_point("conv", 2 * s + i)

    at_point("vectors", 0)
    attention_start(0)
    route_bias()
    at_point("prepared", 0)
    for s in range(SECTIONS):
        at_point("weights", s)
        if s == 2:
            attention_start(s)
        (attention_forward, dense_forward)[s % 2](s)
    fin_ref[0] = dot(gather(), wide[...]).astype(BF).reshape(PATCHES, n, D)
    for s in reversed(range(SECTIONS)):
        (attention_backward, dense_backward)[s % 2](s)
    gin_ref[0] = dot(gather(), g[...]).astype(BF).reshape(PATCHES, n, D)


def layer_scratch(n):
    total = n * ROWS
    return [
        pltpu.VMEM((SECTIONS, total, D), BF),
        pltpu.VMEM((SECTIONS, total, D), F32),
        pltpu.VMEM((SECTIONS, total, 1), F32),
        pltpu.VMEM((SECTIONS, total, D), BF),
        pltpu.VMEM((2, total, HID), BF),
        pltpu.VMEM((2, n, LIVE, HEADS * ROWS), BF),
        pltpu.VMEM((2, total, D), BF),
        pltpu.VMEM((2, total, HID), BF),
        pltpu.VMEM((2, total, HID), F32),
        pltpu.VMEM((2, n, LIVE, ROWS), F32),
        pltpu.VMEM((total, D), F32),
        pltpu.VMEM((total, D), BF),
        pltpu.VMEM((total, HID), BF),
        pltpu.VMEM((LIVE + 2 * HALO, D), F32),
        pltpu.VMEM((LIVE + 2 * HALO, D), F32),
        pltpu.VMEM((LIVE + 2 * HALO, D), F32),
        pltpu.VMEM((HEADS * ROWS, LANES), BF),
        pltpu.VMEM((HEADS * ROWS, LANES), BF),
        pltpu.VMEM((LIVE, HEADS * ROWS), BF),
        pltpu.VMEM((D, ROWS), BF),
        pltpu.VMEM((D, ROWS), F32),
        pltpu.VMEM((ROWS, D), BF),
        pltpu.VMEM((total, D), BF),
    ]


def compute_kernel(n, *refs):
    x_ref, cot_ref, routes_ref, vec_ref, win_ref, wout_ref, fin_ref, gin_ref, gvec_ref, ga_ref, gb_ref, grad_ref = refs[:12]

    def at_point(name, s):
        if name != "grads":
            return
        for j in range(3):
            ga_ref[s, :, j * D : (j + 1) * D] = grad_ref[j]
            if s % 2 == 1 or j == 0:
                gb_ref[s, j * D : (j + 1) * D] = grad_ref[3 + j]
            else:
                gb_ref[s, j * D : (j + 1) * D] = jnp.zeros((D, D), F32)

    layers(
        n, at_point,
        x_ref, cot_ref, routes_ref, vec_ref, win_ref, wout_ref, fin_ref, gin_ref, gvec_ref, grad_ref, *refs[12:],
    )


def compute(x, cot, routes, vec, win, wout):
    n = x.shape[0]
    vmem = pl.BlockSpec(memory_space=pltpu.VMEM)
    by_token = jax.ShapeDtypeStruct((1, PATCHES, n, D), BF)
    fin, gin, gvec, ga, gb = pl.pallas_call(
        functools.partial(compute_kernel, n),
        out_shape=(
            by_token,
            by_token,
            jax.ShapeDtypeStruct((SECTIONS, VEC_ROWS, D), F32),
            jax.ShapeDtypeStruct((SECTIONS, D, HID), F32),
            jax.ShapeDtypeStruct((SECTIONS, HID, D), F32),
        ),
        in_specs=[vmem] * 6,
        out_specs=(vmem,) * 5,
        scratch_shapes=[pltpu.VMEM((6, BLOCK, BLOCK), F32)] + layer_scratch(n),
        compiler_params=pltpu.CompilerParams(vmem_limit_bytes=56 * 1024 * 1024),
        name="layers_alone",
    )(jnp.transpose(x, (1, 0, 2)), jnp.transpose(cot, (1, 0, 2)), jnp.swapaxes(routes, 2, 3), vec, win, wout)
    return jnp.transpose(fin, (0, 2, 1, 3)), jnp.transpose(gin, (0, 2, 1, 3)), gvec, ga, gb


MESH = pl.DeviceIdType.MESH
HALF = BLOCK // 2
PART = HALF // SECTIONS


def blocks_of(t):
    return 6 if t % 2 == 1 else 4


def shares_of(dp):
    chips = dp // 2
    near = min(chips, 4)
    split = min(near, 2)
    return near, PART // split, BLOCK // (near // split), (chips // near).bit_length() - 1


def whole_kernel(
    n, dp, images,
    inputs_ref, cot_in_ref, routes_in_ref, vec_own, win_own, wout_own,
    fin_ref, gin_ref, gvec_ref, ga_ref, gb_ref,
    x_ref, cot_ref, routes_ref, vec_ref, win_ref, wout_ref, gvec_part, grad_ref,
    own_half, send_half, got_half, half_sum, got_part, part_sum, got_near, share, got_far, result, vec_got, vec_sum, vec_mate, vec_near, vec_far,
    in_sem, w_send, w_recv, f_send, f_recv, v_send, v_recv, h_send, h_recv, p_send, p_recv, n_send, n_recv, d_send, d_recv,
    r_send, r_recv, m_send, m_recv, gv_send, gv_recv, gm_send, gm_recv, gn_send, gn_recv, gd_send, gd_recv,
    *scratch,
):
    me, j = lax.axis_index("section"), lax.axis_index("dp")
    core = lax.rem(j, 2)
    chip = j // 2
    near, piece_rows, piece_lanes, far_steps = shares_of(dp)
    place = lax.rem(chip, near)
    xor = lax.bitwise_xor

    def device(k, q, other=0):
        return (xor(me, k), xor(j, 2 * q + other))

    mate = device(0, 0, 1)
    sections = [device(k, 0) for k in range(1, SECTIONS)]
    around = [(k, q) for k in range(SECTIONS) for q in range(near) if (k, q) != (0, 0)]
    far = [(me, xor(j, 2 * near << b)) for b in range(far_steps)]
    waiting = []

    def remote(src, dst, send, recv, to):
        return pltpu.make_async_remote_copy(src, dst, send, recv, device_id=to, device_id_type=MESH)

    def when(condition, act):
        if condition is None:
            act()
        else:
            pl.when(condition)(act)

    def go(copy, condition=None):
        when(condition, lambda: copy.start())
        waiting.append((copy, condition))

    loads = [
        pltpu.make_async_copy(inputs_ref.at[me], x_ref, in_sem.at[0]),
        pltpu.make_async_copy(cot_in_ref.at[me], cot_ref, in_sem.at[1]),
        pltpu.make_async_copy(routes_in_ref.at[0, me], routes_ref.at[0], in_sem.at[2]),
        pltpu.make_async_copy(routes_in_ref.at[1, me], routes_ref.at[1], in_sem.at[3]),
        pltpu.make_async_copy(vec_own.at[0], vec_ref.at[me], in_sem.at[4]),
        pltpu.make_async_copy(win_own.at[0], win_ref.at[me], in_sem.at[5]),
        pltpu.make_async_copy(wout_own.at[0], wout_ref.at[me], in_sem.at[6]),
    ]
    for copy in loads:
        copy.start()

    barrier = pltpu.get_barrier_semaphore()
    everyone = [device(k, q) for k, q in around] + [mate] + far
    for to in everyone:
        pl.semaphore_signal(barrier, inc=1, device_id=to, device_id_type=MESH)
    pl.semaphore_wait(barrier, len(everyone))

    own_rows = pl.ds(pl.multiple_of(core * HALF, HALF), HALF)
    tail_rows = pl.ds(pl.multiple_of(D + core * D, D), D)
    pieces = [(win_own, win_ref, own_rows), (wout_own, wout_ref, own_rows), (wout_own, wout_ref, tail_rows)]

    def has(piece, t):
        return piece < 2 or t % 2 == 1

    odd = lax.rem(me, 2) == 1
    vec_copies = [remote(vec_own.at[0], vec_ref.at[me], v_send.at[k], v_recv.at[k], to) for k, to in enumerate(sections)]
    for copy in vec_copies:
        go(copy)
    for p, (source, target, rows) in enumerate(pieces):
        for k, to in enumerate(sections):
            go(remote(source.at[0, rows], target.at[me, rows], w_send.at[p, k], w_recv.at[p, me], to), None if p < 2 else odd)

    foreign = [me != t for t in range(SECTIONS)]
    hand_on, arrive = {}, {}
    for t in range(SECTIONS):
        for p in range(3):
            if has(p, t):
                spot = pieces[p][1].at[t, pieces[p][2]]
                arrive[t, p] = remote(spot, spot, w_send.at[p, 0], w_recv.at[p, t], mate)
                hand_on[t, p] = remote(spot, spot, f_send.at[p, t], f_recv.at[p, t], mate)
                waiting.append((hand_on[t, p], foreign[t]))

    def forward_weights(t, p):
        if has(p, t):

            @pl.when(foreign[t])
            def _():
                arrive[t, p].wait_recv()
                hand_on[t, p].start()

    def take_weights(t, p):
        if has(p, t):
            pl.when(foreign[t])(lambda: hand_on[t, p].wait_recv())

    other_rows = pl.ds(pl.multiple_of((1 - core) * HALF, HALF), HALF)

    def quarter(k):
        return pl.ds(pl.multiple_of(k * PART, PART), PART)

    def share_rows(q):
        return pl.multiple_of(lax.rem(q, PART // piece_rows) * piece_rows, piece_rows)

    def share_lanes(q):
        return pl.ds(pl.multiple_of((q // (PART // piece_rows)) * piece_lanes, piece_lanes), piece_lanes)

    def share_in_half(k, q):
        return pl.ds(pl.multiple_of(k * PART + share_rows(q), piece_rows), piece_rows), share_lanes(q)

    my_share = share_in_half(me, place)
    steps = {}

    def halves_start(t):
        count = blocks_of(t)
        blocks = pl.ds(0, count)
        for b in range(count):
            send_half[t, b] = grad_ref[b, other_rows].astype(BF)
        copy = remote(send_half.at[t, blocks], got_half.at[t, blocks], h_send.at[t], h_recv.at[t], mate)
        go(copy)
        for b in range(count):
            own_half[t, b] = grad_ref[b, own_rows].astype(BF)
        steps[t] = [copy]

    def halves_end(t):
        steps[t][0].wait_recv()
        for b in range(blocks_of(t)):
            half_sum[t, b] = (own_half[t, b].astype(F32) + got_half[t, b].astype(F32)).astype(BF)

    def parts_start(t):
        blocks = pl.ds(0, blocks_of(t))
        steps[t] = [
            remote(half_sum.at[t, blocks, quarter(to[0])], got_part.at[t, k, blocks], p_send.at[t, k], p_recv.at[t, k], to)
            for k, to in enumerate(sections)
        ]
        for copy in steps[t]:
            go(copy)

    def parts_end(t):
        for copy in steps[t]:
            copy.wait_recv()
        for b in range(blocks_of(t)):
            total = half_sum[t, b, quarter(me)].astype(F32)
            for k in range(SECTIONS - 1):
                total = total + got_part[t, k, b].astype(F32)
            part_sum[t, b] = total.astype(BF)

    def near_start(t):
        blocks = pl.ds(0, blocks_of(t))
        steps[t] = []
        for q in range(1, near):
            to_place = xor(place, q)
            source = part_sum.at[t, blocks, pl.ds(share_rows(to_place), piece_rows), share_lanes(to_place)]
            steps[t].append(remote(source, got_near.at[t, q, blocks], n_send.at[t, q], n_recv.at[t, q], device(0, q)))
        for copy in steps[t]:
            go(copy)

    def around_start(t):
        blocks = pl.ds(0, blocks_of(t))
        steps[t] = []
        for k, q in around:
            rows, lanes = share_in_half(xor(me, k), xor(place, q))
            slot = k * near + q
            source = half_sum.at[t, blocks, rows, lanes]
            steps[t].append(remote(source, got_near.at[t, slot, blocks], n_send.at[t, slot], n_recv.at[t, slot], device(k, q)))
        for copy in steps[t]:
            go(copy)

    def share_end(t, mine, slots):
        for copy in steps[t]:
            copy.wait_recv()
        for b in range(blocks_of(t)):
            total = mine(b).astype(F32)
            for slot in slots:
                total = total + got_near[t, slot, b].astype(F32)
            share[t, 0, b] = total.astype(BF)
        blocks = pl.ds(0, blocks_of(t))
        for step in range(far_steps):
            copy = remote(share.at[t, step, blocks], got_far.at[t, step, blocks], d_send.at[t, step], d_recv.at[t, step], far[step])
            go(copy)
            copy.wait_recv()
            for b in range(blocks_of(t)):
                share[t, step + 1, b] = (share[t, step, b].astype(F32) + got_far[t, step, b].astype(F32)).astype(BF)
        deliver(t)

    def near_end(t):
        rows = pl.ds(share_rows(place), piece_rows)
        share_end(t, lambda b: part_sum[t, b, rows, share_lanes(place)], range(1, near))

    def around_end(t):
        share_end(t, lambda b: half_sum[t, b, my_share[0], my_share[1]], [k * near + q for k, q in around])

    def deliver(t):
        blocks = pl.ds(0, blocks_of(t))
        last = share.at[t, far_steps, blocks]
        spot = result.at[blocks, core, my_share[0], my_share[1]]
        for q in range(near):
            to = (t, xor(j, 2 * q))
            go(remote(last, spot, r_send.at[t, q], r_recv.at[me, place], to), None if q > 0 else me != t)

        @pl.when(me == t)
        def _():
            for b in range(blocks_of(t)):
                result[b, core, my_share[0], my_share[1]] = share[t, far_steps, b]

    copies = {}

    def vectors_start():
        copies["sections"] = [
            remote(gvec_part.at[to[0]], vec_got.at[k], gv_send.at[k], gv_recv.at[k], to) for k, to in enumerate(sections)
        ]
        for copy in copies["sections"]:
            go(copy)

    def vectors_mate():
        for copy in copies["sections"]:
            copy.wait_recv()
        vec_sum[0] = gvec_part[me] + vec_got[0] + vec_got[1] + vec_got[2]
        copies["mate"] = remote(vec_sum.at[0], vec_mate, gm_send.at[0], gm_recv.at[0], mate)
        go(copies["mate"])

    def vectors_near():
        copies["mate"].wait_recv()
        vec_sum[1] = vec_sum[0] + vec_mate[...]
        copies["near"] = [remote(vec_sum.at[1], vec_near.at[q], gn_send.at[q], gn_recv.at[q], device(0, q)) for q in range(1, near)]
        for copy in copies["near"]:
            go(copy)

    def vectors_end():
        for copy in copies["near"]:
            copy.wait_recv()
        vec_near[0] = vec_sum[1]
        total = vec_near[place]
        for q in range(1, near):
            total = total + vec_near[xor(place, q)]
        vec_sum[2] = total
        for step in range(far_steps):
            copy = remote(vec_sum.at[2 + step], vec_far.at[step], gd_send.at[step], gd_recv.at[step], far[step])
            go(copy)
            copy.wait_recv()
            vec_sum[3 + step] = vec_sum[2 + step] + vec_far[step]
        gvec_ref[0] = vec_sum[2 + far_steps] * (1.0 / images)

    def on(act, *rest):
        return lambda: act(*rest)

    def inputs_here():
        for copy in loads[:4]:
            copy.wait()

    def vectors_here():
        for copy in vec_copies:
            copy.wait_recv()
        for copy in loads[4:]:
            copy.wait()

    plan = {
        ("inputs", 0): [inputs_here],
        ("vectors", 0): [vectors_here],
        ("prepared", 0): [on(forward_weights, 0, 0), on(forward_weights, 0, 1)],
    }
    for t in range(SECTIONS):
        plan["weights", t] = [on(take_weights, t, 0), on(take_weights, t, 1), on(take_weights, t, 2)]
        plan["next", t] = [on(forward_weights, t + 1, p) for p in range(3)] if t + 1 < SECTIONS else []
        plan["grads", t] = [on(halves_start, t)]
    plan["image", 6] = [on(halves_end, 3), on(parts_start, 3)]
    plan["image", 5] = [on(parts_end, 3), on(near_start, 3)]
    plan["norm", 4] = [on(halves_end, 2), on(parts_start, 2)]
    plan["image", 2] = [on(halves_end, 1), on(parts_start, 1)]
    plan["image", 3] = [on(near_end, 3)]
    plan["half", 0] = [on(parts_end, 2), on(near_start, 2)]
    plan["half", 1] = [on(parts_end, 1), on(near_start, 1)]
    plan["image", 1] = [on(near_end, 2)]
    plan["norm", 0] = [on(halves_end, 0), on(around_start, 0)]
    plan["conv", 1] = [vectors_start, on(near_end, 1)]
    done = []

    def at_point(name, s):
        for act in plan.get((name, s), []):
            act()
        done.append((name, s))

    layers(
        n, at_point,
        x_ref, cot_ref, routes_ref, vec_ref, win_ref, wout_ref, fin_ref, gin_ref, gvec_part, grad_ref, *scratch,
    )
    assert all(key in done or not plan[key] for key in plan)
    vectors_mate()
    vectors_near()
    around_end(0)
    vectors_end()

    for parity in range(2):
        blocks = pl.ds(0, blocks_of(parity))
        half = result.at[blocks, core]

        @pl.when(lax.rem(me, 2) == parity)
        def _():
            for k, q in around:
                from_me, from_place = xor(me, k), xor(place, q)
                rows, lanes = share_in_half(from_me, from_place)
                spot = result.at[blocks, core, rows, lanes]
                remote(spot, spot, r_send.at[0, 0], r_recv.at[from_me, from_place], mate).wait_recv()

        copy = remote(half, half, m_send.at[parity], m_recv.at[parity], mate)
        go(copy, lax.rem(me, 2) == parity)

    def finish(c):
        for b in range(3):
            rows = pl.ds(pl.multiple_of(c * HALF, HALF), HALF)
            ga_ref[0, rows, b * D : (b + 1) * D] = result[b, c].astype(F32) * (1.0 / images)
            gb_ref[0, pl.ds(pl.multiple_of(b * D + c * HALF, HALF), HALF)] = result[3 + b, c].astype(F32) * (1.0 / images)

    finish(core)
    for parity in range(2):
        half = result.at[pl.ds(0, blocks_of(parity)), 1 - core]
        pl.when(lax.rem(me, 2) == parity)(
            lambda half=half, parity=parity: remote(half, half, m_send.at[parity], m_recv.at[parity], mate).wait_recv()
        )
    finish(1 - core)

    @pl.when(lax.rem(me, 2) == 0)
    def _():
        gb_ref[0, D:HID] = jnp.zeros((HID - D, D), F32)

    for copy, condition in waiting:
        when(condition, lambda copy=copy: copy.wait_send())


def per_device(inputs, cotangent, routes, vectors, in_weight, out_weight):
    micro, n = inputs.shape[:2]
    dp = lax.axis_size("dp")
    near, piece_rows, piece_lanes, far_steps = shares_of(dp)
    images = micro * n * dp
    vmem = pl.BlockSpec(memory_space=pltpu.VMEM)
    hbm = pl.BlockSpec(memory_space=pl.ANY)
    dma = pltpu.SemaphoreType.DMA
    by_token = jax.ShapeDtypeStruct((1, PATCHES, n, D), BF)
    some = max(far_steps, 1)

    def grad_buffer(*shape):
        return pltpu.VMEM((SECTIONS,) + shape, BF)

    fin, gin, gvec, ga, gb = pl.pallas_call(
        functools.partial(whole_kernel, n, dp, images),
        out_shape=(
            by_token,
            by_token,
            jax.ShapeDtypeStruct((1, VEC_ROWS, D), F32),
            jax.ShapeDtypeStruct((1, D, HID), F32),
            jax.ShapeDtypeStruct((1, HID, D), F32),
        ),
        in_specs=[hbm] * 6,
        out_specs=(vmem,) * 5,
        scratch_shapes=[
            pltpu.VMEM((PATCHES, n, D), BF),
            pltpu.VMEM((PATCHES, n, D), BF),
            pltpu.VMEM((2, n, TOPK, REGIONS), jnp.int32),
            pltpu.VMEM((SECTIONS, VEC_ROWS, D), F32),
            pltpu.VMEM((SECTIONS, D, HID), BF),
            pltpu.VMEM((SECTIONS, HID, D), BF),
            pltpu.VMEM((SECTIONS, VEC_ROWS, D), F32),
            pltpu.VMEM((6, BLOCK, BLOCK), F32),
            grad_buffer(6, HALF, BLOCK),
            grad_buffer(6, HALF, BLOCK),
            grad_buffer(6, HALF, BLOCK),
            grad_buffer(6, HALF, BLOCK),
            grad_buffer(3, 6, PART, BLOCK),
            grad_buffer(6, PART, BLOCK),
            grad_buffer(SECTIONS * near, 6, piece_rows, piece_lanes),
            grad_buffer(far_steps + 1, 6, piece_rows, piece_lanes),
            grad_buffer(some, 6, piece_rows, piece_lanes),
            pltpu.VMEM((6, 2, HALF, BLOCK), BF),
            pltpu.VMEM((3, VEC_ROWS, D), F32),
            pltpu.VMEM((3 + far_steps, VEC_ROWS, D), F32),
            pltpu.VMEM((VEC_ROWS, D), F32),
            pltpu.VMEM((near, VEC_ROWS, D), F32),
            pltpu.VMEM((some, VEC_ROWS, D), F32),
            dma((7,)),
            dma((3, 3)), dma((3, SECTIONS)),
            dma((3, SECTIONS)), dma((3, SECTIONS)),
            dma((3,)), dma((3,)),
            dma((SECTIONS,)), dma((SECTIONS,)),
            dma((SECTIONS, 3)), dma((SECTIONS, 3)),
            dma((SECTIONS, SECTIONS * near)), dma((SECTIONS, SECTIONS * near)),
            dma((SECTIONS, some)), dma((SECTIONS, some)),
            dma((SECTIONS, near)), dma((SECTIONS, near)),
            dma((2,)), dma((2,)),
            dma((3,)), dma((3,)),
            dma((1,)), dma((1,)),
            dma((near,)), dma((near,)),
            dma((some,)), dma((some,)),
        ]
        + layer_scratch(n),
        compiler_params=pltpu.CompilerParams(
            vmem_limit_bytes=60 * 1024 * 1024, collective_id=0, has_side_effects=True
        ),
        name="two_layers",
    )(
        jnp.transpose(inputs, (0, 2, 1, 3)),
        jnp.transpose(cotangent, (0, 2, 1, 3)),
        jnp.swapaxes(routes, 3, 4),
        vectors,
        in_weight,
        out_weight,
    )
    return jnp.transpose(fin, (0, 2, 1, 3)), jnp.transpose(gin, (0, 2, 1, 3)), gvec, ga, gb


def solution(mesh):
    in_specs = (
        P(None, "dp", None, None),
        P(None, "dp", None, None),
        P(None, None, "dp", None, None),
        P("section", None, None),
        P("section", None, None),
        P("section", None, None),
    )
    out_specs = (
        P("section", "dp", None, None),
        P("section", "dp", None, None),
        P("section", None, None),
        P("section", None, None),
        P("section", None, None),
    )
    return jax.shard_map(
        per_device, mesh=mesh, in_specs=in_specs, out_specs=out_specs, check_vma=False
    )
```

time: 139 us -> 89.2 us (0.64)
  Pallas kernels: 126 us -> 81.8 us
  local copies, waits for them, and re-layouts: 11.5 us -> 6.48 us
    pallas_call x1, Pallas kernels: 126 us -> 81.8 us  [per_device(): pl.pallas_call(functools.partial(whole_kernel, n, dp, images), out_shape=...]
    pallas_call x2 -> x0, local copies, waits for them, and re-layouts: 3.61 us -> none  [per_device(): pl.pallas_call(functools.partial(whole_kernel, n, dp, images), out_shape=...]
    unnamed x14 -> x11, local copies, waits for them, and re-layouts: 7.93 us -> 6.48 us
where the time goes in v3:
time: 89.2 us; the launch traced here: 88.9 us
  Pallas kernels  81.8 us (92%)
  local copies, waits for them, and re-layouts  6.48 us (7%)
    pallas_call x1, Pallas kernels, per_device(): pl.pallas_call(functools.partial(whole_kernel, n, dp, images), out_shape=...  81.8 us
    unnamed x11, local copies, waits for them, and re-layouts  6.48 us

profile of v3, /device:TPU:1, one launch (start us, length us, event | category | flops | bytes accessed | tf_op | source)
XLA Modules:
  0.0 88.9 jit_solution(14793291167873183015)
XLA Ops:
  0.6 81.8 %two_layers.1 = (bf16[1,196,2,256]{3,2,1,0:T(2,128)(2,1)}, bf16[1,196,2,256]{3,2,1,0:T(2,128)(2,1)}, f32[1,16,256]{2,1,0:T(8,128)}, f32[1,256,768]{2,1,0:T(8,128)}, f32[1,768,256]{2,1,0:T(8,128)}) custom-call(bf16[4,196,2,256]{3,2,1,0:T(2,128)(2,1)} %bitcast.5, bf16[4,196,2,256]{3,2,1,0:T(2,128)(2,1)} %bitcast.6, s32[2,4,2,4,49]{4,3,2,1,0:T(4,128)} %bitcast.9, ...), custom_call_target="tpu_custom_call" | custom-call | tf_op jit(solution)/shard_map/two_layers/pallas_call | solution.py:820
  82.4 0.0 copy-start.1
  82.4 1.8 %copy.16 = bf16[1,2,196,256]{3,1,2,0:T(2,128)(2,1)} copy(bf16[1,2,196,256]{3,1,2,0:T(2,128)(2,1)} %bitcast.8) | data formatting | bytes 401408
  84.2 0.0 copy-start.2
  84.2 1.8 %copy.17 = bf16[1,2,196,256]{3,1,2,0:T(2,128)(2,1)} copy(bf16[1,2,196,256]{3,1,2,0:T(2,128)(2,1)} %bitcast.7) | data formatting | bytes 401408
  86.0 0.0 copy-done.2
  86.0 0.6 copy.18
  86.6 0.0 copy-done.1
  86.6 0.0 copy-start
  86.6 0.9 copy.19
  87.5 0.5 copy-done
  88.0 0.9 copy.20
Async XLA Ops:
  82.4 4.2 %copy-start.1 = (f32[1,256,768]{2,1,0:T(8,128)S(1)}, f32[1,256,768]{2,1,0:T(8,128)}, u32[]{:S(2)}) copy-start(f32[1,256,768]{2,1,0:T(8,128)} %get-tuple-element.23) | copy-start | bytes 2359300
  84.2 1.8 %copy-start.2 = (f32[1,16,256]{2,1,0:T(8,128)S(1)}, f32[1,16,256]{2,1,0:T(8,128)}, u32[]{:S(2)}) copy-start(f32[1,16,256]{2,1,0:T(8,128)} %get-tuple-element.22) | copy-start | bytes 49156
  86.6 1.4 %copy-start = (f32[1,768,256]{2,1,0:T(8,128)S(1)}, f32[1,768,256]{2,1,0:T(8,128)}, u32[]{:S(2)}) copy-start(f32[1,768,256]{2,1,0:T(8,128)} %get-tuple-element.24) | copy-start | bytes 2359300

commit v4 on v3

--- a/solution.py
+++ b/solution.py
@@ -86,9 +86,30 @@
     return one_hot((own == region) & (c < SIDE) & (r < SIDE))
 
 
+def weight_grads(scratch, s, first, count, half):
+    nm, at, act, g, dproj = (scratch[LAYER_SCRATCH.index(name)] for name in ("nm", "at", "act", "g", "dproj"))
+    results = []
+    ins = min(first + count, 3) - first
+    if ins > 0:
+        lanes = pl.ds(pl.multiple_of(half * LANES, LANES), LANES)
+        wide = dot(nm[s, :, lanes], dproj[:, first * D : (first + ins) * D], 0, 0)
+        results += [wide[:, b * D : (b + 1) * D] for b in range(ins)]
+    for b in range(max(first, 3) - 3, first + count - 3):
+        lanes = pl.ds(pl.multiple_of(b * D + half * LANES, LANES), LANES)
+        left = act[s // 2, :, lanes] if s % 2 == 1 else at[s // 2, :, lanes]
+        results.append(dot(left, g[...], 0, 0))
+    return results
+
+
+LAYER_SCRATCH = (
+    "hs", "zh", "inv", "nm", "pr", "pt", "at", "act", "gp", "bias", "mixed", "g", "dproj", "cv", "cvl", "cvr",
+    "dom", "qm", "dsb", "tmp", "dqt", "km", "wide",
+)
+
+
 def layers(
     n, at_point,
-    x_ref, cot_ref, routes_ref, vec_ref, win_ref, wout_ref, fin_ref, gin_ref, gvec_ref, grad_ref,
+    x_ref, cot_ref, routes_ref, vec_ref, win_ref, wout_ref, fin_ref, gin_ref, gvec_ref,
     hs, zh, inv, nm, pr, pt, at, act, gp, bias, mixed, g, dproj, cv, cvl, cvr, dom, qm, dsb, tmp, dqt, km, wide,
 ):
     pairs = PATCHES * n
@@ -213,14 +234,15 @@
                 scores = dot(keys, pr[a, whole, lanes], 1, 1) * (SCALE * LOG2E) + bias[a, i]
                 expo = jnp.exp2(scores - jnp.max(scores, axis=0, keepdims=True))
                 pt[a, i, :, h * ROWS : (h + 1) * ROWS] = (expo * (1.0 / col_sum(expo))).astype(BF)
+            pl.when(i == 0)(lambda: at_point("scores", s))
             for h in range(HEADS):
                 own = slice(h * HEAD_DIM, (h + 1) * HEAD_DIM)
                 dqt[own] = dot(tmp[own, 0:LIVE], pt[a, i, :, h * ROWS : (h + 1) * ROWS])
             attended = transposed(dqt[...].astype(BF)).astype(BF)
             at[a, whole] = attended
+            pl.when(i == 0)(lambda: at_point("out", s))
             out = mixed[rows] + dot(attended[:LIVE], wout_ref[s, 0:D]) + vec[2:3]
             hs[s + 1, rows] = out.astype(BF)
-            pl.when(i == 0)(lambda: at_point("next", s))
             return carry
 
         lax.fori_loop(0, n, image, 0)
@@ -244,13 +266,13 @@
                 value, slope = gelu_pair(hidden)
                 act[a, rows, lanes] = value.astype(BF)
                 gp[a, rows, lanes] = slope
+            pl.when(i == 0)(lambda: at_point("out", s))
             out = hs[s, rows].astype(F32) + dot(act[a, rows], wout_ref[s]) + vec[2:3]
             if s + 1 < SECTIONS:
                 live = (iota((LIVE, D), 0) & (PITCH - 1)) < SIDE
                 hs[s + 1, rows] = jnp.where(live, out, 0.0).astype(BF)
             else:
                 wide[rows] = out.astype(BF)
-            pl.when(i == 0)(lambda: at_point("next", s))
             return carry
 
         lax.fori_loop(0, n, image, 0)
@@ -277,6 +299,7 @@
 
     def dense_backward(s):
         a = s // 2
+        at_point("first grads", s)
         for i in range(n):
             rows = rows_of(i)
             for j in range(3):
@@ -285,10 +308,6 @@
                 d_hidden = (d_active * gp[a, rows, lanes]).astype(BF)
                 dproj[rows, lanes] = d_hidden
                 add_row(s, 3 + j, fold(d_hidden.astype(F32)))
-        for j in range(3):
-            lanes = slice(j * D, (j + 1) * D)
-            grad_ref[j] = dot(nm[s], dproj[:, lanes], 0, 0)
-            grad_ref[3 + j] = dot(act[a, :, lanes], g[...], 0, 0)
         at_point("grads", s)
         for i in range(n):
             rows = rows_of(i)
@@ -308,30 +327,32 @@
         a = s // 2
         vec = vec_ref.at[s]
         nothing = jnp.zeros((), BF)
-        grad_ref[3] = dot(at[a], g[...], 0, 0)
         for i in range(n):
             rows = rows_of(i)
             whole = rows_of(i, ROWS)
-            km[...] = dot(g[whole], wout_ref[s, 0:D], 1, 1).astype(BF)
+            km[whole] = dot(g[whole], wout_ref[s, 0:D], 1, 1).astype(BF)
+            for h in range(HEADS):
+                dom[h * ROWS : (h + 1) * ROWS] = jnp.where(own_lanes(h, ROWS), km[whole, half_of(h)], nothing)
+            for half in range(2):
+                lanes = slice(2 * D + half * LANES, 2 * D + (half + 1) * LANES)
+                four = slice(half * 4 * ROWS, (half + 1) * 4 * ROWS)
+                dproj[rows, lanes] = dot(pt[a, i, :, four], dom[four]).astype(BF)
+        at_point("first grads", s)
+        for i in range(n):
+            rows = rows_of(i)
+            whole = rows_of(i, ROWS)
             tmp[...] = transposed(pr[a, whole, D : 2 * D]).astype(BF)
             for h in range(HEADS):
-                lanes = half_of(h)
-                row = slice(h * ROWS, (h + 1) * ROWS)
-                dom[row] = jnp.where(own_lanes(h, ROWS), km[:, lanes], nothing)
-                qm[row] = jnp.where(own_lanes(h, ROWS), pr[a, whole, lanes], nothing)
+                qm[h * ROWS : (h + 1) * ROWS] = jnp.where(own_lanes(h, ROWS), pr[a, whole, half_of(h)], nothing)
             for h in range(HEADS):
                 lanes = half_of(h)
                 row = slice(h * ROWS, (h + 1) * ROWS)
                 values = jnp.where(own_lanes(h, LIVE), pr[a, rows, slice(2 * D + lanes.start, 2 * D + lanes.stop)], nothing)
-                d_weights = dot(values, km[:, lanes], 1, 1)
+                d_weights = dot(values, km[whole, lanes], 1, 1)
                 weights = pt[a, i, :, row].astype(F32)
                 dsb[:, row] = (weights * (d_weights - col_sum(weights * d_weights))).astype(BF)
                 if h == 3:
                     at_point("half", 2 * s + i)
-            for half in range(2):
-                lanes = slice(2 * D + half * LANES, 2 * D + (half + 1) * LANES)
-                four = slice(half * 4 * ROWS, (half + 1) * 4 * ROWS)
-                dproj[rows, lanes] = dot(pt[a, i, :, four], dom[four]).astype(BF)
             for h in range(HEADS):
                 own = slice(h * HEAD_DIM, (h + 1) * HEAD_DIM)
                 dqt[own] = dot(tmp[own, 0:LIVE], dsb[:, h * ROWS : (h + 1) * ROWS])
@@ -341,8 +362,6 @@
                 dproj[rows, lanes] = (dot(dsb[:, four], qm[four]) * SCALE).astype(BF)
             dproj[rows, 0:D] = (transposed(dqt[...].astype(BF))[:LIVE] * SCALE).astype(BF)
             at_point("image", 2 * s + i)
-        for j in range(3):
-            grad_ref[j] = dot(nm[s], dproj[:, j * D : (j + 1) * D], 0, 0)
         at_point("grads", s)
         for i in range(n):
             rows = rows_of(i)
@@ -384,10 +403,10 @@
         if s == 2:
             attention_start(s)
         (attention_forward, dense_forward)[s % 2](s)
-    fin_ref[0] = dot(gather(), wide[...]).astype(BF).reshape(PATCHES, n, D)
+    fin_ref[...] = dot(gather(), wide[...]).astype(BF).reshape(PATCHES, n, D)
     for s in reversed(range(SECTIONS)):
         (attention_backward, dense_backward)[s % 2](s)
-    gin_ref[0] = dot(gather(), g[...]).astype(BF).reshape(PATCHES, n, D)
+    gin_ref[...] = dot(gather(), g[...]).astype(BF).reshape(PATCHES, n, D)
 
 
 def layer_scratch(n):
@@ -414,28 +433,29 @@
         pltpu.VMEM((LIVE, HEADS * ROWS), BF),
         pltpu.VMEM((D, ROWS), BF),
         pltpu.VMEM((D, ROWS), F32),
-        pltpu.VMEM((ROWS, D), BF),
+        pltpu.VMEM((total, D), BF),
         pltpu.VMEM((total, D), BF),
     ]
 
 
 def compute_kernel(n, *refs):
-    x_ref, cot_ref, routes_ref, vec_ref, win_ref, wout_ref, fin_ref, gin_ref, gvec_ref, ga_ref, gb_ref, grad_ref = refs[:12]
+    x_ref, cot_ref, routes_ref, vec_ref, win_ref, wout_ref, fin_ref, gin_ref, gvec_ref, ga_ref, gb_ref = refs[:11]
 
     def at_point(name, s):
         if name != "grads":
             return
-        for j in range(3):
-            ga_ref[s, :, j * D : (j + 1) * D] = grad_ref[j]
-            if s % 2 == 1 or j == 0:
-                gb_ref[s, j * D : (j + 1) * D] = grad_ref[3 + j]
-            else:
-                gb_ref[s, j * D : (j + 1) * D] = jnp.zeros((D, D), F32)
-
-    layers(
-        n, at_point,
-        x_ref, cot_ref, routes_ref, vec_ref, win_ref, wout_ref, fin_ref, gin_ref, gvec_ref, grad_ref, *refs[12:],
-    )
+        count = 6 if s % 2 == 1 else 4
+        for half in range(2):
+            for b, value in enumerate(weight_grads(refs[11:], s, 0, count, half)):
+                rows = slice(half * LANES, (half + 1) * LANES)
+                if b < 3:
+                    ga_ref[s, rows, b * D : (b + 1) * D] = value
+                else:
+                    gb_ref[s, (b - 3) * D + half * LANES : (b - 3) * D + (half + 1) * LANES] = value
+        if s % 2 == 0:
+            gb_ref[s, D:HID] = jnp.zeros((HID - D, D), F32)
+
+    layers(n, at_point, x_ref, cot_ref, routes_ref, vec_ref, win_ref, wout_ref, fin_ref.at[0], gin_ref.at[0], gvec_ref, *refs[11:])
 
 
 def compute(x, cot, routes, vec, win, wout):
@@ -453,7 +473,7 @@
         ),
         in_specs=[vmem] * 6,
         out_specs=(vmem,) * 5,
-        scratch_shapes=[pltpu.VMEM((6, BLOCK, BLOCK), F32)] + layer_scratch(n),
+        scratch_shapes=layer_scratch(n),
         compiler_params=pltpu.CompilerParams(vmem_limit_bytes=56 * 1024 * 1024),
         name="layers_alone",
     )(jnp.transpose(x, (1, 0, 2)), jnp.transpose(cot, (1, 0, 2)), jnp.swapaxes(routes, 2, 3), vec, win, wout)
@@ -467,6 +487,9 @@
 
 def blocks_of(t):
     return 6 if t % 2 == 1 else 4
+
+
+GROUPS = ((0, 0, 2), (1, 0, 6), (2, 0, 4), (3, 0, 6), (0, 2, 2))
 
 
 def shares_of(dp):
@@ -476,12 +499,53 @@
     return near, PART // split, BLOCK // (near // split), (chips // near).bit_length() - 1
 
 
+def piece_slices(dp, piece):
+    near, piece_rows, piece_lanes, _ = shares_of(dp)
+    k, q = piece // near, piece % near
+    rows = k * PART + q % (PART // piece_rows) * piece_rows
+    lanes = q // (PART // piece_rows) * piece_lanes
+    return slice(rows, rows + piece_rows), slice(lanes, lanes + piece_lanes)
+
+
+def results_kernel(dp, images, fin_in, gin_in, gvec_in, result, fin_ref, gin_ref, gvec_ref, ga_ref, gb_ref, ga, gb, sems):
+    copies = [
+        pltpu.make_async_copy(fin_in, fin_ref.at[0], sems.at[0]),
+        pltpu.make_async_copy(gin_in, gin_ref.at[0], sems.at[1]),
+        pltpu.make_async_copy(ga, ga_ref.at[0], sems.at[2]),
+        pltpu.make_async_copy(gb, gb_ref.at[0], sems.at[3]),
+    ]
+    copies[0].start()
+    copies[1].start()
+    gvec_ref[0] = gvec_in[...] * (1.0 / images)
+    for target, first in ((ga, 0), (gb, 3)):
+        for c in range(2):
+            for piece in range(result.shape[1]):
+                rows, lanes = piece_slices(dp, piece)
+                for b in range(3):
+                    value = result[c, piece, first + b].astype(F32) * (1.0 / images)
+                    start = c * HALF + rows.start
+                    if first == 0:
+                        target[start : start + rows.stop - rows.start, b * D + lanes.start : b * D + lanes.stop] = value
+                    else:
+                        target[b * D + start : b * D + start + rows.stop - rows.start, lanes] = value
+        if first == 0:
+            copies[2].start()
+
+    @pl.when(lax.rem(lax.axis_index("section"), 2) == 0)
+    def _():
+        gb[D:HID] = jnp.zeros((HID - D, D), F32)
+
+    copies[3].start()
+    for copy in copies:
+        copy.wait()
+
+
 def whole_kernel(
     n, dp, images,
     inputs_ref, cot_in_ref, routes_in_ref, vec_own, win_own, wout_own,
-    fin_ref, gin_ref, gvec_ref, ga_ref, gb_ref,
-    x_ref, cot_ref, routes_ref, vec_ref, win_ref, wout_ref, gvec_part, grad_ref,
-    own_half, send_half, got_half, half_sum, got_part, part_sum, got_near, share, got_far, result, vec_got, vec_sum, vec_mate, vec_near, vec_far,
+    fin_ref, gin_ref, gvec_ref, result,
+    x_ref, cot_ref, routes_ref, vec_ref, win_ref, wout_ref, gvec_part,
+    own_half, send_half, got_half, half_sum, got_part, part_sum, got_near, share, got_far, vec_got, vec_sum, vec_mate, vec_near, vec_far,
     in_sem, w_send, w_recv, f_send, f_recv, v_send, v_recv, h_send, h_recv, p_send, p_recv, n_send, n_recv, d_send, d_recv,
     r_send, r_recv, m_send, m_recv, gv_send, gv_recv, gm_send, gm_recv, gn_send, gn_recv, gd_send, gd_recv,
     *scratch,
@@ -537,76 +601,85 @@
     tail_rows = pl.ds(pl.multiple_of(D + core * D, D), D)
     pieces = [(win_own, win_ref, own_rows), (wout_own, wout_ref, own_rows), (wout_own, wout_ref, tail_rows)]
 
-    def has(piece, t):
-        return piece < 2 or t % 2 == 1
-
-    odd = lax.rem(me, 2) == 1
+    def spot(p, t):
+        return pieces[p][1].at[t, pieces[p][2]]
+
+    def odd(t):
+        return lax.rem(t, 2) == 1
+
     vec_copies = [remote(vec_own.at[0], vec_ref.at[me], v_send.at[k], v_recv.at[k], to) for k, to in enumerate(sections)]
+    out_copies = [
+        [
+            remote(source.at[0, rows], target.at[me, rows], w_send.at[p, k - 1], w_recv.at[p, me], device(k, 0))
+            for k in (1, 2)
+        ]
+        for p, (source, target, rows) in enumerate(pieces)
+    ]
+    relayed, relay_to = xor(me, 1 + core), xor(me, 2 - core)
+    relays = [remote(spot(p, relayed), spot(p, relayed), w_send.at[p, 2], w_recv.at[p, relayed], (relay_to, j)) for p in range(3)]
+    arrivals, handings, takings = {}, {}, {}
+    for p in range(3):
+        for k in (1, 2, 3):
+            t = xor(me, k)
+            arrivals[p, k] = remote(spot(p, t), spot(p, t), w_send.at[p, 0], w_recv.at[p, t], mate)
+            handings[p, k] = remote(spot(p, t), spot(p, t), f_send.at[p, t], f_recv.at[p, t], mate)
+        for t in range(SECTIONS):
+            if p < 2 or t % 2 == 1:
+                takings[p, t] = remote(spot(p, t), spot(p, t), f_send.at[p, t], f_recv.at[p, t], mate)
+    foreign = [me != t for t in range(SECTIONS)]
+
+    def send_weights(p):
+        for copy in out_copies[p]:
+            go(copy, odd(me) if p == 2 else None)
+
+    def pass_on(p, ks):
+        for k in ks:
+            condition = odd(xor(me, k)) if p == 2 else None
+            when(condition, lambda: arrivals[p, k].wait_recv())
+        if ks != (3,):
+            go(relays[p], odd(relayed) if p == 2 else None)
+        for k in ks:
+            go(handings[p, k], odd(xor(me, k)) if p == 2 else None)
+
+    def take_weights(t, p):
+        if p < 2 or t % 2 == 1:
+            pl.when(foreign[t])(lambda: takings[p, t].wait_recv())
+
     for copy in vec_copies:
         go(copy)
-    for p, (source, target, rows) in enumerate(pieces):
-        for k, to in enumerate(sections):
-            go(remote(source.at[0, rows], target.at[me, rows], w_send.at[p, k], w_recv.at[p, me], to), None if p < 2 else odd)
-
-    foreign = [me != t for t in range(SECTIONS)]
-    hand_on, arrive = {}, {}
-    for t in range(SECTIONS):
-        for p in range(3):
-            if has(p, t):
-                spot = pieces[p][1].at[t, pieces[p][2]]
-                arrive[t, p] = remote(spot, spot, w_send.at[p, 0], w_recv.at[p, t], mate)
-                hand_on[t, p] = remote(spot, spot, f_send.at[p, t], f_recv.at[p, t], mate)
-                waiting.append((hand_on[t, p], foreign[t]))
-
-    def forward_weights(t, p):
-        if has(p, t):
-
-            @pl.when(foreign[t])
-            def _():
-                arrive[t, p].wait_recv()
-                hand_on[t, p].start()
-
-    def take_weights(t, p):
-        if has(p, t):
-            pl.when(foreign[t])(lambda: hand_on[t, p].wait_recv())
-
-    other_rows = pl.ds(pl.multiple_of((1 - core) * HALF, HALF), HALF)
+    send_weights(0)
+
+
+    def piece_of(k, q):
+        return k * near + q
 
     def quarter(k):
-        return pl.ds(pl.multiple_of(k * PART, PART), PART)
-
-    def share_rows(q):
-        return pl.multiple_of(lax.rem(q, PART // piece_rows) * piece_rows, piece_rows)
-
-    def share_lanes(q):
-        return pl.ds(pl.multiple_of((q // (PART // piece_rows)) * piece_lanes, piece_lanes), piece_lanes)
-
-    def share_in_half(k, q):
-        return pl.ds(pl.multiple_of(k * PART + share_rows(q), piece_rows), piece_rows), share_lanes(q)
-
-    my_share = share_in_half(me, place)
+        return pl.ds(pl.multiple_of(k * near, near), near)
+
+    mine = piece_of(me, place)
     steps = {}
 
     def halves_start(t):
-        count = blocks_of(t)
-        blocks = pl.ds(0, count)
-        for b in range(count):
-            send_half[t, b] = grad_ref[b, other_rows].astype(BF)
-        copy = remote(send_half.at[t, blocks], got_half.at[t, blocks], h_send.at[t], h_recv.at[t], mate)
+        section, first, count = GROUPS[t]
+        for b, value in enumerate(weight_grads(scratch, section, first, count, 1 - core)):
+            send_half[t][b] = value.astype(BF)
+        copy = remote(send_half[t], got_half[t], h_send.at[t], h_recv.at[t], mate)
         go(copy)
-        for b in range(count):
-            own_half[t, b] = grad_ref[b, own_rows].astype(BF)
+        for b, value in enumerate(weight_grads(scratch, section, first, count, core)):
+            own_half[t][b] = value.astype(BF)
         steps[t] = [copy]
 
     def halves_end(t):
         steps[t][0].wait_recv()
-        for b in range(blocks_of(t)):
-            half_sum[t, b] = (own_half[t, b].astype(F32) + got_half[t, b].astype(F32)).astype(BF)
+        for b in range(GROUPS[t][2]):
+            total = own_half[t][b] + got_half[t][b]
+            for piece in range(SECTIONS * near):
+                rows, lanes = piece_slices(dp, piece)
+                half_sum[t][piece, b] = total[rows, lanes]
 
     def parts_start(t):
-        blocks = pl.ds(0, blocks_of(t))
         steps[t] = [
-            remote(half_sum.at[t, blocks, quarter(to[0])], got_part.at[t, k, blocks], p_send.at[t, k], p_recv.at[t, k], to)
+            remote(half_sum[t].at[quarter(to[0])], got_part[t].at[k], p_send.at[t, k], p_recv.at[t, k], to)
             for k, to in enumerate(sections)
         ]
         for copy in steps[t]:
@@ -615,69 +688,53 @@
     def parts_end(t):
         for copy in steps[t]:
             copy.wait_recv()
-        for b in range(blocks_of(t)):
-            total = half_sum[t, b, quarter(me)].astype(F32)
-            for k in range(SECTIONS - 1):
-                total = total + got_part[t, k, b].astype(F32)
-            part_sum[t, b] = total.astype(BF)
+        for q in range(near):
+            for b in range(GROUPS[t][2]):
+                total = half_sum[t][piece_of(me, q), b].astype(F32)
+                for k in range(SECTIONS - 1):
+                    total = total + got_part[t][k, q, b].astype(F32)
+                part_sum[t][q, b] = total.astype(BF)
 
     def near_start(t):
-        blocks = pl.ds(0, blocks_of(t))
         steps[t] = []
         for q in range(1, near):
             to_place = xor(place, q)
-            source = part_sum.at[t, blocks, pl.ds(share_rows(to_place), piece_rows), share_lanes(to_place)]
-            steps[t].append(remote(source, got_near.at[t, q, blocks], n_send.at[t, q], n_recv.at[t, q], device(0, q)))
+            source = part_sum[t].at[to_place]
+            steps[t].append(remote(source, got_near[t].at[q], n_send.at[t, q], n_recv.at[t, q], device(0, q)))
         for copy in steps[t]:
             go(copy)
 
-    def around_start(t):
-        blocks = pl.ds(0, blocks_of(t))
-        steps[t] = []
-        for k, q in around:
-            rows, lanes = share_in_half(xor(me, k), xor(place, q))
-            slot = k * near + q
-            source = half_sum.at[t, blocks, rows, lanes]
-            steps[t].append(remote(source, got_near.at[t, slot, blocks], n_send.at[t, slot], n_recv.at[t, slot], device(k, q)))
-        for copy in steps[t]:
-            go(copy)
-
-    def share_end(t, mine, slots):
+    def share_end(t, own, slots):
         for copy in steps[t]:
             copy.wait_recv()
-        for b in range(blocks_of(t)):
-            total = mine(b).astype(F32)
+        for b in range(GROUPS[t][2]):
+            total = own(b).astype(F32)
             for slot in slots:
-                total = total + got_near[t, slot, b].astype(F32)
-            share[t, 0, b] = total.astype(BF)
-        blocks = pl.ds(0, blocks_of(t))
+                total = total + got_near[t][slot, b].astype(F32)
+            share[t][0, b] = total.astype(BF)
         for step in range(far_steps):
-            copy = remote(share.at[t, step, blocks], got_far.at[t, step, blocks], d_send.at[t, step], d_recv.at[t, step], far[step])
+            copy = remote(share[t].at[step], got_far[t].at[step], d_send.at[t, step], d_recv.at[t, step], far[step])
             go(copy)
             copy.wait_recv()
-            for b in range(blocks_of(t)):
-                share[t, step + 1, b] = (share[t, step, b].astype(F32) + got_far[t, step, b].astype(F32)).astype(BF)
+            for b in range(GROUPS[t][2]):
+                share[t][step + 1, b] = (share[t][step, b].astype(F32) + got_far[t][step, b].astype(F32)).astype(BF)
         deliver(t)
 
     def near_end(t):
-        rows = pl.ds(share_rows(place), piece_rows)
-        share_end(t, lambda b: part_sum[t, b, rows, share_lanes(place)], range(1, near))
-
-    def around_end(t):
-        share_end(t, lambda b: half_sum[t, b, my_share[0], my_share[1]], [k * near + q for k, q in around])
+        share_end(t, lambda b: part_sum[t][place, b], range(1, near))
 
     def deliver(t):
-        blocks = pl.ds(0, blocks_of(t))
-        last = share.at[t, far_steps, blocks]
-        spot = result.at[blocks, core, my_share[0], my_share[1]]
+        section, first, count = GROUPS[t]
+        last = share[t].at[far_steps]
+        spot = result.at[core, mine, pl.ds(first, count)]
         for q in range(near):
-            to = (t, xor(j, 2 * q))
-            go(remote(last, spot, r_send.at[t, q], r_recv.at[me, place], to), None if q > 0 else me != t)
-
-        @pl.when(me == t)
+            to = (section, xor(j, 2 * q))
+            go(remote(last, spot, r_send.at[t, q], r_recv.at[t // 4, me, place], to), None if q > 0 else me != section)
+
+        @pl.when(me == section)
         def _():
-            for b in range(blocks_of(t)):
-                result[b, core, my_share[0], my_share[1]] = share[t, far_steps, b]
+            for b in range(count):
+                result[core, mine, first + b] = share[t][far_steps, b]
 
     copies = {}
 
@@ -715,7 +772,7 @@
             go(copy)
             copy.wait_recv()
             vec_sum[3 + step] = vec_sum[2 + step] + vec_far[step]
-        gvec_ref[0] = vec_sum[2 + far_steps] * (1.0 / images)
+        gvec_ref[...] = vec_sum[2 + far_steps]
 
     def on(act, *rest):
         return lambda: act(*rest)
@@ -733,22 +790,29 @@
     plan = {
         ("inputs", 0): [inputs_here],
         ("vectors", 0): [vectors_here],
-        ("prepared", 0): [on(forward_weights, 0, 0), on(forward_weights, 0, 1)],
+        ("prepared", 0): [
+            on(send_weights, 1),
+            on(send_weights, 2),
+            on(pass_on, 0, (1, 2)),
+            on(pass_on, 1, (1, 2)),
+            on(pass_on, 2, (1, 2)),
+            on(pass_on, 0, (3,)),
+        ],
+        ("weights", 1): [on(pass_on, 2, (3,))],
     }
     for t in range(SECTIONS):
-        plan["weights", t] = [on(take_weights, t, 0), on(take_weights, t, 1), on(take_weights, t, 2)]
-        plan["next", t] = [on(forward_weights, t + 1, p) for p in range(3)] if t + 1 < SECTIONS else []
+        plan["weights", t] = plan.get(("weights", t), []) + [on(take_weights, t, 0)]
+        plan["out", t] = [on(take_weights, t, 1), on(take_weights, t, 2)]
         plan["grads", t] = [on(halves_start, t)]
-    plan["image", 6] = [on(halves_end, 3), on(parts_start, 3)]
-    plan["image", 5] = [on(parts_end, 3), on(near_start, 3)]
-    plan["norm", 4] = [on(halves_end, 2), on(parts_start, 2)]
-    plan["image", 2] = [on(halves_end, 1), on(parts_start, 1)]
-    plan["image", 3] = [on(near_end, 3)]
-    plan["half", 0] = [on(parts_end, 2), on(near_start, 2)]
-    plan["half", 1] = [on(parts_end, 1), on(near_start, 1)]
-    plan["image", 1] = [on(near_end, 2)]
-    plan["norm", 0] = [on(halves_end, 0), on(around_start, 0)]
-    plan["conv", 1] = [vectors_start, on(near_end, 1)]
+    plan["scores", 0] = [on(pass_on, 1, (3,))]
+    plan["first grads", 0] = [on(halves_start, 4)]
+    plan["first grads", 2] = [on(halves_end, 3), on(parts_start, 3)]
+    plan["conv", 4] = [on(halves_end, 2), on(parts_start, 2)]
+    plan["image", 3] = [on(halves_end, 1), on(parts_start, 1)]
+    plan["half", 0] = [on(parts_end, 3), on(near_start, 3), on(halves_end, 4), on(parts_start, 4)]
+    plan["half", 1] = [on(parts_end, 2), on(near_start, 2)]
+    plan["norm", 1] = [on(halves_end, 0), on(parts_start, 0)]
+    plan["conv", 1] = [vectors_start, on(near_end, 3)]
     done = []
 
     def at_point(name, s):
@@ -758,46 +822,40 @@
 
     layers(
         n, at_point,
-        x_ref, cot_ref, routes_ref, vec_ref, win_ref, wout_ref, fin_ref, gin_ref, gvec_part, grad_ref, *scratch,
+        x_ref, cot_ref, routes_ref, vec_ref, win_ref, wout_ref, fin_ref, gin_ref, gvec_part, *scratch,
     )
     assert all(key in done or not plan[key] for key in plan)
+    for t in (1, 4):
+        parts_end(t)
+        near_start(t)
+    near_end(2)
+    parts_end(0)
+    near_start(0)
     vectors_mate()
+    near_end(1)
     vectors_near()
-    around_end(0)
+    near_end(4)
+    near_end(0)
     vectors_end()
 
-    for parity in range(2):
-        blocks = pl.ds(0, blocks_of(parity))
-        half = result.at[blocks, core]
-
-        @pl.when(lax.rem(me, 2) == parity)
+    for section in range(SECTIONS):
+        half = result.at[core, :, pl.ds(0, blocks_of(section))]
+
+        @pl.when(me == section)
         def _():
-            for k, q in around:
-                from_me, from_place = xor(me, k), xor(place, q)
-                rows, lanes = share_in_half(from_me, from_place)
-                spot = result.at[blocks, core, rows, lanes]
-                remote(spot, spot, r_send.at[0, 0], r_recv.at[from_me, from_place], mate).wait_recv()
-
-        copy = remote(half, half, m_send.at[parity], m_recv.at[parity], mate)
-        go(copy, lax.rem(me, 2) == parity)
-
-    def finish(c):
-        for b in range(3):
-            rows = pl.ds(pl.multiple_of(c * HALF, HALF), HALF)
-            ga_ref[0, rows, b * D : (b + 1) * D] = result[b, c].astype(F32) * (1.0 / images)
-            gb_ref[0, pl.ds(pl.multiple_of(b * D + c * HALF, HALF), HALF)] = result[3 + b, c].astype(F32) * (1.0 / images)
-
-    finish(core)
-    for parity in range(2):
-        half = result.at[pl.ds(0, blocks_of(parity)), 1 - core]
-        pl.when(lax.rem(me, 2) == parity)(
-            lambda half=half, parity=parity: remote(half, half, m_send.at[parity], m_recv.at[parity], mate).wait_recv()
-        )
-    finish(1 - core)
-
-    @pl.when(lax.rem(me, 2) == 0)
-    def _():
-        gb_ref[0, D:HID] = jnp.zeros((HID - D, D), F32)
+            for t, (owner, first, count) in enumerate(GROUPS):
+                if owner == section:
+                    for k, q in around:
+                        from_me, from_place = xor(me, k), xor(place, q)
+                        spot = result.at[core, piece_of(from_me, from_place), pl.ds(first, count)]
+                        remote(spot, spot, r_send.at[0, 0], r_recv.at[t // 4, from_me, from_place], mate).wait_recv()
+
+        go(remote(half, half, m_send.at[section], m_recv.at[section], mate), me == section)
+
+    for section in range(SECTIONS):
+        half = result.at[1 - core, :, pl.ds(0, blocks_of(section))]
+        copy = remote(half, half, m_send.at[section], m_recv.at[section], mate)
+        pl.when(me == section)(lambda copy=copy: copy.wait_recv())
 
     for copy, condition in waiting:
         when(condition, lambda copy=copy: copy.wait_send())
@@ -809,25 +867,23 @@
     near, piece_rows, piece_lanes, far_steps = shares_of(dp)
     images = micro * n * dp
     vmem = pl.BlockSpec(memory_space=pltpu.VMEM)
-    hbm = pl.BlockSpec(memory_space=pl.ANY)
+    hbm = pl.BlockSpec(memory_space=pltpu.HBM)
     dma = pltpu.SemaphoreType.DMA
-    by_token = jax.ShapeDtypeStruct((1, PATCHES, n, D), BF)
-    some = max(far_steps, 1)
+    some, groups = max(far_steps, 1), len(GROUPS)
 
     def grad_buffer(*shape):
-        return pltpu.VMEM((SECTIONS,) + shape, BF)
-
-    fin, gin, gvec, ga, gb = pl.pallas_call(
+        return [pltpu.VMEM(tuple(count if size == "blocks" else size for size in shape), BF) for _, _, count in GROUPS]
+
+    made = pl.pallas_call(
         functools.partial(whole_kernel, n, dp, images),
         out_shape=(
-            by_token,
-            by_token,
-            jax.ShapeDtypeStruct((1, VEC_ROWS, D), F32),
-            jax.ShapeDtypeStruct((1, D, HID), F32),
-            jax.ShapeDtypeStruct((1, HID, D), F32),
+            jax.ShapeDtypeStruct((PATCHES, n, D), BF),
+            jax.ShapeDtypeStruct((PATCHES, n, D), BF),
+            jax.ShapeDtypeStruct((VEC_ROWS, D), F32),
+            jax.ShapeDtypeStruct((2, SECTIONS * near, 6, piece_rows, piece_lanes), BF),
         ),
         in_specs=[hbm] * 6,
-        out_specs=(vmem,) * 5,
+        out_specs=(vmem,) * 4,
         scratch_shapes=[
             pltpu.VMEM((PATCHES, n, D), BF),
             pltpu.VMEM((PATCHES, n, D), BF),
@@ -836,17 +892,15 @@
             pltpu.VMEM((SECTIONS, D, HID), BF),
             pltpu.VMEM((SECTIONS, HID, D), BF),
             pltpu.VMEM((SECTIONS, VEC_ROWS, D), F32),
-            pltpu.VMEM((6, BLOCK, BLOCK), F32),
-            grad_buffer(6, HALF, BLOCK),
-            grad_buffer(6, HALF, BLOCK),
-            grad_buffer(6, HALF, BLOCK),
-            grad_buffer(6, HALF, BLOCK),
-            grad_buffer(3, 6, PART, BLOCK),
-            grad_buffer(6, PART, BLOCK),
-            grad_buffer(SECTIONS * near, 6, piece_rows, piece_lanes),
-            grad_buffer(far_steps + 1, 6, piece_rows, piece_lanes),
-            grad_buffer(some, 6, piece_rows, piece_lanes),
-            pltpu.VMEM((6, 2, HALF, BLOCK), BF),
+            grad_buffer("blocks", HALF, BLOCK),
+            grad_buffer("blocks", HALF, BLOCK),
+            grad_buffer("blocks", HALF, BLOCK),
+            grad_buffer(SECTIONS * near, "blocks", piece_rows, piece_lanes),
+            grad_buffer(3, near, "blocks", piece_rows, piece_lanes),
+            grad_buffer(near, "blocks", piece_rows, piece_lanes),
+            grad_buffer(near, "blocks", piece_rows, piece_lanes),
+            grad_buffer(far_steps + 1, "blocks", piece_rows, piece_lanes),
+            grad_buffer(some, "blocks", piece_rows, piece_lanes),
             pltpu.VMEM((3, VEC_ROWS, D), F32),
             pltpu.VMEM((3 + far_steps, VEC_ROWS, D), F32),
             pltpu.VMEM((VEC_ROWS, D), F32),
@@ -856,12 +910,12 @@
             dma((3, 3)), dma((3, SECTIONS)),
             dma((3, SECTIONS)), dma((3, SECTIONS)),
             dma((3,)), dma((3,)),
+            dma((groups,)), dma((groups,)),
+            dma((groups, 3)), dma((groups, 3)),
+            dma((groups, near)), dma((groups, near)),
+            dma((groups, some)), dma((groups, some)),
+            dma((groups, near)), dma((2, SECTIONS, near)),
             dma((SECTIONS,)), dma((SECTIONS,)),
-            dma((SECTIONS, 3)), dma((SECTIONS, 3)),
-            dma((SECTIONS, SECTIONS * near)), dma((SECTIONS, SECTIONS * near)),
-            dma((SECTIONS, some)), dma((SECTIONS, some)),
-            dma((SECTIONS, near)), dma((SECTIONS, near)),
-            dma((2,)), dma((2,)),
             dma((3,)), dma((3,)),
             dma((1,)), dma((1,)),
             dma((near,)), dma((near,)),
@@ -880,6 +934,22 @@
         in_weight,
         out_weight,
     )
+    by_token = jax.ShapeDtypeStruct((1, PATCHES, n, D), BF)
+    fin, gin, gvec, ga, gb = pl.pallas_call(
+        functools.partial(results_kernel, dp, images),
+        out_shape=(
+            by_token,
+            by_token,
+            jax.ShapeDtypeStruct((1, VEC_ROWS, D), F32),
+            jax.ShapeDtypeStruct((1, D, HID), F32),
+            jax.ShapeDtypeStruct((1, HID, D), F32),
+        ),
+        in_specs=[vmem] * 4,
+        out_specs=(hbm, hbm, vmem, hbm, hbm),
+        scratch_shapes=[pltpu.VMEM((D, HID), F32), pltpu.VMEM((HID, D), F32), dma((4,))],
+        compiler_params=pltpu.CompilerParams(vmem_limit_bytes=60 * 1024 * 1024),
+        name="results",
+    )(*made)
     return jnp.transpose(fin, (0, 2, 1, 3)), jnp.transpose(gin, (0, 2, 1, 3)), gvec, ga, gb
 
 

time: 89.2 us -> 72.6 us (0.81)
  Pallas kernels: 81.8 us -> 71.6 us
  local copies, waits for them, and re-layouts: 6.48 us -> 0 us
    pallas_call x1, Pallas kernels: 81.8 us -> 68.4 us  [per_device(): pl.pallas_call(functools.partial(whole_kernel, n, dp, images), out_shape=...]
    unnamed x11 -> x0, local copies, waits for them, and re-layouts: 6.48 us -> none
    pallas_call x0 -> x1, Pallas kernels: none -> 3.27 us  [per_device(): pl.pallas_call(functools.partial(results_kernel, dp, images), out_shape=(...]
where the time goes in v4:
time: 72.6 us; the launch traced here: 72.4 us
  Pallas kernels  71.6 us (99%)
  between operations  0.8 us (1%)
    pallas_call x1, Pallas kernels, per_device(): pl.pallas_call(functools.partial(whole_kernel, n, dp, images), out_shape=...  68.4 us
    pallas_call x1, Pallas kernels, per_device(): pl.pallas_call(functools.partial(results_kernel, dp, images), out_shape=(...  3.27 us

profile of v4, /device:TPU:1, one launch (start us, length us, event | category | flops | bytes accessed | tf_op | source)
XLA Modules:
  0.0 72.4 jit_solution(4440116547176282288)
XLA Ops:
  0.6 68.4 %two_layers.1 = (bf16[196,2,256]{2,1,0:T(2,128)(2,1)}, bf16[196,2,256]{2,1,0:T(2,128)(2,1)}, f32[16,256]{1,0:T(8,128)}, bf16[2,16,6,16,128]{4,3,2,1,0:T(8,128)(2,1)}) custom-call(bf16[4,196,2,256]{3,2,1,0:T(2,128)(2,1)} %bitcast.5, bf16[4,196,2,256]{3,2,1,0:T(2,128)(2,1)} %bitcast.6, s32[2,4,2,4,49]{4,3,2,1,0:T(4,128)} %bitcast.7, f32[1,16,256]{2,1,0:T(8,128)} %vec_own.1, ...), custom_call_target="tpu_custom_call" | custom-call | tf_op jit(solution)/shard_map/two_layers/pallas_call | solution.py:877
  69.0 3.3 %results.1 = (bf16[1,196,2,256]{3,2,1,0:T(2,128)(2,1)}, bf16[1,196,2,256]{3,2,1,0:T(2,128)(2,1)}, f32[1,16,256]{2,1,0:T(8,128)}, f32[1,256,768]{2,1,0:T(8,128)}, f32[1,768,256]{2,1,0:T(8,128)}) custom-call(bf16[196,2,256]{2,1,0:T(2,128)(2,1)} %get-tuple-element.14.fin_in, bf16[196,2,256]{2,1,0:T(2,128)(2,1)} %get-tuple-element.15.gin_in, ...), custom_call_target="tpu_custom_call" | custom-call | tf_op jit(solution)/shard_map/results/pallas_call | solution.py:938

commit v5 on v4

--- a/solution.py
+++ b/solution.py
@@ -87,22 +87,21 @@
 
 
 def weight_grads(scratch, s, first, count, half):
-    nm, at, act, g, dproj = (scratch[LAYER_SCRATCH.index(name)] for name in ("nm", "at", "act", "g", "dproj"))
+    nmt, att, actt, g, dproj = (scratch[LAYER_SCRATCH.index(name)] for name in ("nmt", "att", "actt", "g", "dproj"))
     results = []
     ins = min(first + count, 3) - first
     if ins > 0:
-        lanes = pl.ds(pl.multiple_of(half * LANES, LANES), LANES)
-        wide = dot(nm[s, :, lanes], dproj[:, first * D : (first + ins) * D], 0, 0)
+        rows = pl.ds(pl.multiple_of(half * LANES, LANES), LANES)
+        wide = dot(nmt[s, rows], dproj[:, first * D : (first + ins) * D])
         results += [wide[:, b * D : (b + 1) * D] for b in range(ins)]
     for b in range(max(first, 3) - 3, first + count - 3):
-        lanes = pl.ds(pl.multiple_of(b * D + half * LANES, LANES), LANES)
-        left = act[s // 2, :, lanes] if s % 2 == 1 else at[s // 2, :, lanes]
-        results.append(dot(left, g[...], 0, 0))
+        rows = pl.ds(pl.multiple_of(b * D + half * LANES, LANES), LANES)
+        results.append(dot((actt if s % 2 == 1 else att)[s // 2, rows], g[...]))
     return results
 
 
 LAYER_SCRATCH = (
-    "hs", "zh", "inv", "nm", "pr", "pt", "at", "act", "gp", "bias", "mixed", "g", "dproj", "cv", "cvl", "cvr",
+    "hs", "zh", "inv", "nm", "nmt", "pr", "pt", "att", "act", "actt", "gp", "bias", "mixed", "g", "dproj", "cv", "cvl", "cvr",
     "dom", "qm", "dsb", "tmp", "dqt", "km", "wide",
 )
 
@@ -110,7 +109,7 @@
 def layers(
     n, at_point,
     x_ref, cot_ref, routes_ref, vec_ref, win_ref, wout_ref, fin_ref, gin_ref, gvec_ref,
-    hs, zh, inv, nm, pr, pt, at, act, gp, bias, mixed, g, dproj, cv, cvl, cvr, dom, qm, dsb, tmp, dqt, km, wide,
+    hs, zh, inv, nm, nmt, pr, pt, att, act, actt, gp, bias, mixed, g, dproj, cv, cvl, cvr, dom, qm, dsb, tmp, dqt, km, wide,
 ):
     pairs = PATCHES * n
 
@@ -152,7 +151,6 @@
         for a in range(2):
             pr[a, tail(i)] = none_wide
             act[a, tail(i)] = none_wide
-            at[a, tail(i)] = none
         wide[tail(i)] = none
         dproj[tail(i)] = none_wide
     gvec_ref[...] = jnp.zeros_like(gvec_ref)
@@ -177,10 +175,12 @@
         start = HALO + (r + u) * PITCH
         return (cvl, cv, cvr)[v + 1][start : start + PITCH]
 
+    def columns(i):
+        return slice(i * ROWS, (i + 1) * ROWS)
+
     def attention_start(s):
         vec = vec_ref.at[s]
-
-        def image(i, carry):
+        for i in range(n):
             for rows in chunks():
                 conv_load(rows.start, CHUNK, hs[s, rows_at(i, rows.start, CHUNK)].astype(F32))
             conv_shift()
@@ -196,9 +196,8 @@
                 zh[s, here] = hat
                 inv[s, here] = inverse
                 nm[s, here] = (hat * vec[0:1] + vec[1:2]).astype(BF)
-            return carry
-
-        lax.fori_loop(0, n, image, 0)
+        for i in range(n):
+            nmt[s, :, columns(i)] = transposed(nm[s, rows_of(i, ROWS)]).astype(BF)
 
     def route_bias():
         key_region = region_one_hot((LIVE, REGIONS), 0)
@@ -222,60 +221,69 @@
     def attention_forward(s):
         a = s // 2
         vec = vec_ref.at[s]
-
-        def image(i, carry):
+        at_point("weights", s)
+        for i in range(n):
             rows = rows_of(i)
-            whole = rows_of(i, ROWS)
-            pr[a, rows] = dot(nm[s, rows], win_ref[s]).astype(BF)
-            tmp[...] = transposed(pr[a, whole, 2 * D : 3 * D]).astype(BF)
+            pr[a, rows, 0 : 2 * D] = dot(nm[s, rows], win_ref[s, :, 0 : 2 * D]).astype(BF)
+        for i in range(n):
+            rows, whole = rows_of(i), rows_of(i, ROWS)
             for h in range(HEADS):
                 lanes = half_of(h)
                 keys = jnp.where(own_lanes(h, LIVE), pr[a, rows, slice(D + lanes.start, D + lanes.stop)], jnp.zeros((), BF))
                 scores = dot(keys, pr[a, whole, lanes], 1, 1) * (SCALE * LOG2E) + bias[a, i]
                 expo = jnp.exp2(scores - jnp.max(scores, axis=0, keepdims=True))
                 pt[a, i, :, h * ROWS : (h + 1) * ROWS] = (expo * (1.0 / col_sum(expo))).astype(BF)
-            pl.when(i == 0)(lambda: at_point("scores", s))
+        at_point("scores", s)
+        at_point("values", s)
+        for i in range(n):
+            rows, whole = rows_of(i), rows_of(i, ROWS)
+            pr[a, rows, 2 * D : 3 * D] = dot(nm[s, rows], win_ref[s, :, 2 * D : 3 * D]).astype(BF)
+            tmp[i] = transposed(pr[a, whole, 2 * D : 3 * D]).astype(BF)
+        for i in range(n):
             for h in range(HEADS):
                 own = slice(h * HEAD_DIM, (h + 1) * HEAD_DIM)
-                dqt[own] = dot(tmp[own, 0:LIVE], pt[a, i, :, h * ROWS : (h + 1) * ROWS])
-            attended = transposed(dqt[...].astype(BF)).astype(BF)
-            at[a, whole] = attended
-            pl.when(i == 0)(lambda: at_point("out", s))
-            out = mixed[rows] + dot(attended[:LIVE], wout_ref[s, 0:D]) + vec[2:3]
-            hs[s + 1, rows] = out.astype(BF)
-            return carry
-
-        lax.fori_loop(0, n, image, 0)
+                att[a, own, columns(i)] = dot(tmp[i, own, 0:LIVE], pt[a, i, :, h * ROWS : (h + 1) * ROWS]).astype(BF)
+        at_point("out", s)
+        for i in range(n):
+            attended = transposed(att[a, :, columns(i)]).astype(BF)
+            out = mixed[rows_of(i)] + dot(attended[:LIVE], wout_ref[s, 0:D]) + vec[2:3]
+            hs[s + 1, rows_of(i)] = out.astype(BF)
 
     def dense_forward(s):
         a = s // 2
         vec = vec_ref.at[s]
-        token = iota((CHUNK, D), 0)
-
-        def image(i, carry):
-            rows = rows_of(i)
+        for i in range(n):
             for part in chunks():
                 here = rows_at(i, part.start, CHUNK)
                 hat, inverse = ln_stats(hs[s, here].astype(F32))
                 zh[s, here] = hat
                 inv[s, here] = inverse
                 nm[s, here] = (hat * vec[0:1] + vec[1:2]).astype(BF)
-            for j in range(3):
-                lanes = slice(j * D, (j + 1) * D)
+        for i in range(n):
+            nmt[s, :, columns(i)] = transposed(nm[s, rows_of(i, ROWS)]).astype(BF)
+        at_point("weights", s)
+        at_point("values", s)
+        for j in range(3):
+            lanes = slice(j * D, (j + 1) * D)
+            for i in range(n):
+                rows = rows_of(i)
                 hidden = dot(nm[s, rows], win_ref[s, :, lanes]) + vec[3 + j : 4 + j]
                 value, slope = gelu_pair(hidden)
                 act[a, rows, lanes] = value.astype(BF)
                 gp[a, rows, lanes] = slope
-            pl.when(i == 0)(lambda: at_point("out", s))
+        at_point("out", s)
+        for i in range(n):
+            rows = rows_of(i)
             out = hs[s, rows].astype(F32) + dot(act[a, rows], wout_ref[s]) + vec[2:3]
             if s + 1 < SECTIONS:
                 live = (iota((LIVE, D), 0) & (PITCH - 1)) < SIDE
                 hs[s + 1, rows] = jnp.where(live, out, 0.0).astype(BF)
             else:
                 wide[rows] = out.astype(BF)
-            return carry
-
-        lax.fori_loop(0, n, image, 0)
+        for j in range(3):
+            lanes = slice(j * D, (j + 1) * D)
+            for i in range(n):
+                actt[a, lanes, columns(i)] = transposed(act[a, rows_of(i, ROWS), lanes]).astype(BF)
 
     def norm_backward(s, here, d_normed, sums):
         vec = vec_ref.at[s]
@@ -341,7 +349,7 @@
         for i in range(n):
             rows = rows_of(i)
             whole = rows_of(i, ROWS)
-            tmp[...] = transposed(pr[a, whole, D : 2 * D]).astype(BF)
+            tmp[i] = transposed(pr[a, whole, D : 2 * D]).astype(BF)
             for h in range(HEADS):
                 qm[h * ROWS : (h + 1) * ROWS] = jnp.where(own_lanes(h, ROWS), pr[a, whole, half_of(h)], nothing)
             for h in range(HEADS):
@@ -355,7 +363,7 @@
                     at_point("half", 2 * s + i)
             for h in range(HEADS):
                 own = slice(h * HEAD_DIM, (h + 1) * HEAD_DIM)
-                dqt[own] = dot(tmp[own, 0:LIVE], dsb[:, h * ROWS : (h + 1) * ROWS])
+                dqt[own] = dot(tmp[i, own, 0:LIVE], dsb[:, h * ROWS : (h + 1) * ROWS])
             for half in range(2):
                 lanes = slice(D + half * LANES, D + (half + 1) * LANES)
                 four = slice(half * 4 * ROWS, (half + 1) * 4 * ROWS)
@@ -394,12 +402,11 @@
                 add_row(s, 6 + j, taps[j])
             at_point("conv", 2 * s + i)
 
-    at_point("vectors", 0)
+    route_bias()
+    at_point("routed", 0)
     attention_start(0)
-    route_bias()
     at_point("prepared", 0)
     for s in range(SECTIONS):
-        at_point("weights", s)
         if s == 2:
             attention_start(s)
         (attention_forward, dense_forward)[s % 2](s)
@@ -416,10 +423,12 @@
         pltpu.VMEM((SECTIONS, total, D), F32),
         pltpu.VMEM((SECTIONS, total, 1), F32),
         pltpu.VMEM((SECTIONS, total, D), BF),
+        pltpu.VMEM((SECTIONS, D, total), BF),
         pltpu.VMEM((2, total, HID), BF),
         pltpu.VMEM((2, n, LIVE, HEADS * ROWS), BF),
-        pltpu.VMEM((2, total, D), BF),
+        pltpu.VMEM((2, D, total), BF),
         pltpu.VMEM((2, total, HID), BF),
+        pltpu.VMEM((2, HID, total), BF),
         pltpu.VMEM((2, total, HID), F32),
         pltpu.VMEM((2, n, LIVE, ROWS), F32),
         pltpu.VMEM((total, D), F32),
@@ -431,7 +440,7 @@
         pltpu.VMEM((HEADS * ROWS, LANES), BF),
         pltpu.VMEM((HEADS * ROWS, LANES), BF),
         pltpu.VMEM((LIVE, HEADS * ROWS), BF),
-        pltpu.VMEM((D, ROWS), BF),
+        pltpu.VMEM((n, D, ROWS), BF),
         pltpu.VMEM((D, ROWS), F32),
         pltpu.VMEM((total, D), BF),
         pltpu.VMEM((total, D), BF),
@@ -789,10 +798,8 @@
 
     plan = {
         ("inputs", 0): [inputs_here],
-        ("vectors", 0): [vectors_here],
+        ("routed", 0): [on(send_weights, 1), on(send_weights, 2), vectors_here],
         ("prepared", 0): [
-            on(send_weights, 1),
-            on(send_weights, 2),
             on(pass_on, 0, (1, 2)),
             on(pass_on, 1, (1, 2)),
             on(pass_on, 2, (1, 2)),

time: 72.6 us -> 71.3 us (0.982)
  Pallas kernels: 71.6 us -> 70.3 us
    pallas_call x1, Pallas kernels: 68.4 us -> 67 us  [per_device(): pl.pallas_call(functools.partial(whole_kernel, n, dp, images), out_shape=...]
where the time goes in v5:
time: 71.3 us; the launch traced here: 71.1 us
  Pallas kernels  70.3 us (99%)
  between operations  0.8 us (1%)
    pallas_call x1, Pallas kernels, per_device(): pl.pallas_call(functools.partial(whole_kernel, n, dp, images), out_shape=...  67 us
    pallas_call x1, Pallas kernels, per_device(): pl.pallas_call(functools.partial(results_kernel, dp, images), out_shape=(...  3.27 us

profile of v5, /device:TPU:1, one launch (start us, length us, event | category | flops | bytes accessed | tf_op | source)
XLA Modules:
  0.0 71.1 jit_solution(17517828314444927503)
XLA Ops:
  0.6 67.0 %two_layers.1 = (bf16[196,2,256]{2,1,0:T(2,128)(2,1)}, bf16[196,2,256]{2,1,0:T(2,128)(2,1)}, f32[16,256]{1,0:T(8,128)}, bf16[2,16,6,16,128]{4,3,2,1,0:T(8,128)(2,1)}) custom-call(bf16[4,196,2,256]{3,2,1,0:T(2,128)(2,1)} %bitcast.5, bf16[4,196,2,256]{3,2,1,0:T(2,128)(2,1)} %bitcast.6, s32[2,4,2,4,49]{4,3,2,1,0:T(4,128)} %bitcast.7, f32[1,16,256]{2,1,0:T(8,128)} %vec_own.1, ...), custom_call_target="tpu_custom_call" | custom-call | tf_op jit(solution)/shard_map/two_layers/pallas_call | solution.py:884
  67.7 3.3 %results.1 = (bf16[1,196,2,256]{3,2,1,0:T(2,128)(2,1)}, bf16[1,196,2,256]{3,2,1,0:T(2,128)(2,1)}, f32[1,16,256]{2,1,0:T(8,128)}, f32[1,256,768]{2,1,0:T(8,128)}, f32[1,768,256]{2,1,0:T(8,128)}) custom-call(bf16[196,2,256]{2,1,0:T(2,128)(2,1)} %get-tuple-element.14.fin_in, bf16[196,2,256]{2,1,0:T(2,128)(2,1)} %get-tuple-element.15.gin_in, ...), custom_call_target="tpu_custom_call" | custom-call | tf_op jit(solution)/shard_map/results/pallas_call | solution.py:945

commit v6 on v5

--- a/solution.py
+++ b/solution.py
@@ -347,28 +347,32 @@
                 dproj[rows, lanes] = dot(pt[a, i, :, four], dom[four]).astype(BF)
         at_point("first grads", s)
         for i in range(n):
-            rows = rows_of(i)
             whole = rows_of(i, ROWS)
             tmp[i] = transposed(pr[a, whole, D : 2 * D]).astype(BF)
             for h in range(HEADS):
-                qm[h * ROWS : (h + 1) * ROWS] = jnp.where(own_lanes(h, ROWS), pr[a, whole, half_of(h)], nothing)
+                qm[i, h * ROWS : (h + 1) * ROWS] = jnp.where(own_lanes(h, ROWS), pr[a, whole, half_of(h)], nothing)
+        for i in range(n):
+            rows = rows_of(i)
+            whole = rows_of(i, ROWS)
             for h in range(HEADS):
                 lanes = half_of(h)
                 row = slice(h * ROWS, (h + 1) * ROWS)
                 values = jnp.where(own_lanes(h, LIVE), pr[a, rows, slice(2 * D + lanes.start, 2 * D + lanes.stop)], nothing)
                 d_weights = dot(values, km[whole, lanes], 1, 1)
                 weights = pt[a, i, :, row].astype(F32)
-                dsb[:, row] = (weights * (d_weights - col_sum(weights * d_weights))).astype(BF)
-                if h == 3:
-                    at_point("half", 2 * s + i)
+                dsb[i, :, row] = (weights * (d_weights - col_sum(weights * d_weights))).astype(BF)
+            at_point("half", 2 * s + i)
+        for i in range(n):
+            rows = rows_of(i)
             for h in range(HEADS):
                 own = slice(h * HEAD_DIM, (h + 1) * HEAD_DIM)
-                dqt[own] = dot(tmp[i, own, 0:LIVE], dsb[:, h * ROWS : (h + 1) * ROWS])
+                dqt[own, columns(i)] = dot(tmp[i, own, 0:LIVE], dsb[i, :, h * ROWS : (h + 1) * ROWS])
             for half in range(2):
                 lanes = slice(D + half * LANES, D + (half + 1) * LANES)
                 four = slice(half * 4 * ROWS, (half + 1) * 4 * ROWS)
-                dproj[rows, lanes] = (dot(dsb[:, four], qm[four]) * SCALE).astype(BF)
-            dproj[rows, 0:D] = (transposed(dqt[...].astype(BF))[:LIVE] * SCALE).astype(BF)
+                dproj[rows, lanes] = (dot(dsb[i, :, four], qm[i, four]) * SCALE).astype(BF)
+        for i in range(n):
+            dproj[rows_of(i), 0:D] = (transposed(dqt[:, columns(i)].astype(BF))[:LIVE] * SCALE).astype(BF)
             at_point("image", 2 * s + i)
         at_point("grads", s)
         for i in range(n):
@@ -410,10 +414,15 @@
         if s == 2:
             attention_start(s)
         (attention_forward, dense_forward)[s % 2](s)
-    fin_ref[...] = dot(gather(), wide[...]).astype(BF).reshape(PATCHES, n, D)
     for s in reversed(range(SECTIONS)):
         (attention_backward, dense_backward)[s % 2](s)
-    gin_ref[...] = dot(gather(), g[...]).astype(BF).reshape(PATCHES, n, D)
+
+    def finish():
+        pick = gather()
+        fin_ref[...] = dot(pick, wide[...]).astype(BF).reshape(PATCHES, n, D)
+        gin_ref[...] = dot(pick, g[...]).astype(BF).reshape(PATCHES, n, D)
+
+    return finish
 
 
 def layer_scratch(n):
@@ -438,10 +447,10 @@
         pltpu.VMEM((LIVE + 2 * HALO, D), F32),
         pltpu.VMEM((LIVE + 2 * HALO, D), F32),
         pltpu.VMEM((HEADS * ROWS, LANES), BF),
-        pltpu.VMEM((HEADS * ROWS, LANES), BF),
-        pltpu.VMEM((LIVE, HEADS * ROWS), BF),
+        pltpu.VMEM((n, HEADS * ROWS, LANES), BF),
+        pltpu.VMEM((n, LIVE, HEADS * ROWS), BF),
         pltpu.VMEM((n, D, ROWS), BF),
-        pltpu.VMEM((D, ROWS), F32),
+        pltpu.VMEM((D, total), F32),
         pltpu.VMEM((total, D), BF),
         pltpu.VMEM((total, D), BF),
     ]
@@ -464,7 +473,7 @@
         if s % 2 == 0:
             gb_ref[s, D:HID] = jnp.zeros((HID - D, D), F32)
 
-    layers(n, at_point, x_ref, cot_ref, routes_ref, vec_ref, win_ref, wout_ref, fin_ref.at[0], gin_ref.at[0], gvec_ref, *refs[11:])
+    layers(n, at_point, x_ref, cot_ref, routes_ref, vec_ref, win_ref, wout_ref, fin_ref.at[0], gin_ref.at[0], gvec_ref, *refs[11:])()
 
 
 def compute(x, cot, routes, vec, win, wout):
@@ -610,11 +619,11 @@
     tail_rows = pl.ds(pl.multiple_of(D + core * D, D), D)
     pieces = [(win_own, win_ref, own_rows), (wout_own, wout_ref, own_rows), (wout_own, wout_ref, tail_rows)]
 
+    def needed(p, t):
+        return None if p < 2 else lax.rem(t, 2) == 1
+
     def spot(p, t):
         return pieces[p][1].at[t, pieces[p][2]]
-
-    def odd(t):
-        return lax.rem(t, 2) == 1
 
     vec_copies = [remote(vec_own.at[0], vec_ref.at[me], v_send.at[k], v_recv.at[k], to) for k, to in enumerate(sections)]
     out_copies = [
@@ -626,12 +635,12 @@
     ]
     relayed, relay_to = xor(me, 1 + core), xor(me, 2 - core)
     relays = [remote(spot(p, relayed), spot(p, relayed), w_send.at[p, 2], w_recv.at[p, relayed], (relay_to, j)) for p in range(3)]
+    origins = {"relayed": relayed, "other": relay_to, "corner": xor(me, 3)}
     arrivals, handings, takings = {}, {}, {}
     for p in range(3):
-        for k in (1, 2, 3):
-            t = xor(me, k)
-            arrivals[p, k] = remote(spot(p, t), spot(p, t), w_send.at[p, 0], w_recv.at[p, t], mate)
-            handings[p, k] = remote(spot(p, t), spot(p, t), f_send.at[p, t], f_recv.at[p, t], mate)
+        for name, t in origins.items():
+            arrivals[p, name] = remote(spot(p, t), spot(p, t), w_send.at[p, 0], w_recv.at[p, t], mate)
+            handings[p, name] = remote(spot(p, t), spot(p, t), f_send.at[p, t], f_recv.at[p, t], mate)
         for t in range(SECTIONS):
             if p < 2 or t % 2 == 1:
                 takings[p, t] = remote(spot(p, t), spot(p, t), f_send.at[p, t], f_recv.at[p, t], mate)
@@ -639,25 +648,23 @@
 
     def send_weights(p):
         for copy in out_copies[p]:
-            go(copy, odd(me) if p == 2 else None)
-
-    def pass_on(p, ks):
-        for k in ks:
-            condition = odd(xor(me, k)) if p == 2 else None
-            when(condition, lambda: arrivals[p, k].wait_recv())
-        if ks != (3,):
-            go(relays[p], odd(relayed) if p == 2 else None)
-        for k in ks:
-            go(handings[p, k], odd(xor(me, k)) if p == 2 else None)
+            go(copy, needed(p, me))
+
+    def pass_on(p, *names):
+        for name in names:
+            when(needed(p, origins[name]), lambda: arrivals[p, name].wait_recv())
+            if name == "relayed":
+                go(relays[p], needed(p, relayed))
+        for name in names:
+            go(handings[p, name], needed(p, origins[name]))
 
     def take_weights(t, p):
         if p < 2 or t % 2 == 1:
             pl.when(foreign[t])(lambda: takings[p, t].wait_recv())
 
-    for copy in vec_copies:
+    for copy in reversed(vec_copies):
         go(copy)
     send_weights(0)
-
 
     def piece_of(k, q):
         return k * near + q
@@ -691,7 +698,7 @@
             remote(half_sum[t].at[quarter(to[0])], got_part[t].at[k], p_send.at[t, k], p_recv.at[t, k], to)
             for k, to in enumerate(sections)
         ]
-        for copy in steps[t]:
+        for copy in reversed(steps[t]):
             go(copy)
 
     def parts_end(t):
@@ -706,7 +713,7 @@
 
     def near_start(t):
         steps[t] = []
-        for q in range(1, near):
+        for q in reversed(range(1, near)):
             to_place = xor(place, q)
             source = part_sum[t].at[to_place]
             steps[t].append(remote(source, got_near[t].at[q], n_send.at[t, q], n_recv.at[t, q], device(0, q)))
@@ -736,7 +743,7 @@
         section, first, count = GROUPS[t]
         last = share[t].at[far_steps]
         spot = result.at[core, mine, pl.ds(first, count)]
-        for q in range(near):
+        for q in reversed(range(near)):
             to = (section, xor(j, 2 * q))
             go(remote(last, spot, r_send.at[t, q], r_recv.at[t // 4, me, place], to), None if q > 0 else me != section)
 
@@ -800,24 +807,24 @@
         ("inputs", 0): [inputs_here],
         ("routed", 0): [on(send_weights, 1), on(send_weights, 2), vectors_here],
         ("prepared", 0): [
-            on(pass_on, 0, (1, 2)),
-            on(pass_on, 1, (1, 2)),
-            on(pass_on, 2, (1, 2)),
-            on(pass_on, 0, (3,)),
+            on(pass_on, 0, "relayed", "other"),
+            on(pass_on, 1, "relayed", "other"),
+            on(pass_on, 2, "relayed", "other"),
+            on(pass_on, 0, "corner"),
         ],
-        ("weights", 1): [on(pass_on, 2, (3,))],
+        ("weights", 1): [on(pass_on, 2, "corner")],
     }
     for t in range(SECTIONS):
         plan["weights", t] = plan.get(("weights", t), []) + [on(take_weights, t, 0)]
         plan["out", t] = [on(take_weights, t, 1), on(take_weights, t, 2)]
         plan["grads", t] = [on(halves_start, t)]
-    plan["scores", 0] = [on(pass_on, 1, (3,))]
+    plan["scores", 0] = [on(pass_on, 1, "corner")]
     plan["first grads", 0] = [on(halves_start, 4)]
-    plan["first grads", 2] = [on(halves_end, 3), on(parts_start, 3)]
-    plan["conv", 4] = [on(halves_end, 2), on(parts_start, 2)]
-    plan["image", 3] = [on(halves_end, 1), on(parts_start, 1)]
-    plan["half", 0] = [on(parts_end, 3), on(near_start, 3), on(halves_end, 4), on(parts_start, 4)]
-    plan["half", 1] = [on(parts_end, 2), on(near_start, 2)]
+    plan["half", 4] = [on(halves_end, 3), on(parts_start, 3)]
+    plan["conv", 5] = [on(halves_end, 2), on(parts_start, 2)]
+    plan["first grads", 0] = [on(halves_end, 1), on(parts_start, 1), on(halves_start, 4)]
+    plan["half", 1] = [on(parts_end, 3), on(near_start, 3), on(halves_end, 4), on(parts_start, 4)]
+    plan["image", 1] = [on(parts_end, 2), on(near_start, 2)]
     plan["norm", 1] = [on(halves_end, 0), on(parts_start, 0)]
     plan["conv", 1] = [vectors_start, on(near_end, 3)]
     done = []
@@ -827,7 +834,7 @@
             act()
         done.append((name, s))
 
-    layers(
+    finish = layers(
         n, at_point,
         x_ref, cot_ref, routes_ref, vec_ref, win_ref, wout_ref, fin_ref, gin_ref, gvec_part, *scratch,
     )
@@ -838,6 +845,7 @@
     near_end(2)
     parts_end(0)
     near_start(0)
+    finish()
     vectors_mate()
     near_end(1)
     vectors_near()

time: 71.3 us -> 69.9 us (0.980)
  Pallas kernels: 70.3 us -> 68.9 us
    pallas_call x1, Pallas kernels: 67 us -> 65.7 us  [per_device(): pl.pallas_call(functools.partial(whole_kernel, n, dp, images), out_shape=...]
where the time goes in v6:
time: 69.9 us; the launch traced here: 69.7 us
  Pallas kernels  68.9 us (99%)
  between operations  0.8 us (1%)
    pallas_call x1, Pallas kernels, per_device(): pl.pallas_call(functools.partial(whole_kernel, n, dp, images), out_shape=...  65.7 us
    pallas_call x1, Pallas kernels, per_device(): pl.pallas_call(functools.partial(results_kernel, dp, images), out_shape=(...  3.27 us

profile of v6, /device:TPU:1, one launch (start us, length us, event | category | flops | bytes accessed | tf_op | source)
XLA Modules:
  0.0 69.7 jit_solution(2887104342557006459)
XLA Ops:
  0.6 65.7 %two_layers.1 = (bf16[196,2,256]{2,1,0:T(2,128)(2,1)}, bf16[196,2,256]{2,1,0:T(2,128)(2,1)}, f32[16,256]{1,0:T(8,128)}, bf16[2,16,6,16,128]{4,3,2,1,0:T(8,128)(2,1)}) custom-call(bf16[4,196,2,256]{3,2,1,0:T(2,128)(2,1)} %bitcast.5, bf16[4,196,2,256]{3,2,1,0:T(2,128)(2,1)} %bitcast.6, s32[2,4,2,4,49]{4,3,2,1,0:T(4,128)} %bitcast.7, f32[1,16,256]{2,1,0:T(8,128)} %vec_own.1, ...), custom_call_target="tpu_custom_call" | custom-call | tf_op jit(solution)/shard_map/two_layers/pallas_call | solution.py:892
  66.3 3.3 %results.1 = (bf16[1,196,2,256]{3,2,1,0:T(2,128)(2,1)}, bf16[1,196,2,256]{3,2,1,0:T(2,128)(2,1)}, f32[1,16,256]{2,1,0:T(8,128)}, f32[1,256,768]{2,1,0:T(8,128)}, f32[1,768,256]{2,1,0:T(8,128)}) custom-call(bf16[196,2,256]{2,1,0:T(2,128)(2,1)} %get-tuple-element.14.fin_in, bf16[196,2,256]{2,1,0:T(2,128)(2,1)} %get-tuple-element.15.gin_in, ...), custom_call_target="tpu_custom_call" | custom-call | tf_op jit(solution)/shard_map/results/pallas_call | solution.py:953
